TPU v7x, 32 devices: a whole 2x2x4 slice. The times are simulated.
32 devices in a mesh: dp: 4 (over y, x), fsdp: 8 (over z, core).
Axes of the slice: x: 2, y: 2, z: 4, core: 2. Of those that a mesh axis runs over, the one named last changes fastest.
Arguments:
- tokens: bfloat16 [256, 104, 768], P(('dp', 'fsdp')), may hold values from -6 to 6
- captions: int32 [256], P(('dp', 'fsdp')), may hold values from 5 to 60, as said below
- cotangent: bfloat16 [256, 104, 768], P(('dp', 'fsdp')), may hold values from -6 to 6
- project_weight: bfloat16 [768, 2304], P('fsdp'), may hold values from -0.21875 to 0.21875
- project_bias: bfloat16 [1536], P('fsdp'), may hold values from -3 to 3
- output_weight: bfloat16 [768, 768], P('fsdp'), may hold values from -1.75 to 1.75
- output_bias: bfloat16 [768], P('fsdp'), may hold values from -3 to 3
- first_gain: bfloat16 [768], P('fsdp'), may hold values from 0.25 to 1.75
- first_shift: bfloat16 [768], P('fsdp'), may hold values from -2 to 2
- expand_weight: bfloat16 [768, 3072], P('fsdp'), may hold values from -0.21875 to 0.21875
- expand_bias: bfloat16 [3072], P('fsdp'), may hold values from -3 to 3
- shrink_weight: bfloat16 [3072, 768], P('fsdp'), may hold values from -0.15625 to 0.15625
- shrink_bias: bfloat16 [768], P('fsdp'), may hold values from -3 to 3
- second_gain: bfloat16 [768], P('fsdp'), may hold values from 0.25 to 1.75
- second_shift: bfloat16 [768], P('fsdp'), may hold values from -2 to 2
Outputs:
- layer_out: bfloat16 [256, 104, 768], P(('dp', 'fsdp'))
- token_grad: float32 [256, 104, 768], P(('dp', 'fsdp'))
- grad_project_weight: float32 [768, 2304], P('fsdp')
- grad_project_bias: float32 [1536], P('fsdp')
- grad_output_weight: float32 [768, 768], P('fsdp')
- grad_output_bias: float32 [768], P('fsdp')
- grad_first_gain: float32 [768], P('fsdp')
- grad_first_shift: float32 [768], P('fsdp')
- grad_expand_weight: float32 [768, 3072], P('fsdp')
- grad_expand_bias: float32 [3072], P('fsdp')
- grad_shrink_weight: float32 [3072, 768], P('fsdp')
- grad_shrink_bias: float32 [768], P('fsdp')
- grad_second_gain: float32 [768], P('fsdp')
- grad_second_shift: float32 [768], P('fsdp')
Inputs may be any that keep to these rules, and one draw needn't show every extreme that they name: In every draw some pair's caption has exactly 5 words and some pair's exactly 60; most captions are short (lengths are heavy-tailed toward 5).
All inputs are finite; a program needn't handle non-finite values.
Results may differ from a plain program's by a relative error of at most 0.017.
Values may be sent and summed in bfloat16 or wider, within the bound.
No kernel may reach another device: no remote copies, remote signals or barrier semaphores. Data moves between devices by JAX's collectives and lax.ppermute only.
A program may use at most 128 MiB of HBM per device.

v0:
```python
import functools

import jax
import jax.numpy as jnp
from jax import lax
from jax.experimental import pallas as pl
from jax.experimental.pallas import tpu as pltpu
from jax.sharding import PartitionSpec as P

HEADS = 12
HEAD_DIM = 64
REGIONS = 36
BF16 = jnp.bfloat16
F32 = jnp.float32

COVER = 100 * 10**9

NN = (((1,), (0,)), ((), ()))
NT = (((1,), (1,)), ((), ()))
TN = (((0,), (0,)), ((), ()))


def dot(left, right, dims=NN):
    return lax.dot_general(left, right, dims, preferred_element_type=F32)


def params(mebibytes):
    return pltpu.CompilerParams(vmem_limit_bytes=mebibytes * 1024 * 1024)


def cost(flops=0):
    return pl.CostEstimate(flops=flops, bytes_accessed=0, transcendentals=0)


def whole(shape, buffers=None):
    mode = None if buffers is None else pl.Buffered(buffers)
    return pl.BlockSpec(shape, lambda *at: (0,) * len(shape), pipeline_mode=mode)


HELD = pl.BlockSpec(memory_space=pltpu.VMEM)


def inside(shape, dtype=BF16):
    return pltpu.VMEM(shape, dtype)


def outside(shape, dtype=BF16):
    return pltpu.HBM(shape, dtype)


def in_vmem(values):
    return pltpu.with_memory_space_constraint(values, pltpu.VMEM)


def in_hbm(values):
    return pltpu.with_memory_space_constraint(values, pltpu.HBM)


def tile_of(size, most):
    return max(t for t in range(128, most + 1, 128) if size % t == 0)


def rows_of(count, most):
    fits = [t for t in range(16, most + 1, 16) if count % t == 0]
    return max(fits) if fits else count


CHIPS = (1, 3, 2)


def halves_copies(refs, into, pos, at, high, wide):
    half = wide // 2
    rows = high // 2
    for side in range(2):
        core = pos[1] if side == 0 else 1 - pos[1]
        shard = pos[0] * 2 + core
        yield refs[side], into.at[pl.ds(pl.multiple_of(shard * high, 16), high), :]
        for flip in range(4):
            buffer, first = refs[2 + side * 2 + (flip > 0)], max(flip - 1, 0) * 3 * rows
            up = pos[2] ^ (flip // 2)
            along = pos[3] ^ (flip % 2)
            for place, chip in enumerate(CHIPS):
                shard = (pos[0] ^ chip) * 2 + core
                to_row = pl.multiple_of(shard * high + up * rows, 16)
                to_column = pl.multiple_of(along * half, 128)
                yield (
                    buffer.at[pl.ds(first + place * rows, rows), pl.ds(at, half)],
                    into.at[pl.ds(to_row, rows), pl.ds(to_column, half)],
                )


def stacked_copies(refs, into, pos, high, wide):
    rows = high // 8
    own = pos[2] * 2 + pos[3]
    for side in range(2):
        core = pos[1] if side == 0 else 1 - pos[1]
        shard = pos[0] * 2 + core
        yield refs[side], into.at[pl.ds(pl.multiple_of(shard * high, 16), high), :]
        for place, chip in enumerate(CHIPS):
            shard = (pos[0] ^ chip) * 2 + core
            for plane in range(2):
                for block in range(2):
                    for part in range(2):
                        flip = block * (2 if part == plane else 1)
                        if plane:
                            flip = (1, 3)[block] if part == 0 else (2, 3)[block]
                        to_row = pl.multiple_of(shard * high + ((own ^ flip) * 2 + part) * rows, 16)
                        yield (
                            refs[2 + side * 2 + plane].at[
                                pl.ds((place * 2 + block) * rows, rows), pl.ds(part * wide, wide)
                            ],
                            into.at[pl.ds(to_row, rows), :],
                        )


def natural_copies(refs, into, pos):
    yield refs[0], into


class Weight:
    def __init__(self, shape, arrays, copies=natural_copies):
        self.shape, self.copies = shape, copies
        self.arrays = [in_vmem(array) for array in arrays]

    def specs(self):
        return [HELD] * len(self.arrays)

    def out(self):
        return inside(self.shape)

    def split(self, refs):
        return refs[: len(self.arrays)], refs[len(self.arrays) : -1], refs[-1]

    def arrive(self, refs, full, pos):
        @pl.when(pl.program_id(0) == 0)
        def _():
            for source, target in self.copies(refs, full, pos):
                target[...] = source[...]


def spread_kernel(pos, own, other, bias, hidden, rows, held):
    part = held.shape[2] * 3 // 4
    for at, chip in enumerate((0, *CHIPS)):
        held[(pos[0] ^ chip) * 2 + pos[1]] = own[at * 16 : at * 16 + 16].astype(F32)
        held[(pos[0] ^ chip) * 2 + 1 - pos[1]] = other[at * 16 : at * 16 + 16].astype(F32)
    bias[...] = jnp.zeros_like(bias)
    width = rows.shape[1]
    for shard in range(8):
        for at in range(2):
            to = (shard * 2 + at) * part
            to += width if to >= width else 0
            bias[0:1, to : to + part] = held[shard, at : at + 1, :part]
        for at in range(4):
            to = (shard * 4 + at) * part
            hidden[0:1, to : to + part] = held[shard, 5 + at : 6 + at, :part]
        to = shard * part
        rows[0:3, to : to + part] = held[shard, 2:5, :part]
        rows[3:6, to : to + part] = held[shard, 9:12, :part]


def spread(pos, shards, width, hidden_width):
    shapes = [(1, 3 * width), (1, hidden_width), (8, width)]
    return pl.pallas_call(
        spread_kernel,
        grid_spec=pltpu.PrefetchScalarGridSpec(
            num_scalar_prefetch=1,
            grid=(1,),
            in_specs=[whole((64, 128))] * 2,
            out_specs=[whole(shape) for shape in shapes],
            scratch_shapes=[pltpu.VMEM((8, 16, 128), F32)],
        ),
        out_shape=[jax.ShapeDtypeStruct(shape, F32) for shape in shapes],
        compiler_params=params(4),
        cost_estimate=cost(COVER),
        name="spread",
    )(pos, *shards)


def bundle_kernel(joined, first, second, hidden, out):
    part = out.shape[2] * 3 // 4
    out[...] = jnp.zeros_like(out)
    for shard in range(8):
        for at in range(2):
            of = (shard * 2 + at) * part
            out[shard, at : at + 1, :part] = joined[0:1, of : of + part]
        for at in range(4):
            of = (shard * 4 + at) * part
            out[shard, 5 + at : 6 + at, :part] = hidden[0:1, of : of + part]
        of = shard * part
        out[shard, 2:5, :part] = first[0:3, of : of + part]
        out[shard, 9:12, :part] = second[0:3, of : of + part]


def bundle(joined, first, second, hidden):
    return pl.pallas_call(
        bundle_kernel,
        out_shape=jax.ShapeDtypeStruct((8, 16, 128), F32),
        compiler_params=params(4),
        cost_estimate=cost(),
        name="bundle",
    )(joined, first, second, hidden)


def step_of(size):
    return pl.ds(pl.multiple_of(pl.program_id(0) * size, 16), size)


def columns_of(size):
    return pl.ds(pl.multiple_of(pl.program_id(0) * size, 128), size)


def join_kernel(pos, tokens, bias, *rest, weight, tile):
    pieces, (out, kept), (full, sem) = rest[: len(weight.arrays)], rest[-4:-2], rest[-2:]
    weight.arrive(pieces, full, pos)
    write = pltpu.make_async_copy(full, kept, sem)

    @pl.when(pl.program_id(0) == 0)
    def _():
        write.start()

    out[...] = (dot(tokens[...], full[:, columns_of(tile)]) + bias[...]).astype(BF16)

    @pl.when(pl.program_id(0) == pl.num_programs(0) - 1)
    def _():
        write.wait()


def join(pos, token_rows, weight, bias):
    rows, width = token_rows.shape
    columns = weight.shape[1]
    tile = tile_of(columns, 768)
    return pl.pallas_call(
        functools.partial(join_kernel, weight=weight, tile=tile),
        grid_spec=pltpu.PrefetchScalarGridSpec(
            num_scalar_prefetch=1,
            grid=(columns // tile,),
            in_specs=[whole((rows, width), 1), pl.BlockSpec((1, tile), lambda i, p: (0, i))] + weight.specs(),
            out_specs=[pl.BlockSpec((rows, tile), lambda i, p: (0, i)), pl.BlockSpec(memory_space=pltpu.HBM)],
            scratch_shapes=[pltpu.VMEM(weight.shape, BF16), pltpu.SemaphoreType.DMA(())],
        ),
        out_shape=[outside((rows, columns)), outside(weight.shape)],
        compiler_params=params(15),
        cost_estimate=cost(),
        name="join",
    )(pos, token_rows, bias, *weight.arrays)


def head_stack(block, low_half, padded):
    rows = block.shape[0]
    filler = jnp.zeros((padded - rows, block.shape[1]), F32)
    first = jnp.where(low_half, block, 0.0)
    second = jnp.where(low_half, 0.0, block)
    return jnp.concatenate([first, filler, second, filler], axis=0).astype(BF16)


def attend_kernel(captions, joined, context, probs):
    seq = joined.shape[1]
    width = context.shape[2]
    padded = probs.shape[3] // 2
    valid = captions[pl.program_id(0)] + 2 + REGIONS
    keep = lax.broadcasted_iota(jnp.int32, (seq, 2 * padded), 0) < valid
    low_half = lax.broadcasted_iota(jnp.int32, (1, 2 * HEAD_DIM), 1) < HEAD_DIM
    places = [pair * 2 * HEAD_DIM for pair in range(HEADS // 2)]
    scores = []
    for at in places:
        query = joined[0, :, at : at + 2 * HEAD_DIM].astype(F32)
        keys = joined[0, :, width + at : width + at + 2 * HEAD_DIM]
        scores.append(dot(keys, head_stack(query, low_half, padded), NT) * HEAD_DIM ** (-0.5))
    probabilities = []
    for score in scores:
        score = jnp.where(keep, score, -1000000000.0)
        grown = jnp.exp(score - jnp.max(score, axis=0, keepdims=True))
        total = jnp.sum(grown, axis=0, keepdims=True)
        probabilities.append((grown * (1.0 / total)).astype(BF16))
    for pair, at in enumerate(places):
        values = joined[0, :, 2 * width + at : 2 * width + at + 2 * HEAD_DIM]
        mixed = dot(probabilities[pair], values, TN)
        probs[0, pair] = probabilities[pair]
        context[0, :, at : at + 2 * HEAD_DIM] = jnp.where(
            low_half, mixed[:seq], mixed[padded : padded + seq]
        ).astype(BF16)


def attend(joined, captions):
    pairs, seq, columns = joined.shape
    width = columns // 3
    padded = (seq + 127) // 128 * 128
    return pl.pallas_call(
        attend_kernel,
        grid_spec=pltpu.PrefetchScalarGridSpec(
            num_scalar_prefetch=1,
            grid=(pairs,),
            in_specs=[pl.BlockSpec((1, seq, columns), lambda i, c: (i, 0, 0))],
            out_specs=[
                pl.BlockSpec((1, seq, width), lambda i, c: (i, 0, 0)),
                pl.BlockSpec((1, HEADS // 2, seq, 2 * padded), lambda i, c: (i, 0, 0, 0)),
            ],
        ),
        out_shape=[
            inside((pairs, seq, width)),
            outside((pairs, HEADS // 2, seq, 2 * padded)),
        ],
        compiler_params=params(8),
        cost_estimate=cost(),
        name="attend",
    )(captions, in_hbm(joined))


def attend_back_kernel(joined, probs, grads, out, sums):
    seq = joined.shape[1]
    width = grads.shape[2]
    padded = probs.shape[3] // 2
    low_half = lax.broadcasted_iota(jnp.int32, (1, 2 * HEAD_DIM), 1) < HEAD_DIM

    @pl.when(pl.program_id(0) == 0)
    def _():
        sums[...] = jnp.zeros_like(sums)

    places = [pair * 2 * HEAD_DIM for pair in range(HEADS // 2)]
    prob_grads, grad_stacks = [], []
    for at in places:
        values = joined[0, :, 2 * width + at : 2 * width + at + 2 * HEAD_DIM]
        grad_stacks.append(head_stack(grads[0, :, at : at + 2 * HEAD_DIM].astype(F32), low_half, padded))
        prob_grads.append(dot(values, grad_stacks[-1], NT))
    score_grads = []
    for pair, prob_grad in enumerate(prob_grads):
        prob = probs[0, pair].astype(F32)
        row_dot = jnp.sum(prob * prob_grad, axis=0, keepdims=True)
        score_grads.append((prob * (prob_grad - row_dot) * HEAD_DIM ** (-0.5)).astype(BF16))
    results = []
    for pair, at in enumerate(places):
        query = joined[0, :, at : at + 2 * HEAD_DIM].astype(F32)
        keys = joined[0, :, width + at : width + at + 2 * HEAD_DIM]
        mixed = dot(score_grads[pair], keys, TN)
        query_grad = jnp.where(low_half, mixed[:seq], mixed[padded : padded + seq])
        keys_grad = dot(score_grads[pair], head_stack(query, low_half, padded))
        results.append((query_grad, keys_grad, dot(probs[0, pair], grad_stacks[pair])))
    for at, blocks in zip(places, results):
        for part, block in enumerate(blocks):
            out[0, :, part * width + at : part * width + at + 2 * HEAD_DIM] = block.astype(BF16)
            if part != 1:
                to = part // 2 * width + at
                sums[:, to : to + 2 * HEAD_DIM] += jnp.sum(block, axis=0, keepdims=True)


def attend_back(joined, probs, grads):
    pairs, seq, columns = joined.shape
    width = columns // 3
    padded = probs.shape[3] // 2
    return pl.pallas_call(
        attend_back_kernel,
        grid=(pairs,),
        in_specs=[
            pl.BlockSpec((1, seq, columns), lambda i: (i, 0, 0)),
            pl.BlockSpec((1, HEADS // 2, seq, 2 * padded), lambda i: (i, 0, 0, 0)),
            pl.BlockSpec((1, seq, width), lambda i: (i, 0, 0)),
        ],
        out_specs=[
            pl.BlockSpec((1, seq, columns), lambda i: (i, 0, 0)),
            pl.BlockSpec((1, 2 * width), lambda i: (0, 0)),
        ],
        out_shape=[
            inside((pairs, seq, columns)),
            jax.ShapeDtypeStruct((1, 2 * width), F32),
        ],
        compiler_params=params(10),
        cost_estimate=cost(),
        name="attend_back",
    )(in_hbm(joined), in_hbm(probs), in_vmem(grads))


def norm_parts(values):
    centred = values - jnp.mean(values, axis=-1, keepdims=True)
    spread = jnp.mean(centred * centred, axis=-1, keepdims=True)
    scale = lax.rsqrt(spread + 1e-05)
    return centred * scale, scale


def norm_back(upstream, unit, scale, gain):
    scaled = upstream * gain
    return scale * (
        scaled
        - jnp.mean(scaled, axis=-1, keepdims=True)
        - unit * jnp.mean(scaled * unit, axis=-1, keepdims=True)
    )


def add_sums(sums, rows):
    for at, values in enumerate(rows):
        sums[at : at + 1, :] += jnp.sum(values, axis=0, keepdims=True)


def chunked(count, load, use):
    ready = load(0)
    for at in range(count):
        following = load(at + 1) if at + 1 < count else None
        use(at, ready)
        ready = following


def chunk_slices(rows, most):
    tile = rows_of(rows, most)
    return [slice(at, at + tile) for at in range(0, rows, tile)]


def first_kernel(pos, context, bias, tokens, gain, shift, *rest, weight):
    pieces, (unit, scale, normed_low), full = weight.split(rest)
    weight.arrive(pieces, full, pos)
    chunks = chunk_slices(tokens.shape[0], 416)

    def normalise(at, branch):
        rows = chunks[at]
        unit_rows, scale_rows = norm_parts(tokens[rows, :].astype(F32) + (branch + bias[...]))
        unit[rows, :] = unit_rows
        scale[rows, :] = scale_rows
        normed_low[rows, :] = (unit_rows * gain[...] + shift[...]).astype(BF16)

    chunked(len(chunks), lambda at: dot(context[chunks[at], :], full[...]), normalise)


def first_norm(pos, context, weight, bias, token_rows, gain, shift):
    rows, width = token_rows.shape
    row = whole((1, width))
    return pl.pallas_call(
        functools.partial(first_kernel, weight=weight),
        grid_spec=pltpu.PrefetchScalarGridSpec(
            num_scalar_prefetch=1,
            grid=(1,),
            in_specs=[HELD, row, HELD, row, row] + weight.specs(),
            out_specs=[HELD] * 4,
        ),
        out_shape=[inside((rows, width), F32), inside((rows, 1), F32), inside((rows, width)), weight.out()],
        compiler_params=params(10),
        cost_estimate=cost(),
        name="first_norm",
    )(pos, in_vmem(context), bias, in_vmem(token_rows), gain, shift, *weight.arrays)


def expand_kernel(pos, normed_low, bias, *rest, weight, tile):
    pieces, (active, slope), full = weight.split(rest)
    weight.arrive(pieces, full, pos)
    at = columns_of(tile)
    expand = dot(normed_low[...], full[:, at]) + bias[...]
    half = 0.5 * (1.0 + lax.erf(expand * 0.7071067811865476))
    active[:, at] = (expand * half).astype(BF16)
    slope[:, at] = (half + expand * jnp.exp(-0.5 * expand * expand) * 0.3989422804014327).astype(BF16)


def expand_act(pos, normed_low, weight, bias):
    rows, width = normed_low.shape
    columns = weight.shape[1]
    tile = tile_of(columns, 768)
    return pl.pallas_call(
        functools.partial(expand_kernel, weight=weight, tile=tile),
        grid_spec=pltpu.PrefetchScalarGridSpec(
            num_scalar_prefetch=1,
            grid=(columns // tile,),
            in_specs=[HELD, pl.BlockSpec((1, tile), lambda i, p: (0, i))] + weight.specs(),
            out_specs=[HELD] * 3,
        ),
        out_shape=[inside((rows, columns))] * 2 + [weight.out()],
        compiler_params=params(12),
        cost_estimate=cost(),
        name="expand_act",
    )(pos, in_vmem(normed_low), bias, *weight.arrays)


def second_kernel(pos, captions, active, bias, unit, gain, shift, gain2, shift2, cotangent, *rest, weight, seq):
    pieces, (out, low, grad, sums), full, (held, sems) = *weight.split(rest[:-2]), rest[-2:]
    weight.arrive(pieces, full, pos)
    sums[...] = jnp.zeros_like(sums)
    tile = rows_of(held.shape[0], 4 * seq)
    count = held.shape[0] // tile

    def write(at):
        rows = pl.ds(pl.multiple_of(at * tile, 16), tile)
        return pltpu.make_async_copy(held.at[rows, :], out.at[rows, :], sems.at[at])

    def chunk(at, carry):
        rows = pl.ds(pl.multiple_of(at * tile, 16), tile)
        normed = unit[rows, :] * gain[...] + shift[...]
        unit2, scale2 = norm_parts(normed + (dot(active[rows, :], full[...]) + bias[...]))
        held[rows, :] = (unit2 * gain2[...] + shift2[...]).astype(BF16)
        write(at).start()
        row = lax.broadcasted_iota(jnp.int32, (tile, 1), 0)
        live = jnp.zeros(row.shape, jnp.bool_)
        for pair in range(tile // seq):
            valid = captions[at * (tile // seq) + pair] + 2 + REGIONS
            live = live | ((row >= pair * seq) & (row < pair * seq + valid))
        upstream = jnp.where(live, cotangent[rows, :].astype(F32), 0.0)
        second = norm_back(upstream, unit2, scale2, gain2[...])
        grad[rows, :] = second
        low[rows, :] = second.astype(BF16)
        add_sums(sums, (second, upstream * unit2, upstream))
        return carry

    lax.fori_loop(0, count, chunk, 0)
    for at in range(count):
        write(at).wait()


def second_norm(pos, captions, active, weight, bias, unit, gain, shift, gain2, shift2, cotangent, seq):
    rows, width = unit.shape
    row = whole((1, width))
    return pl.pallas_call(
        functools.partial(second_kernel, weight=weight, seq=seq),
        grid_spec=pltpu.PrefetchScalarGridSpec(
            num_scalar_prefetch=2,
            grid=(1,),
            in_specs=[HELD, row, HELD, row, row, row, row, HELD] + weight.specs(),
            out_specs=[pl.BlockSpec(memory_space=pltpu.HBM), HELD, HELD, whole((8, width)), HELD],
            scratch_shapes=[pltpu.VMEM((rows, width), BF16), pltpu.SemaphoreType.DMA((rows // 16,))],
        ),
        out_shape=[
            outside((rows, width)),
            inside((rows, width)),
            inside((rows, width), F32),
            jax.ShapeDtypeStruct((8, width), F32),
            weight.out(),
        ],
        compiler_params=params(12),
        cost_estimate=cost(),
        name="second_norm",
    )(pos, captions, in_vmem(active), bias, in_vmem(unit), gain, shift, gain2, shift2, in_vmem(cotangent), *weight.arrays)


def hidden_back_kernel(low, weight, slope, out, sums):
    at = columns_of(sums.shape[1])
    grad = dot(low[...], weight[at, :], NT) * slope[:, at].astype(F32)
    out[:, at] = grad.astype(BF16)
    sums[...] = jnp.sum(grad, axis=0, keepdims=True)


def hidden_back(low, weight, slope):
    rows, width = low.shape
    hidden = weight.shape[0]
    tile = tile_of(hidden, 768)
    return pl.pallas_call(
        hidden_back_kernel,
        grid=(hidden // tile,),
        in_specs=[HELD] * 3,
        out_specs=[HELD, pl.BlockSpec((1, tile), lambda i: (0, i))],
        out_shape=[inside((rows, hidden)), jax.ShapeDtypeStruct((1, hidden), F32)],
        compiler_params=params(10),
        cost_estimate=cost(),
        name="hidden_back",
    )(in_vmem(low), in_vmem(weight), in_vmem(slope))


def first_back_kernel(hidden, weight, second, unit, scale, gain, out_weight, grad, low, context_grad, sums):
    sums[...] = jnp.zeros_like(sums)
    chunks = chunk_slices(grad.shape[0], 416)
    waiting = []

    def pass_on():
        rows, first_low = waiting.pop()
        context_grad[rows, :] = dot(first_low, out_weight[...], NT).astype(BF16)

    def normalise(at, product):
        rows = chunks[at]
        unit_rows = unit[rows, :]
        normed_grad = product + second[rows, :]
        first = norm_back(normed_grad, unit_rows, scale[rows, :], gain[...])
        grad[rows, :] = first
        first_low = first.astype(BF16)
        low[rows, :] = first_low
        add_sums(sums, (first, normed_grad * unit_rows, normed_grad))
        if waiting:
            pass_on()
        waiting.append((rows, first_low))

    chunked(len(chunks), lambda at: dot(hidden[chunks[at], :], weight[...], NT), normalise)
    pass_on()


def first_back(hidden, weight, second, unit, scale, gain, out_weight):
    rows, width = second.shape
    return pl.pallas_call(
        first_back_kernel,
        grid=(1,),
        in_specs=[HELD] * 5 + [whole((1, width)), HELD],
        out_specs=[HELD, HELD, HELD, whole((8, width))],
        out_shape=[
            inside((rows, width), F32),
            inside((rows, width)),
            inside((rows, width)),
            jax.ShapeDtypeStruct((8, width), F32),
        ],
        compiler_params=params(13),
        cost_estimate=cost(COVER),
        name="first_back",
    )(in_vmem(hidden), in_vmem(weight), in_vmem(second), in_vmem(unit), in_vmem(scale), gain, in_vmem(out_weight))


def token_back_kernel(grads, weight, first, out):
    at = step_of(out.shape[0])
    out[...] = dot(grads[at, :], weight[...], NT) + first[at, :]


def token_back(grads, weight, first):
    rows, width = first.shape
    tile = rows_of(rows, 416)
    return pl.pallas_call(
        token_back_kernel,
        grid=(rows // tile,),
        in_specs=[HELD] * 3,
        out_specs=pl.BlockSpec((tile, width), lambda i: (i, 0)),
        out_shape=outside((rows, width), F32),
        compiler_params=params(9),
        cost_estimate=cost(),
        name="token_back",
    )(in_vmem(grads), in_vmem(weight), in_vmem(first))


def weight_grad_kernel(left, right, out):
    out[...] = dot(left[...], right[...], TN).astype(BF16)


def weight_grad(left, right):
    rows, height = left.shape
    columns = right.shape[1]
    tile = tile_of(columns, 768)
    high = tile_of(height, 768)
    return pl.pallas_call(
        weight_grad_kernel,
        grid=(height // high, columns // tile),
        in_specs=[
            pl.BlockSpec((rows, high), lambda i, j: (0, i)),
            pl.BlockSpec((rows, tile), lambda i, j: (0, j)),
        ],
        out_specs=pl.BlockSpec((high, tile), lambda i, j: (i, j)),
        out_shape=outside((height, columns)),
        compiler_params=params(24),
        cost_estimate=cost(),
        name="weight_grad",
    )(left, right)


def store_halves(out, core, grads, pos, along, extra):
    rows, wide = out.shape[3], grads.shape[1]
    for chip in range(4):
        for up in range(2):
            at = ((chip * 2 + core) * 2 + up) * rows
            to = (chip ^ pos[0], up ^ pos[2], along ^ pos[3])
            out[(*to, slice(None), slice(0, wide))] = grads[at : at + rows].astype(BF16)
            if extra is not None:
                out[(*to, slice(None), slice(wide, None))] = jnp.zeros((rows, 128), BF16)
                out[(*to, slice(0, 16), slice(wide, None))] = extra[chip * 2 + core].astype(BF16)


def store_stacked(out, core, grads, pos, chip):
    rows, wide = out.shape[3], grads.shape[1]
    for quarter in range(4):
        for part in range(2):
            at = ((core * 4 + quarter) * 2 + part) * rows
            to = (chip ^ pos[0], (quarter // 2) ^ pos[2], (quarter % 2) ^ pos[3])
            out[(*to, slice(None), slice(part * wide, (part + 1) * wide))] = grads[at : at + rows].astype(BF16)


def by_core(pos, mine, theirs, store):
    for core in range(2):

        @pl.when(pos[1] == core)
        def _(core=core):
            store(mine, core)
            store(theirs, 1 - core)


def halves_grad_kernel(pos, left, right, *rest):
    extra, (mine, theirs) = (rest[0] if len(rest) == 3 else None), rest[-2:]
    along, half = pl.program_id(0), right.shape[1] // 2
    grads = dot(left[...], right[:, columns_of(half)], TN)
    by_core(pos, mine, theirs, lambda out, core: store_halves(out, core, grads, pos, along, extra))


def stacked_grad_kernel(pos, left, right, mine, theirs):
    high = left.shape[1] // 4
    grads = dot(left[:, columns_of(2 * high)], right[...], TN)
    for part in range(2):
        chip, block = pl.program_id(0) * 2 + part, grads[part * high : (part + 1) * high]
        by_core(pos, mine, theirs, lambda out, core: store_stacked(out, core, block, pos, chip))


def pieces_grad(kernel, name, pos, left, right, shape, extra=()):
    out = inside((4, 2, 2) + shape)
    return pl.pallas_call(
        kernel,
        grid_spec=pltpu.PrefetchScalarGridSpec(
            num_scalar_prefetch=1,
            grid=(2,),
            in_specs=[HELD, HELD] + [whole(array.shape) for array in extra],
            out_specs=[HELD, HELD],
        ),
        out_shape=[out, out],
        compiler_params=params(13),
        cost_estimate=cost(),
        name=name,
    )(pos, in_vmem(left), in_vmem(right), *extra)


def halves_grad(pos, left, right, extra=None):
    shape = (left.shape[1] // 16, right.shape[1] // 2 + (0 if extra is None else 128))
    more = () if extra is None else (extra,)
    return pieces_grad(halves_grad_kernel, "halves_grad", pos, left, right, shape, more)


def stacked_grad(pos, left, right):
    shape = (left.shape[1] // 64, 2 * right.shape[1])
    return pieces_grad(stacked_grad_kernel, "stacked_grad", pos, left, right, shape)


def held_call(kernel, name, outs, values, flops=0):
    return pl.pallas_call(
        kernel,
        in_specs=[HELD] * len(values),
        out_specs=[HELD] * len(outs),
        out_shape=[inside(out) for out in outs],
        compiler_params=params(4),
        cost_estimate=cost(flops),
        name=name,
    )(*map(in_vmem, values))


def add(*terms):
    total = terms[0].astype(F32)
    for term in terms[1:]:
        total += term.astype(F32)
    return total


FIRST = 1024


def shrink_sum_kernel(mine, theirs, keep, near, kept, send):
    for chip in range(4):
        for flip in range(4):
            pick = (chip, flip // 2, flip % 2)
            total = add(mine[pick], theirs[pick]).astype(BF16)
            (keep, near)[chip % 2][chip // 2, flip] = total[:, :FIRST]
            (kept, send)[flip % 2][flip // 2, chip] = total[:, FIRST:]


def shrink_sum(mine, theirs):
    rows, wide = mine.shape[3:]
    outs = [(2, 4, rows, FIRST)] * 2 + [(2, 4, rows, wide - FIRST)] * 2
    return held_call(shrink_sum_kernel, "shrink_sum", outs, [mine, theirs])


def core_split_kernel(*refs, count):
    outs = refs[-6:]
    for half in range(2):
        own, later, send = outs[3 * half : 3 * half + 3]
        first = 1 + half
        for flip, out in ((0, own), (3 - first, later), (first, send.at[0]), (3, send.at[1])):
            at = 0
            for mine, theirs in zip(refs[:count], refs[count : 2 * count]):
                wide = mine.shape[4]
                for chip in range(2):
                    pick = (2 * half + chip, flip // 2, flip % 2)
                    out[chip, :, at : at + wide] = add(mine[pick], theirs[pick]).astype(BF16)
                at += wide
            if len(refs) > 2 * count + 6:
                near, far = refs[2 * count : 2 * count + 2]
                wide = near.shape[2] // 4
                for chip in range(2):
                    columns = slice((2 * half + chip) * wide, (2 * half + chip + 1) * wide)
                    out[chip, :, at:] = add(near[flip, :, columns], far[flip, :, columns]).astype(BF16)


def core_split(mine, theirs, more=()):
    shape = (2, mine[0].shape[3], sum(m.shape[4] for m in mine) + sum(m.shape[2] // 8 for m in more))
    kernel = functools.partial(core_split_kernel, count=len(mine))
    return held_call(kernel, "core_split", [shape, shape, (2,) + shape] * 2, [*mine, *theirs, *more])


def middle_sum_kernel(*refs):
    for half in range(2):
        own, later, received = refs[3 * half : 3 * half + 3]
        refs[6 + 2 * half][...] = add(own[...], received[0]).astype(BF16)
        refs[7 + 2 * half][...] = add(later[...], received[1]).astype(BF16)


def middle_sum(parts):
    return held_call(middle_sum_kernel, "middle_sum", [parts[0].shape] * 4, parts)


def split_sum_kernel(own, received, own_too, received_too, keep, near, *rest):
    for chip in range(4):
        one, two = (own, received) if chip < 2 else (own_too, received_too)
        total = add(one[chip % 2], two[chip % 2]).astype(BF16)
        wide = keep.shape[2]
        (keep, near)[chip % 2][chip // 2] = total[:, :wide]
        if rest:
            part = total.shape[1] - wide
            rest[0][:, chip * part : (chip + 1) * part] = total[:, wide:]


def split_sum(parts, more=0, flops=0):
    _, rows, wide = parts[0].shape
    outs = [(2, rows, wide - more)] * 2 + ([(rows, 4 * more)] if more else [])
    return held_call(split_sum_kernel, "split_sum", outs, parts, flops)


def ahead_sum_kernel(one, two, keep, near, keep_out, near_out):
    wide = one.shape[2]
    for chip in range(4):
        source, out = (keep, keep_out) if chip % 2 == 0 else (near, near_out)
        out[chip // 2, :, :wide] = add(one[chip], two[chip]).astype(BF16)
        out[chip // 2, :, wide:] = source[chip // 2]


def ahead_sum(one, two, keep, near):
    shape = keep.shape[:2] + (keep.shape[2] + one.shape[2],)
    return held_call(ahead_sum_kernel, "ahead_sum", [shape] * 2, [one, two, keep, near])


def pair_sum_kernel(keep, received, one, two):
    one[...] = add(keep[0], received[0]).astype(BF16)
    two[...] = add(keep[1], received[1]).astype(BF16)


def pair_sum(keep, received, flops=0):
    return held_call(pair_sum_kernel, "pair_sum", [keep.shape[1:]] * 2, [keep, received], flops)


def last_sum_kernel(*refs, counts):
    out, at = refs[-1], 0
    for count in counts:
        terms, refs = refs[:count], refs[count:]
        wide = terms[0].shape[1]
        out[:, at : at + wide] = add(*(term[...] for term in terms)).astype(BF16)
        at += wide


def last_sum(*groups):
    kernel = functools.partial(last_sum_kernel, counts=[len(group) for group in groups])
    shape = (groups[0][0].shape[0], sum(group[0].shape[1] for group in groups))
    return held_call(kernel, "last_sum", [shape], [part for group in groups for part in group])[0]


def place_kernel(pos, *refs, layout):
    parts, outs = refs[:4], refs[4:]
    rows = parts[0].shape[0]
    for flip, part in enumerate(parts):
        up, along = pos[2] ^ (flip // 2), pos[3] ^ (flip % 2)
        at = 0
        for (kind, wide), out in zip(layout, outs):
            if kind == "halves":
                to_row = pl.multiple_of(up * rows, 16)
                to_column = pl.multiple_of(along * wide, 128)
                out[pl.ds(to_row, rows), pl.ds(to_column, wide)] = part[:, at : at + wide].astype(F32)
            elif kind == "stacked":
                for side in range(2):
                    to_row = pl.multiple_of(((up * 2 + along) * 2 + side) * rows, 16)
                    from_column = at + side * (wide // 2)
                    out[pl.ds(to_row, rows), :] = part[:, from_column : from_column + wide // 2].astype(F32)
            else:

                @pl.when((up == 0) & (along == 0))
                def _(part=part, at=at):
                    row = 0
                    for vector in outs[len(layout) - 1 :]:
                        for to in range(0, vector.shape[1], 96):
                            vector[:, to : to + 96] = part[row : row + 1, at : at + 96].astype(F32)
                            row += 1

            at += wide


def place(pos, parts, layout, sizes=()):
    rows = parts[0].shape[0]
    shapes = {
        "halves": lambda wide: (2 * rows, 2 * wide),
        "stacked": lambda wide: (8 * rows, wide // 2),
    }
    outs = [jax.ShapeDtypeStruct(shapes[kind](wide), F32) for kind, wide in layout if kind != "small"]
    outs += [jax.ShapeDtypeStruct((1, size), F32) for size in sizes]
    return pl.pallas_call(
        functools.partial(place_kernel, layout=layout),
        grid_spec=pltpu.PrefetchScalarGridSpec(
            num_scalar_prefetch=1,
            grid=(1,),
            in_specs=[HELD] * 4,
            out_specs=[whole(out.shape, 1) for out in outs],
        ),
        out_shape=outs,
        compiler_params=params(10),
        cost_estimate=cost(),
        name="place",
    )(pos, *map(in_vmem, parts))


def from_core(values):
    return lax.ppermute(values, "fsdp", [(i, i ^ 1) for i in range(8)])


def from_plane(values):
    parts = values if isinstance(values, (list, tuple)) else [values] * 3
    return [
        lax.ppermute(part, "dp", [(i, i ^ flip) for i in range(4)]) for flip, part in zip((1, 2, 3), parts)
    ]


def from_x(values):
    return lax.ppermute(values, "dp", [(i, i ^ 1) for i in range(4)])


def from_y(values):
    return lax.ppermute(values, "dp", [(i, i ^ 2) for i in range(4)])


def from_chips(values):
    return [from_chip(values, flip) for flip in CHIPS]


def from_chip(values, flip):
    return lax.ppermute(values, "fsdp", [(i, i ^ (2 * flip)) for i in range(8)])


def below_kernel(*refs):
    at = 0
    for ref in refs[:-1]:
        rows, wide = ref.shape[0], refs[-1].shape[1]
        refs[-1][at : at + rows] = ref[:, :wide]
        at += rows


def below(*parts, wide=None, flops=0):
    rows = sum(part.shape[0] for part in parts)
    return pl.pallas_call(
        below_kernel,
        in_specs=[HELD] * len(parts),
        out_specs=HELD,
        out_shape=inside((rows, wide or parts[0].shape[1])),
        compiler_params=params(4),
        cost_estimate=cost(flops),
        name="below",
    )(*map(in_vmem, parts))


def pick_kernel(pos, shard, out):
    rows, wide = out.shape[0] // 2, shard.shape[1]
    own = pos[2] * 2 + pos[3]
    for block, part, flip in ((0, 0, 0), (0, 1, 0), (1, 0, 2), (1, 1, 1)):
        from_row = pl.multiple_of(((own ^ flip) * 2 + part) * rows, 16)
        out[block * rows : (block + 1) * rows, part * wide : (part + 1) * wide] = shard[pl.ds(from_row, rows), :]


def pick(pos, shard):
    return pl.pallas_call(
        pick_kernel,
        grid_spec=pltpu.PrefetchScalarGridSpec(
            num_scalar_prefetch=1, grid=(1,), in_specs=[whole(shard.shape, 1)], out_specs=HELD
        ),
        out_shape=inside((shard.shape[0] // 4, 2 * shard.shape[1])),
        compiler_params=params(4),
        cost_estimate=cost(),
        name="pick",
    )(pos, shard)


def left_right_kernel(whole_ref, left, right):
    half = left.shape[1]
    left[...] = whole_ref[:, :half]
    right[...] = whole_ref[:, half:]


def left_right(values):
    rows, wide = values.shape
    return held_call(left_right_kernel, "left_right", [(rows, wide // 2)] * 2, [values])


def beside_kernel(left, right, out):
    half = left.shape[1]
    out[:, :half] = left[...]
    out[:, half:] = right[...]


def beside(left, right):
    rows, wide = left.shape
    return held_call(beside_kernel, "beside", [(rows, 2 * wide)], [left, right])[0]


def after(values, *others):
    return lax.optimization_barrier((values, others))[0]


def half_of(pos, shard):
    rows, wide = shard.shape[0] // 2, shard.shape[1] // 2
    return lax.dynamic_slice(shard, (pos[2] * rows, pos[3] * wide), (rows, wide))


def both_cores(pieces):
    return [*pieces, *(from_core(piece) for piece in pieces)]


def gather(values):
    return lax.all_gather(values, "fsdp", axis=0, tiled=True)


def local(
    pieces,
    tokens,
    captions,
    cotangent,
    project_weight,
    project_bias,
    output_weight,
    output_bias,
    first_gain,
    first_shift,
    expand_weight,
    expand_bias,
    shrink_weight,
    shrink_bias,
    second_gain,
    second_shift,
):
    pairs, seq, width = tokens.shape
    rows = pairs * seq
    parts = lax.axis_size("fsdp")
    token_rows = tokens.reshape(rows, width)
    cot_rows = cotangent.reshape(rows, width)

    vectors = (project_bias, output_bias, first_gain, first_shift, expand_bias, shrink_bias, second_gain, second_shift)
    widths = [vector.shape[0] for vector in vectors]
    replica, part = lax.axis_index("dp"), lax.axis_index("fsdp")
    pos = jnp.stack([part // 2, part % 2, replica // 2, replica % 2]).astype(jnp.int32)
    shapes = [(parts * shard.shape[0], shard.shape[1]) for shard in (project_weight, output_weight, expand_weight, shrink_weight)]
    if pieces:
        chips_p = from_chips(half_of(pos, project_weight))
        sibling_p = from_core(project_weight)
        held = jnp.concatenate([vector.reshape(-1, 96) for vector in vectors], axis=0)
        held = jnp.pad(held, ((0, 4), (0, 32)))
        quarter_e = [half_of(pos, expand_weight), half_of(pos, output_weight), jnp.pad(held, ((0, 32), (0, 0)))]
        quarter_e = jnp.concatenate(quarter_e, axis=1)
        wide_e = quarter_e.shape[1] - 128
        chips_p = after(chips_p, sibling_p, quarter_e)
        mine_p = below(*chips_p)
        quarter_e = after(quarter_e, *chips_p)
        far_e = from_chip(quarter_e, 2)
        near_e = [from_chip(quarter_e, 1), from_chip(far_e, 1)]
        plane_p = from_plane(mine_p)
        plane_p = below(*plane_p, flops=COVER)
        near_e = after(near_e, plane_p)
        other_p = [from_core(mine_p), from_core(plane_p)]

        def halves(shape, shard, sibling, group, at):
            copies = functools.partial(halves_copies, at=at, high=shard.shape[0], wide=shard.shape[1])
            return Weight(shape, [shard, sibling, *group], copies)

        project = halves(shapes[0], project_weight, sibling_p, (mine_p, plane_p, *other_p), 0)
        quarter_s = pick(pos, after(shrink_weight, quarter_e))
        quarter_s = after(quarter_s, plane_p)
        far_s = from_chip(quarter_s, 2)
        mine_e = below(*near_e, far_e, wide=wide_e)
        plane_e = from_plane(mine_e)
        held = jnp.concatenate([held, *(chip[:16, wide_e:] for chip in (*near_e, far_e))], axis=0)
        held = after(held, mine_e)
        bias_full, hidden_bias, rows6 = spread(pos, [held, from_core(held)], width, expand_weight.shape[1])
        out_bias, gain1, shift1, down_bias, gain2, shift2 = (rows6[at : at + 1] for at in range(6))
    else:
        project, output, expand, shrink = (
            Weight(shape, [gather(shard)])
            for shape, shard in zip(shapes, (project_weight, output_weight, expand_weight, shrink_weight))
        )
        packed = gather(jnp.concatenate(vectors)[None, :])
        full, at = [], 0
        for size in widths:
            full.append(packed[:, at : at + size].reshape(1, parts * size).astype(F32))
            at += size
        bias_row, out_bias, gain1, shift1, hidden_bias, down_bias, gain2, shift2 = full
        bias_full = jnp.concatenate([bias_row[:, :width], jnp.zeros((1, width), F32), bias_row[:, width:]], axis=1)

    joined, project = join(pos, token_rows, project, bias_full)
    joined3 = joined.reshape(pairs, seq, 3 * width)
    if pieces:
        near_s = from_chip(after(quarter_s, joined), 1)
    context, probs = attend(joined3, captions)
    context_rows = context.reshape(rows, width)
    if pieces:
        far_s = after(far_s, context)
        near_s = [near_s, from_chip(far_s, 1)]
        plane_e = below(*after(plane_e, far_s))
        mine_s = below(*after(near_s, plane_e), far_s, flops=COVER)
        left_s, right_s = left_right(mine_s)
        plane_s = [from_x(left_s), from_y(right_s)]
        context_rows = after(context_rows, mine_s)
        group_e = (mine_e, plane_e, *after([from_core(mine_e), from_core(plane_e)], mine_s))
        sibling_e = from_core(after(expand_weight, joined))
        sibling_o = from_core(after(output_weight, joined))
        expand = halves(shapes[2], expand_weight, sibling_e, group_e, 0)
        output = halves(shapes[1], output_weight, sibling_o, group_e, expand_weight.shape[1] // 2)
    unit1, scale1, normed_low, output = first_norm(pos, context_rows, output, out_bias, token_rows, gain1, shift1)
    active, slope, expand = expand_act(pos, normed_low, expand, hidden_bias)
    if pieces:
        plane_s = beside(*after(plane_s, active))
        other_s = [from_core(mine_s), from_core(plane_s)]
        sibling_s = from_core(after(shrink_weight, active))
        shrink = Weight(
            shapes[3],
            [shrink_weight, sibling_s, mine_s, plane_s, *other_s],
            functools.partial(stacked_copies, high=shrink_weight.shape[0], wide=shrink_weight.shape[1]),
        )
    out_rows, shrink_low, second_grad, sums2, shrink = second_norm(
        pos, captions, active, shrink, down_bias, unit1, gain1, shift1, gain2, shift2, cot_rows, seq
    )
    if pieces:
        mine_s, theirs_s = stacked_grad(pos, active, shrink_low)
        theirs_s = from_core(theirs_s)
        shrink_low = after(shrink_low, mine_s)
    else:
        grad_shrink = weight_grad(active, shrink_low)
    expand_low, sums_hidden = hidden_back(shrink_low, shrink, slope)
    if pieces:
        keep_s, near_s, kept_s, send_s = shrink_sum(mine_s, after(theirs_s, expand_low))
        expand_low = after(expand_low, kept_s)
        near_s, send_s = from_chip(near_s, 1), from_x(send_s)
        mine_e, theirs_e = halves_grad(pos, normed_low, expand_low)
        theirs_e = from_core(theirs_e)
        expand_low = after(expand_low, mine_e)
    first_grad, branch_low, context_grad, sums1 = first_back(
        expand_low, expand, second_grad, unit1, scale1, gain1, output
    )
    if pieces:
        own_s, later_s = pair_sum(kept_s, after(send_s, branch_low))
        mine_o, theirs_o = halves_grad(pos, context_rows, after(branch_low, own_s))
        theirs_o = from_core(theirs_o)
        later_s = from_y(later_s)
        keep_s, far_s = pair_sum(keep_s, after(near_s, mine_o))
        own_x, later_x, out_x, own_y, later_y, out_y = core_split(
            [mine_e, mine_o], after([theirs_e, theirs_o], keep_s)
        )
        far_s = from_chip(far_s, 2)
        out_x, out_y = from_x(out_x), from_y(out_y)
        context_grad = after(context_grad, own_x)
    else:
        grad_expand = weight_grad(normed_low, expand_low)
        grad_output = weight_grad(context_rows, branch_low)
    joined_grad, sums_joined = attend_back(joined3, probs, context_grad.reshape(pairs, seq, width))
    joined_grad_rows = joined_grad.reshape(rows, 3 * width)
    if pieces:
        extra = bundle(sums_joined, sums1, sums2, sums_hidden)
        mine_p, theirs_p = halves_grad(pos, token_rows, joined_grad_rows, extra)
        theirs_p = from_core(theirs_p)
        out_x, out_y = after((out_x, out_y), mine_p)
        own_x, later_x, own_y, later_y = middle_sum([own_x, later_x, out_x, own_y, later_y, out_y])
        later_x, later_y = after((from_y(later_x), from_x(later_y)), far_s)
        keep_eo, near_eo = split_sum([own_x, later_x, own_y, later_y], flops=COVER)
        keep_eo, near_eo = ahead_sum(own_s, after(later_s, keep_eo), keep_eo, near_eo)
        own_x, later_x, out_x, own_y, later_y, out_y = core_split(
            [mine_p], [after(theirs_p, near_eo)], (keep_s, far_s)
        )
        near_eo = from_chip(near_eo, 1)
        out_x, out_y = from_x(out_x), from_y(out_y)
        joined_grad_rows = after(joined_grad_rows, own_x)
    else:
        grad_project = weight_grad(token_rows, joined_grad_rows)

        def owned(grad):
            part = lax.psum_scatter(grad, "fsdp", scatter_dimension=0, tiled=True)
            return lax.psum(part, "dp").astype(F32)

        own_project, own_output, own_expand, own_shrink = (
            owned(grad) for grad in (grad_project, grad_output, grad_expand, grad_shrink)
        )
        small = (sums_joined[0], sums1[0], sums1[1], sums1[2], sums_hidden[0], sums2[0], sums2[1], sums2[2])
        packed_grad = jnp.concatenate([v.reshape(parts, -1) for v in small], axis=1)
        shard = lax.psum(lax.psum_scatter(packed_grad.reshape(-1), "fsdp", scatter_dimension=0, tiled=True), "dp")
    token_grad = token_back(joined_grad_rows, project, first_grad)
    if pieces:
        half_p, half_e, half_o = project_weight.shape[1] // 2, expand_weight.shape[1] // 2, width // 2
        out_x, out_y = after((out_x, out_y), token_grad)
        own_x, later_x, own_y, later_y = middle_sum([own_x, later_x, out_x, own_y, later_y, out_y])
        later_x, later_y = from_y(later_x), from_x(later_y)
        keep_eo, far_eo = pair_sum(keep_eo, after(near_eo, own_x))
        far_eo = from_chip(far_eo, 2)
        later_x, later_y = after((later_x, later_y), keep_eo)
        keep_p, near_p, total_s = split_sum([own_x, later_x, own_y, later_y], more=FIRST // 4)
        near_p = from_chip(near_p, 1)
        total_seo = last_sum((total_s,), (keep_eo, after(far_eo, keep_p)))
        quarters_seo = from_plane(total_seo)
        keep_p, far_p = pair_sum(keep_p, after(near_p, total_seo))
        total_p = last_sum((keep_p, from_chip(far_p, 2)))
        quarters_p = from_plane(total_p)
        own_shrink, own_expand, own_output = place(
            pos,
            [total_seo, *after(quarters_seo, total_p)],
            (("stacked", 2 * width), ("halves", half_e), ("halves", half_o)),
        )
        own_project, *smalls = place(
            pos, [total_p, *after(quarters_p, own_expand)], (("halves", half_p), ("small", 128)), widths
        )
        smalls = [vector.reshape(-1) for vector in smalls]

    if not pieces:
        smalls, at = [], 0
        for size in widths:
            smalls.append(shard[at : at + size])
            at += size
    return (
        out_rows.reshape(pairs, seq, width),
        token_grad.reshape(pairs, seq, width),
        own_project,
        smalls[0],
        own_output,
        smalls[1],
        smalls[2],
        smalls[3],
        own_expand,
        smalls[4],
        own_shrink,
        smalls[5],
        smalls[6],
        smalls[7],
    )


def solution(mesh):
    rows3 = P(("dp", "fsdp"), None, None)
    matrix, vector = P("fsdp", None), P("fsdp")
    pieces = mesh.shape["dp"] == 4 and mesh.shape["fsdp"] == 8
    return jax.shard_map(
        functools.partial(local, pieces),
        mesh=mesh,
        in_specs=(
            rows3, P(("dp", "fsdp")), rows3,
            matrix, vector, matrix, vector, vector, vector,
            matrix, vector, matrix, vector, vector, vector,
        ),
        out_specs=(
            rows3, rows3,
            matrix, vector, matrix, vector, vector, vector,
            matrix, vector, matrix, vector, vector, vector,
        ),
        check_vma=False,
    )
```

profile of v0, /device:TPU:0, one launch (start us, length us, event | category | flops | bytes accessed | tf_op | source)
XLA Modules:
  0.0 211.7 jit_solution(11715119516549487308)
XLA Ops:
  2.1 3.7 %collective-permute-start.2 = (bf16[48,1152]{1,0:T(8,128)(2,1)S(1)}, bf16[48,1152]{1,0:T(8,128)(2,1)S(1)}, u32[]{:S(2)}, u32[]{:S(2)}) collective-permute-start(bf16[48,1152]{1,0:T(8,128)(2,1)S(1)} %dynamic_slice.11), channel_id=1, source_target_pairs={{0,4},{1,5},{2,6},{3,7},{4,0},{5,1},{6,2},{7,3},{8,12},{9,13},{10,... | collective-permute-start | bytes 331784 | tf_op jit(solution)/shard_map/ppermute | solution.py:917
  12.1 2.4 %collective-permute-done.2.refs_2_ = bf16[48,1152]{1,0:T(8,128)(2,1)S(1)} collective-permute-done((bf16[48,1152]{1,0:T(8,128)(2,1)S(1)}, bf16[48,1152]{1,0:T(8,128)(2,1)S(1)}, u32[]{:S(2)}, u32[]{:S(2)}) %collective-permute-start.2) | collective-permute-done | bytes 110624 | tf_op jit(solution)/shard_map/ppermute | solution.py:917
  16.4 2.6 %collective-permute-start.9 = (bf16[144,1152]{1,0:T(8,128)(2,1)S(1)}, bf16[144,1152]{1,0:T(8,128)(2,1)S(1)}, u32[]{:S(2)}, u32[]{:S(2)}) collective-permute-start(bf16[144,1152]{1,0:T(8,128)(2,1)S(1)} %below.5.rest_2_), channel_id=1, source_target_pairs={{0,24},{8,16},{16,8},{24,0},{1,25},{9,17},{17,9},{25,1},{2,26},{10... | collective-permute-start | bytes 995336 | tf_op jit(solution)/shard_map/ppermute | solution.py:900
  19.9 3.7 %collective-permute-start.5 = (bf16[48,2048]{1,0:T(8,128)(2,1)S(1)}, bf16[48,2048]{1,0:T(8,128)(2,1)S(1)}, u32[]{:S(2)}, u32[]{:S(2)}) collective-permute-start(bf16[48,2048]{1,0:T(8,128)(2,1)S(1)} %fusion.1), channel_id=1, source_target_pairs={{0,4},{1,5},{2,6},{3,7},{4,0},{5,1},{6,2},{7,3},{8,12},{9,13},{10,... | collective-permute-start | bytes 589832 | tf_op jit(solution)/shard_map/ppermute | solution.py:917
  24.0 8.2 %collective-permute-done.5.refs_2_ = bf16[48,2048]{1,0:T(8,128)(2,1)S(1)} collective-permute-done((bf16[48,2048]{1,0:T(8,128)(2,1)S(1)}, bf16[48,2048]{1,0:T(8,128)(2,1)S(1)}, u32[]{:S(2)}, u32[]{:S(2)}) %collective-permute-start.5) | collective-permute-done | bytes 196640 | tf_op jit(solution)/shard_map/ppermute | solution.py:917
  33.5 6.1 %collective-permute-done.6.refs_1_ = bf16[48,2048]{1,0:T(8,128)(2,1)S(1)} collective-permute-done((bf16[48,2048]{1,0:T(8,128)(2,1)S(1)}, bf16[48,2048]{1,0:T(8,128)(2,1)S(1)}, u32[]{:S(2)}, u32[]{:S(2)}) %collective-permute-start.6) | collective-permute-done | bytes 196640 | tf_op jit(solution)/shard_map/ppermute | solution.py:917
  41.4 2.4 %collective-permute-start.18 = (bf16[144,1920]{1,0:T(8,128)(2,1)S(1)}, bf16[144,1920]{1,0:T(8,128)(2,1)S(1)}, u32[]{:S(2)}, u32[]{:S(2)}) collective-permute-start(bf16[144,1920]{1,0:T(8,128)(2,1)S(1)} %below.7.rest_2_), channel_id=1, source_target_pairs={{0,24},{8,16},{16,8},{24,0},{1,25},{9,17},{17,9},{25,1},{2,26},{10... | collective-permute-start | bytes 1658888 | tf_op jit(solution)/shard_map/ppermute | solution.py:900
  45.7 5.5 %join.1 = (bf16[832,2304]{1,0:T(8,128)(2,1)}, bf16[768,2304]{1,0:T(8,128)(2,1)}) custom-call(s32[4]{0:T(128)S(1)} %pad_add_fusion.pos, bf16[832,768]{1,0:T(8,128)(2,1)S(1)} %bitcast.27, f32[1,2304]{1,0:T(1,128)S(1)} %get-tuple-element.163.bias, bf16[96,2304]{1,0:T(8,128)(2,1)S(1)} %copy-done.6, bf16[96,2304]{1,0:T(8,128)(2,1)S(1)} %copy-done.8, ...), custom_call_target="tpu_custom_call" | custom-call | tf_op jit(solution)/shard_map/join/pallas_call | solution.py:232
  53.0 8.7 %attend.1 = (bf16[8,104,768]{2,1,0:T(8,128)(2,1)S(1)}, bf16[8,6,104,256]{3,2,1,0:T(8,128)(2,1)}) custom-call(s32[8]{0:T(128)S(1)} %copy-done.10, bf16[8,104,2304]{2,1,0:T(8,128)(2,1)} %bitcast.34), custom_call_target="tpu_custom_call" | custom-call | tf_op jit(solution)/shard_map/attend/pallas_call | solution.py:288
  62.0 6.4 %collective-permute-done.17.refs_1_ = bf16[144,1920]{1,0:T(8,128)(2,1)S(1)} collective-permute-done((bf16[144,1920]{1,0:T(8,128)(2,1)S(1)}, bf16[144,1920]{1,0:T(8,128)(2,1)S(1)}, u32[]{:S(2)}, u32[]{:S(2)}) %collective-permute-start.17) | collective-permute-done | bytes 552992 | tf_op jit(solution)/shard_map/ppermute | solution.py:900
  74.2 2.4 %first_norm.1 = (f32[832,768]{1,0:T(8,128)S(1)}, f32[832,1]{1,0:T(8,128)S(1)}, bf16[832,768]{1,0:T(8,128)(2,1)S(1)}, bf16[768,768]{1,0:T(8,128)(2,1)S(1)}) custom-call(s32[4]{0:T(128)S(1)} %pad_add_fusion.pos, bf16[832,768]{1,0:T(8,128)(2,1)S(1)} %bitcast.30, f32[1,768]{1,0:T(1,128)S(1)} %get-tuple-element.303.bias, bf16[832,768]{1,0:T(8,128)(2,1)S(1)} %bitcast.28, ...), custom_call_target="tpu_custom_call" | custom-call | tf_op jit(solution)/shard_map/first_norm/pallas_call | solution.py:424
  76.6 8.5 %expand_act.1 = (bf16[832,3072]{1,0:T(8,128)(2,1)S(1)}, bf16[832,3072]{1,0:T(8,128)(2,1)S(1)}, bf16[768,3072]{1,0:T(8,128)(2,1)S(1)}) custom-call(s32[4]{0:T(128)S(1)} %pad_add_fusion.pos, bf16[832,768]{1,0:T(8,128)(2,1)S(1)} %get-tuple-element.180.normed_low.left, f32[1,3072]{1,0:T(1,128)S(1)} %get-tuple-element.181.bias, bf16[96,3072]{1,0:T(8,128)(2,1)S(1)} %copy-done.5, ...), custom_call_target="tpu_custom_call" | custom-call | tf_op jit(solution)/shard_map/expand_act/pallas_call | solution.py:453
  85.9 2.8 %collective-permute-done.23.rest_1_ = bf16[384,768]{1,0:T(8,128)(2,1)S(1)} collective-permute-done((bf16[384,768]{1,0:T(8,128)(2,1)S(1)}, bf16[384,768]{1,0:T(8,128)(2,1)S(1)}, u32[]{:S(2)}, u32[]{:S(2)}) %collective-permute-start.23) | collective-permute-done | bytes 589856 | tf_op jit(solution)/shard_map/ppermute | solution.py:894
  88.6 8.4 %second_norm.1 = (bf16[832,768]{1,0:T(8,128)(2,1)}, bf16[832,768]{1,0:T(8,128)(2,1)S(1)}, f32[832,768]{1,0:T(8,128)S(1)}, f32[8,768]{1,0:T(8,128)S(1)}, bf16[3072,768]{1,0:T(8,128)(2,1)S(1)}) custom-call(s32[4]{0:T(128)S(1)} %pad_add_fusion.pos, s32[8]{0:T(128)S(1)} %copy-done.10, bf16[832,3072]{1,0:T(8,128)(2,1)S(1)} %get-tuple-element.183.active.left, ...), custom_call_target="tpu_custom_call" | custom-call | tf_op jit(solution)/shard_map/second_norm/pallas_call | solution.py:505
  97.1 6.7 %stacked_grad.1 = (bf16[4,2,2,48,1536]{4,3,2,1,0:T(8,128)(2,1)S(1)}, bf16[4,2,2,48,1536]{4,3,2,1,0:T(8,128)(2,1)S(1)}) custom-call(s32[4]{0:T(128)S(1)} %pad_add_fusion.pos, bf16[832,3072]{1,0:T(8,128)(2,1)S(1)} %get-tuple-element.183.active.left, bf16[832,768]{1,0:T(8,128)(2,1)S(1)} %get-tuple-element.194.right.low), custom_call_target="tpu_custom_call" | custom-call | tf_op jit(solution)/shard_map/stacked_grad/pallas_call | solution.py:686
  104.0 4.9 %hidden_back.1 = (bf16[832,3072]{1,0:T(8,128)(2,1)S(1)}, f32[1,3072]{1,0:T(1,128)S(1)}) custom-call(bf16[832,768]{1,0:T(8,128)(2,1)S(1)} %get-tuple-element.194.right.low, bf16[3072,768]{1,0:T(8,128)(2,1)S(1)} %get-tuple-element.195.weight, bf16[832,3072]{1,0:T(8,128)(2,1)S(1)} %get-tuple-element.196.slope), custom_call_target="tpu_custom_call" | custom-call | tf_op jit(solution)/shard_map/hidden_back/pallas_call | solution.py:538
  111.9 6.3 %halves_grad.3 = (bf16[4,2,2,48,1536]{4,3,2,1,0:T(8,128)(2,1)S(1)}, bf16[4,2,2,48,1536]{4,3,2,1,0:T(8,128)(2,1)S(1)}) custom-call(s32[4]{0:T(128)S(1)} %pad_add_fusion.pos, bf16[832,768]{1,0:T(8,128)(2,1)S(1)} %get-tuple-element.180.normed_low.left, bf16[832,3072]{1,0:T(8,128)(2,1)S(1)} %get-tuple-element.203.right.hidden), custom_call_target="tpu_custom_call" | custom-call | tf_op jit(solution)/shard_map/halves_grad/pallas_call | solution.py:686
  118.3 6.0 %first_back.1 = (f32[832,768]{1,0:T(8,128)S(1)}, bf16[832,768]{1,0:T(8,128)(2,1)S(1)}, bf16[832,768]{1,0:T(8,128)(2,1)S(1)}, f32[8,768]{1,0:T(8,128)S(1)}) custom-call(bf16[832,3072]{1,0:T(8,128)(2,1)S(1)} %get-tuple-element.203.right.hidden, bf16[768,3072]{1,0:T(8,128)(2,1)S(1)} %get-tuple-element.204.weight, f32[832,768]{1,0:T(8,128)S(1)} %get-tuple-element.205.second, ...), custom_call_target="tpu_custom_call" | custom-call | flops 99999997952 | tf_op jit(solution)/shard_map/first_back/pallas_call | solution.py:578
  124.4 2.9 %halves_grad.4 = (bf16[4,2,2,48,384]{4,3,2,1,0:T(8,128)(2,1)S(1)}, bf16[4,2,2,48,384]{4,3,2,1,0:T(8,128)(2,1)S(1)}) custom-call(s32[4]{0:T(128)S(1)} %pad_add_fusion.pos, bf16[832,768]{1,0:T(8,128)(2,1)S(1)} %bitcast.31, bf16[832,768]{1,0:T(8,128)(2,1)S(1)} %get-tuple-element.213.right), custom_call_target="tpu_custom_call" | custom-call | tf_op jit(solution)/shard_map/halves_grad/pallas_call | solution.py:686
  127.9 1.8 collective-permute-done.32.received
  132.7 2.4 %collective-permute-start.39 = (bf16[4,48,1024]{2,1,0:T(8,128)(2,1)S(1)}, bf16[4,48,1024]{2,1,0:T(8,128)(2,1)S(1)}, u32[]{:S(2)}, u32[]{:S(2)}) collective-permute-start(bf16[4,48,1024]{2,1,0:T(8,128)(2,1)S(1)} %get-tuple-element.243), channel_id=1, source_target_pairs={{0,4},{1,5},{2,6},{3,7},{4,0},{5,1},{6,2},{7,3},{8,12},{9,13},{10,... | collective-permute-start | bytes 1179656 | tf_op jit(solution)/shard_map/ppermute | solution.py:917
  135.0 8.4 %attend_back.1 = (bf16[8,104,2304]{2,1,0:T(8,128)(2,1)S(1)}, f32[1,1536]{1,0:T(1,128)S(1)}) custom-call(bf16[8,104,2304]{2,1,0:T(8,128)(2,1)} %bitcast.35, bf16[8,6,104,256]{3,2,1,0:T(8,128)(2,1)} %get-tuple-element.191.probs, bf16[8,104,768]{2,1,0:T(8,128)(2,1)S(1)} %bitcast.33), custom_call_target="tpu_custom_call" | custom-call | tf_op jit(solution)/shard_map/attend_back/pallas_call | solution.py:350
  143.5 5.4 %halves_grad.5 = (bf16[4,2,2,48,1280]{4,3,2,1,0:T(8,128)(2,1)S(1)}, bf16[4,2,2,48,1280]{4,3,2,1,0:T(8,128)(2,1)S(1)}) custom-call(s32[4]{0:T(128)S(1)} %pad_add_fusion.pos, bf16[832,768]{1,0:T(8,128)(2,1)S(1)} %bitcast.29, bf16[832,2304]{1,0:T(8,128)(2,1)S(1)} %bitcast.25, f32[8,16,128]{2,1,0:T(8,128)S(1)} %bundle.1.rest_0_), custom_call_target="tpu_custom_call" | custom-call | tf_op jit(solution)/shard_map/halves_grad/pallas_call | solution.py:686
  153.2 7.9 %collective-permute-done.37.received = bf16[2,48,1920]{2,1,0:T(8,128)(2,1)S(1)} collective-permute-done((bf16[2,48,1920]{2,1,0:T(8,128)(2,1)S(1)}, bf16[2,48,1920]{2,1,0:T(8,128)(2,1)S(1)}, u32[]{:S(2)}, u32[]{:S(2)}) %collective-permute-start.37) | collective-permute-done | bytes 368672 | tf_op jit(solution)/shard_map/ppermute | solution.py:909
  161.3 1.9 collective-permute-done.34.two
  166.4 4.5 %token_back.1 = f32[832,768]{1,0:T(8,128)} custom-call(bf16[832,2304]{1,0:T(8,128)(2,1)S(1)} %bitcast.26, bf16[768,2304]{1,0:T(8,128)(2,1)S(1)} %copy-done.1, f32[832,768]{1,0:T(8,128)S(1)} %get-tuple-element.255.first), custom_call_target="tpu_custom_call" | custom-call | tf_op jit(solution)/shard_map/token_back/pallas_call | solution.py:603
  170.9 6.0 %collective-permute-done.40.refs_2_ = bf16[2,2,48,1536]{3,2,1,0:T(8,128)(2,1)S(1)} collective-permute-done((bf16[2,2,48,1536]{3,2,1,0:T(8,128)(2,1)S(1)}, bf16[2,2,48,1536]{3,2,1,0:T(8,128)(2,1)S(1)}, u32[]{:S(2)}, u32[]{:S(2)}) %collective-permute-start.40) | collective-permute-done | bytes 589856 | tf_op jit(solution)/shard_map/ppermute | solution.py:905
  181.2 4.4 %collective-permute-done.42.received = bf16[2,48,1536]{2,1,0:T(8,128)(2,1)S(1)} collective-permute-done((bf16[2,48,1536]{2,1,0:T(8,128)(2,1)S(1)}, bf16[2,48,1536]{2,1,0:T(8,128)(2,1)S(1)}, u32[]{:S(2)}, u32[]{:S(2)}) %collective-permute-start.42) | collective-permute-done | bytes 294944 | tf_op jit(solution)/shard_map/ppermute | solution.py:909
  186.8 3.8 %collective-permute-done.46.refs_2_ = bf16[48,2432]{1,0:T(8,128)(2,1)S(1)} collective-permute-done((bf16[48,2432]{1,0:T(8,128)(2,1)S(1)}, bf16[48,2432]{1,0:T(8,128)(2,1)S(1)}, u32[]{:S(2)}, u32[]{:S(2)}) %collective-permute-start.46) | collective-permute-done | bytes 233504 | tf_op jit(solution)/shard_map/ppermute | solution.py:917
  194.4 6.4 %collective-permute-done.47.refs_1_ = bf16[48,1280]{1,0:T(8,128)(2,1)S(1)} collective-permute-done((bf16[48,1280]{1,0:T(8,128)(2,1)S(1)}, bf16[48,1280]{1,0:T(8,128)(2,1)S(1)}, u32[]{:S(2)}, u32[]{:S(2)}) %collective-permute-start.47) | collective-permute-done | bytes 122912 | tf_op jit(solution)/shard_map/ppermute | solution.py:917
  204.4 2.5 %collective-permute-done.52.refs_2_ = bf16[48,3456]{1,0:T(8,128)(2,1)S(1)} collective-permute-done((bf16[48,3456]{1,0:T(8,128)(2,1)S(1)}, bf16[48,3456]{1,0:T(8,128)(2,1)S(1)}, u32[]{:S(2)}, u32[]{:S(2)}) %collective-permute-start.52) | collective-permute-done | bytes 331808 | tf_op jit(solution)/shard_map/ppermute | solution.py:900
  206.9 2.2 %place.2 = (f32[384,768]{1,0:T(8,128)}, f32[96,3072]{1,0:T(8,128)}, f32[96,768]{1,0:T(8,128)}) custom-call(s32[4]{0:T(128)S(1)} %pad_add_fusion.pos, bf16[48,3456]{1,0:T(8,128)(2,1)S(1)} %last_sum.2.refs_0_, bf16[48,3456]{1,0:T(8,128)(2,1)S(1)} %collective-permute-done.51.refs_1_, bf16[48,3456]{1,0:T(8,128)(2,1)S(1)} %collective-permute-done.52.refs_2_, ...), custom_call_target="tpu_custom_call" | custom-call | tf_op jit(solution)/shard_map/place/pallas_call | solution.py:878
  (152 shorter events, 54.3 us)
Async XLA Ops:
  0.6 14.9 %collective-permute-start.3 = (bf16[96,2304]{1,0:T(8,128)(2,1)}, bf16[96,2304]{1,0:T(8,128)(2,1)S(1)}, u32[]{:S(2)}, u32[]{:S(2)}) collective-permute-start(bf16[96,2304]{1,0:T(8,128)(2,1)} %rest_0_.4), channel_id=1, source_target_pairs={{0,1},{1,0},{2,3},{3,2},{4,5},{5,4},{6,7},{7,6},{8,9},{9,8},{10,11... | collective-permute-start | bytes 1327112 | tf_op jit(solution)/shard_map/ppermute | solution.py:894
  2.1 12.4 %collective-permute-start.2 = (bf16[48,1152]{1,0:T(8,128)(2,1)S(1)}, bf16[48,1152]{1,0:T(8,128)(2,1)S(1)}, u32[]{:S(2)}, u32[]{:S(2)}) collective-permute-start(bf16[48,1152]{1,0:T(8,128)(2,1)S(1)} %dynamic_slice.11), channel_id=1, source_target_pairs={{0,4},{1,5},{2,6},{3,7},{4,0},{5,1},{6,2},{7,3},{8,12},{9,13},{10,... | collective-permute-start | bytes 331784 | tf_op jit(solution)/shard_map/ppermute | solution.py:917
  16.4 15.8 %collective-permute-start.9 = (bf16[144,1152]{1,0:T(8,128)(2,1)S(1)}, bf16[144,1152]{1,0:T(8,128)(2,1)S(1)}, u32[]{:S(2)}, u32[]{:S(2)}) collective-permute-start(bf16[144,1152]{1,0:T(8,128)(2,1)S(1)} %below.5.rest_2_), channel_id=1, source_target_pairs={{0,24},{8,16},{16,8},{24,0},{1,25},{9,17},{17,9},{25,1},{2,26},{10... | collective-permute-start | bytes 995336 | tf_op jit(solution)/shard_map/ppermute | solution.py:900
  18.9 14.4 %collective-permute-start.8 = (bf16[144,1152]{1,0:T(8,128)(2,1)S(1)}, bf16[144,1152]{1,0:T(8,128)(2,1)S(1)}, u32[]{:S(2)}, u32[]{:S(2)}) collective-permute-start(bf16[144,1152]{1,0:T(8,128)(2,1)S(1)} %below.5.rest_2_), channel_id=1, source_target_pairs={{0,16},{8,24},{16,0},{24,8},{1,17},{9,25},{17,1},{25,9},{2,18},{10... | collective-permute-start | bytes 995336 | tf_op jit(solution)/shard_map/ppermute | solution.py:900
  19.4 14.0 %collective-permute-start.7 = (bf16[144,1152]{1,0:T(8,128)(2,1)S(1)}, bf16[144,1152]{1,0:T(8,128)(2,1)S(1)}, u32[]{:S(2)}, u32[]{:S(2)}) collective-permute-start(bf16[144,1152]{1,0:T(8,128)(2,1)S(1)} %below.5.rest_2_), channel_id=1, source_target_pairs={{0,8},{8,0},{16,24},{24,16},{1,9},{9,1},{17,25},{25,17},{2,10},{10... | collective-permute-start | bytes 995336 | tf_op jit(solution)/shard_map/ppermute | solution.py:900
  19.9 12.3 %collective-permute-start.5 = (bf16[48,2048]{1,0:T(8,128)(2,1)S(1)}, bf16[48,2048]{1,0:T(8,128)(2,1)S(1)}, u32[]{:S(2)}, u32[]{:S(2)}) collective-permute-start(bf16[48,2048]{1,0:T(8,128)(2,1)S(1)} %fusion.1), channel_id=1, source_target_pairs={{0,4},{1,5},{2,6},{3,7},{4,0},{5,1},{6,2},{7,3},{8,12},{9,13},{10,... | collective-permute-start | bytes 589832 | tf_op jit(solution)/shard_map/ppermute | solution.py:917
  32.2 11.7 %collective-permute-start.11 = (bf16[144,1152]{1,0:T(8,128)(2,1)S(1)}, bf16[144,1152]{1,0:T(8,128)(2,1)S(1)}, u32[]{:S(2)}, u32[]{:S(2)}) collective-permute-start(bf16[144,1152]{1,0:T(8,128)(2,1)S(1)} %below.5.rest_2_), channel_id=1, source_target_pairs={{0,1},{1,0},{2,3},{3,2},{4,5},{5,4},{6,7},{7,6},{8,9},{9,8},{10,11... | collective-permute-start | bytes 995336 | tf_op jit(solution)/shard_map/ppermute | solution.py:894
  41.0 20.8 %collective-permute-start.14 = (bf16[96,1536]{1,0:T(8,128)(2,1)S(1)}, bf16[96,1536]{1,0:T(8,128)(2,1)S(1)}, u32[]{:S(2)}, u32[]{:S(2)}) collective-permute-start(bf16[96,1536]{1,0:T(8,128)(2,1)S(1)} %pick.1), channel_id=1, source_target_pairs={{0,4},{1,5},{2,6},{3,7},{4,0},{5,1},{6,2},{7,3},{8,12},{9,13},{10,... | collective-permute-start | bytes 884744 | tf_op jit(solution)/shard_map/ppermute | solution.py:917
  41.4 20.6 %collective-permute-start.18 = (bf16[144,1920]{1,0:T(8,128)(2,1)S(1)}, bf16[144,1920]{1,0:T(8,128)(2,1)S(1)}, u32[]{:S(2)}, u32[]{:S(2)}) collective-permute-start(bf16[144,1920]{1,0:T(8,128)(2,1)S(1)} %below.7.rest_2_), channel_id=1, source_target_pairs={{0,24},{8,16},{16,8},{24,0},{1,25},{9,17},{17,9},{25,1},{2,26},{10... | collective-permute-start | bytes 1658888 | tf_op jit(solution)/shard_map/ppermute | solution.py:900
  43.9 24.5 %collective-permute-start.17 = (bf16[144,1920]{1,0:T(8,128)(2,1)S(1)}, bf16[144,1920]{1,0:T(8,128)(2,1)S(1)}, u32[]{:S(2)}, u32[]{:S(2)}) collective-permute-start(bf16[144,1920]{1,0:T(8,128)(2,1)S(1)} %below.7.rest_2_), channel_id=1, source_target_pairs={{0,16},{8,24},{16,0},{24,8},{1,17},{9,25},{17,1},{25,9},{2,18},{10... | collective-permute-start | bytes 1658888 | tf_op jit(solution)/shard_map/ppermute | solution.py:900
  44.4 24.1 %collective-permute-start.16 = (bf16[144,1920]{1,0:T(8,128)(2,1)S(1)}, bf16[144,1920]{1,0:T(8,128)(2,1)S(1)}, u32[]{:S(2)}, u32[]{:S(2)}) collective-permute-start(bf16[144,1920]{1,0:T(8,128)(2,1)S(1)} %below.7.rest_2_), channel_id=1, source_target_pairs={{0,8},{8,0},{16,24},{24,16},{1,9},{9,1},{17,25},{25,17},{2,10},{10... | collective-permute-start | bytes 1658888 | tf_op jit(solution)/shard_map/ppermute | solution.py:900
  51.2 18.0 %collective-permute-start.13 = (bf16[96,1536]{1,0:T(8,128)(2,1)S(1)}, bf16[96,1536]{1,0:T(8,128)(2,1)S(1)}, u32[]{:S(2)}, u32[]{:S(2)}) collective-permute-start(bf16[96,1536]{1,0:T(8,128)(2,1)S(1)} %pick.1), channel_id=1, source_target_pairs={{0,2},{1,3},{2,0},{3,1},{4,6},{5,7},{6,4},{7,5},{8,10},{9,11},{10,... | collective-permute-start | bytes 884744 | tf_op jit(solution)/shard_map/ppermute | solution.py:917
  62.0 10.7 %collective-permute-start.20 = (bf16[144,1920]{1,0:T(8,128)(2,1)S(1)}, bf16[144,1920]{1,0:T(8,128)(2,1)S(1)}, u32[]{:S(2)}, u32[]{:S(2)}) collective-permute-start(bf16[144,1920]{1,0:T(8,128)(2,1)S(1)} %below.7.rest_2_), channel_id=1, source_target_pairs={{0,1},{1,0},{2,3},{3,2},{4,5},{5,4},{6,7},{7,6},{8,9},{9,8},{10,11... | collective-permute-start | bytes 1658888 | tf_op jit(solution)/shard_map/ppermute | solution.py:894
  69.7 15.5 %collective-permute-start.24 = (bf16[288,768]{1,0:T(8,128)(2,1)S(1)}, bf16[288,768]{1,0:T(8,128)(2,1)S(1)}, u32[]{:S(2)}, u32[]{:S(2)}) collective-permute-start(bf16[288,768]{1,0:T(8,128)(2,1)S(1)} %get-tuple-element.186), channel_id=1, source_target_pairs={{0,8},{8,0},{16,24},{24,16},{1,9},{9,1},{17,25},{25,17},{2,10},{10... | collective-permute-start | bytes 1327112 | tf_op jit(solution)/shard_map/ppermute | solution.py:905
  71.3 13.9 %collective-permute-start.25 = (bf16[288,768]{1,0:T(8,128)(2,1)S(1)}, bf16[288,768]{1,0:T(8,128)(2,1)S(1)}, u32[]{:S(2)}, u32[]{:S(2)}) collective-permute-start(bf16[288,768]{1,0:T(8,128)(2,1)S(1)} %get-tuple-element.187), channel_id=1, source_target_pairs={{0,16},{8,24},{16,0},{24,8},{1,17},{9,25},{17,1},{25,9},{2,18},{10... | collective-permute-start | bytes 1327112 | tf_op jit(solution)/shard_map/ppermute | solution.py:909
  72.8 13.0 %collective-permute-start.26 = (bf16[288,1536]{1,0:T(8,128)(2,1)S(1)}, bf16[288,1536]{1,0:T(8,128)(2,1)S(1)}, u32[]{:S(2)}, u32[]{:S(2)}) collective-permute-start(bf16[288,1536]{1,0:T(8,128)(2,1)S(1)} %below.9.whole_ref.rest_2_), channel_id=1, source_target_pairs={{0,1},{1,0},{2,3},{3,2},{4,5},{5,4},{6,7},{7,6},{8,9},{9,8},{10,11... | collective-permute-start | bytes 2654216 | tf_op jit(solution)/shard_map/ppermute | solution.py:894
  109.6 14.7 %collective-permute-start.29 = (bf16[2,4,48,512]{3,2,1,0:T(8,128)(2,1)S(1)}, bf16[2,4,48,512]{3,2,1,0:T(8,128)(2,1)S(1)}, u32[]{:S(2)}, u32[]{:S(2)}) collective-permute-start(bf16[2,4,48,512]{3,2,1,0:T(8,128)(2,1)S(1)} %get-tuple-element.210), channel_id=1, source_target_pairs={{0,8},{8,0},{16,24},{24,16},{1,9},{9,1},{17,25},{25,17},{2,10},{10... | collective-permute-start | bytes 1179656 | tf_op jit(solution)/shard_map/ppermute | solution.py:905
  110.2 19.5 %collective-permute-start.32 = (bf16[2,4,48,1024]{3,2,1,0:T(8,128)(2,1)S(1)}, bf16[2,4,48,1024]{3,2,1,0:T(8,128)(2,1)S(1)}, u32[]{:S(2)}, u32[]{:S(2)}) collective-permute-start(bf16[2,4,48,1024]{3,2,1,0:T(8,128)(2,1)S(1)} %get-tuple-element.218), channel_id=1, source_target_pairs={{0,2},{1,3},{2,0},{3,1},{4,6},{5,7},{6,4},{7,5},{8,10},{9,11},{10,... | collective-permute-start | bytes 2359304 | tf_op jit(solution)/shard_map/ppermute | solution.py:917
  118.2 11.7 %collective-permute-start.30 = (bf16[4,2,2,48,1536]{4,3,2,1,0:T(8,128)(2,1)S(1)}, bf16[4,2,2,48,1536]{4,3,2,1,0:T(8,128)(2,1)S(1)}, u32[]{:S(2)}, u32[]{:S(2)}) collective-permute-start(bf16[4,2,2,48,1536]{4,3,2,1,0:T(8,128)(2,1)S(1)} %get-tuple-element.215), channel_id=1, source_target_pairs={{0,1},{1,0},{2,3},{3,2},{4,5},{5,4},{6,7},{7,6},{8,9},{9,8},{10,11... | collective-permute-start | bytes 7077896 | tf_op jit(solution)/shard_map/ppermute | solution.py:894
  130.6 18.4 %collective-permute-start.35 = (bf16[2,2,48,1920]{3,2,1,0:T(8,128)(2,1)S(1)}, bf16[2,2,48,1920]{3,2,1,0:T(8,128)(2,1)S(1)}, u32[]{:S(2)}, u32[]{:S(2)}) collective-permute-start(bf16[2,2,48,1920]{3,2,1,0:T(8,128)(2,1)S(1)} %get-tuple-element.234), channel_id=1, source_target_pairs={{0,8},{8,0},{16,24},{24,16},{1,9},{9,1},{17,25},{25,17},{2,10},{10... | collective-permute-start | bytes 2211848 | tf_op jit(solution)/shard_map/ppermute | solution.py:905
  132.1 17.3 %collective-permute-start.36 = (bf16[2,2,48,1920]{3,2,1,0:T(8,128)(2,1)S(1)}, bf16[2,2,48,1920]{3,2,1,0:T(8,128)(2,1)S(1)}, u32[]{:S(2)}, u32[]{:S(2)}) collective-permute-start(bf16[2,2,48,1920]{3,2,1,0:T(8,128)(2,1)S(1)} %get-tuple-element.235), channel_id=1, source_target_pairs={{0,16},{8,24},{16,0},{24,8},{1,17},{9,25},{17,1},{25,9},{2,18},{10... | collective-permute-start | bytes 2211848 | tf_op jit(solution)/shard_map/ppermute | solution.py:909
  132.7 20.5 %collective-permute-start.39 = (bf16[4,48,1024]{2,1,0:T(8,128)(2,1)S(1)}, bf16[4,48,1024]{2,1,0:T(8,128)(2,1)S(1)}, u32[]{:S(2)}, u32[]{:S(2)}) collective-permute-start(bf16[4,48,1024]{2,1,0:T(8,128)(2,1)S(1)} %get-tuple-element.243), channel_id=1, source_target_pairs={{0,4},{1,5},{2,6},{3,7},{4,0},{5,1},{6,2},{7,3},{8,12},{9,13},{10,... | collective-permute-start | bytes 1179656 | tf_op jit(solution)/shard_map/ppermute | solution.py:917
  149.8 11.3 %collective-permute-start.37 = (bf16[2,48,1920]{2,1,0:T(8,128)(2,1)S(1)}, bf16[2,48,1920]{2,1,0:T(8,128)(2,1)S(1)}, u32[]{:S(2)}, u32[]{:S(2)}) collective-permute-start(bf16[2,48,1920]{2,1,0:T(8,128)(2,1)S(1)} %get-tuple-element.241), channel_id=1, source_target_pairs={{0,16},{8,24},{16,0},{24,8},{1,17},{9,25},{17,1},{25,9},{2,18},{10... | collective-permute-start | bytes 1105928 | tf_op jit(solution)/shard_map/ppermute | solution.py:909
  151.2 9.9 %collective-permute-start.38 = (bf16[2,48,1920]{2,1,0:T(8,128)(2,1)S(1)}, bf16[2,48,1920]{2,1,0:T(8,128)(2,1)S(1)}, u32[]{:S(2)}, u32[]{:S(2)}) collective-permute-start(bf16[2,48,1920]{2,1,0:T(8,128)(2,1)S(1)} %get-tuple-element.242), channel_id=1, source_target_pairs={{0,8},{8,0},{16,24},{24,16},{1,9},{9,1},{17,25},{25,17},{2,10},{10... | collective-permute-start | bytes 1105928 | tf_op jit(solution)/shard_map/ppermute | solution.py:905
  152.0 11.2 %collective-permute-start.34 = (bf16[4,48,512]{2,1,0:T(8,128)(2,1)S(1)}, bf16[4,48,512]{2,1,0:T(8,128)(2,1)S(1)}, u32[]{:S(2)}, u32[]{:S(2)}) collective-permute-start(bf16[4,48,512]{2,1,0:T(8,128)(2,1)S(1)} %get-tuple-element.232), channel_id=1, source_target_pairs={{0,16},{8,24},{16,0},{24,8},{1,17},{9,25},{17,1},{25,9},{2,18},{10... | collective-permute-start | bytes 589832 | tf_op jit(solution)/shard_map/ppermute | solution.py:909
  153.2 10.1 %collective-permute-start.33 = (bf16[4,2,2,48,1280]{4,3,2,1,0:T(8,128)(2,1)S(1)}, bf16[4,2,2,48,1280]{4,3,2,1,0:T(8,128)(2,1)S(1)}, u32[]{:S(2)}, u32[]{:S(2)}) collective-permute-start(bf16[4,2,2,48,1280]{4,3,2,1,0:T(8,128)(2,1)S(1)} %get-tuple-element.231), channel_id=1, source_target_pairs={{0,1},{1,0},{2,3},{3,2},{4,5},{5,4},{6,7},{7,6},{8,9},{9,8},{10,11... | collective-permute-start | bytes 5898248 | tf_op jit(solution)/shard_map/ppermute | solution.py:894
  163.9 13.0 %collective-permute-start.40 = (bf16[2,2,48,1536]{3,2,1,0:T(8,128)(2,1)S(1)}, bf16[2,2,48,1536]{3,2,1,0:T(8,128)(2,1)S(1)}, u32[]{:S(2)}, u32[]{:S(2)}) collective-permute-start(bf16[2,2,48,1536]{3,2,1,0:T(8,128)(2,1)S(1)} %get-tuple-element.257), channel_id=1, source_target_pairs={{0,8},{8,0},{16,24},{24,16},{1,9},{9,1},{17,25},{25,17},{2,10},{10... | collective-permute-start | bytes 1769480 | tf_op jit(solution)/shard_map/ppermute | solution.py:905
  165.4 13.2 %collective-permute-start.41 = (bf16[2,2,48,1536]{3,2,1,0:T(8,128)(2,1)S(1)}, bf16[2,2,48,1536]{3,2,1,0:T(8,128)(2,1)S(1)}, u32[]{:S(2)}, u32[]{:S(2)}) collective-permute-start(bf16[2,2,48,1536]{3,2,1,0:T(8,128)(2,1)S(1)} %get-tuple-element.258), channel_id=1, source_target_pairs={{0,16},{8,24},{16,0},{24,8},{1,17},{9,25},{17,1},{25,9},{2,18},{10... | collective-permute-start | bytes 1769480 | tf_op jit(solution)/shard_map/ppermute | solution.py:909
  166.4 14.6 %collective-permute-start.44 = (bf16[2,48,2432]{2,1,0:T(8,128)(2,1)S(1)}, bf16[2,48,2432]{2,1,0:T(8,128)(2,1)S(1)}, u32[]{:S(2)}, u32[]{:S(2)}) collective-permute-start(bf16[2,48,2432]{2,1,0:T(8,128)(2,1)S(1)} %get-tuple-element.250), channel_id=1, source_target_pairs={{0,2},{1,3},{2,0},{3,1},{4,6},{5,7},{6,4},{7,5},{8,10},{9,11},{10,... | collective-permute-start | bytes 1400840 | tf_op jit(solution)/shard_map/ppermute | solution.py:917
  190.7 12.0 %collective-permute-start.53 = (bf16[48,3456]{1,0:T(8,128)(2,1)S(1)}, bf16[48,3456]{1,0:T(8,128)(2,1)S(1)}, u32[]{:S(2)}, u32[]{:S(2)}) collective-permute-start(bf16[48,3456]{1,0:T(8,128)(2,1)S(1)} %last_sum.2.refs_0_), channel_id=1, source_target_pairs={{0,24},{8,16},{16,8},{24,0},{1,25},{9,17},{17,9},{25,1},{2,26},{10... | collective-permute-start | bytes 995336 | tf_op jit(solution)/shard_map/ppermute | solution.py:900
  192.0 14.9 %collective-permute-start.52 = (bf16[48,3456]{1,0:T(8,128)(2,1)S(1)}, bf16[48,3456]{1,0:T(8,128)(2,1)S(1)}, u32[]{:S(2)}, u32[]{:S(2)}) collective-permute-start(bf16[48,3456]{1,0:T(8,128)(2,1)S(1)} %last_sum.2.refs_0_), channel_id=1, source_target_pairs={{0,16},{8,24},{16,0},{24,8},{1,17},{9,25},{17,1},{25,9},{2,18},{10... | collective-permute-start | bytes 995336 | tf_op jit(solution)/shard_map/ppermute | solution.py:900
  193.0 13.8 %collective-permute-start.51 = (bf16[48,3456]{1,0:T(8,128)(2,1)S(1)}, bf16[48,3456]{1,0:T(8,128)(2,1)S(1)}, u32[]{:S(2)}, u32[]{:S(2)}) collective-permute-start(bf16[48,3456]{1,0:T(8,128)(2,1)S(1)} %last_sum.2.refs_0_), channel_id=1, source_target_pairs={{0,8},{8,0},{16,24},{24,16},{1,9},{9,1},{17,25},{25,17},{2,10},{10... | collective-permute-start | bytes 995336 | tf_op jit(solution)/shard_map/ppermute | solution.py:900
  (33 other events, 207.5 us)
where the time goes:
time: 212 us
  Pallas kernels  87.7 us (41%)
  waiting for transfers between devices  67.8 us (32%)
  starting transfers between devices  47.9 us (23%)
  local copies, waits for them, and re-layouts  6.45 us (3%)
    ppermute x15, waiting for transfers between devices, from_chip(): return lax.ppermute(values, 'fsdp', [(i, i ^ 2 * flip) for i in range(8)])  30.2 us
    pallas_call x4, Pallas kernels, pieces_grad(): pl.pallas_call(kernel, grid_spec=pltpu.PrefetchScalarGridSpec(num_scalar_...  21.3 us
    ppermute x6, waiting for transfers between devices, from_y(): return lax.ppermute(values, 'dp', [(i, i ^ 2) for i in range(4)])  16.3 us
    ppermute x15, starting transfers between devices, from_chip(): return lax.ppermute(values, 'fsdp', [(i, i ^ 2 * flip) for i in range(8)])  16.3 us
    ppermute x12, starting transfers between devices, from_plane(): lax.ppermute(part, 'dp', [(i, i ^ flip) for i in range(4)])  14.2 us
    ppermute x12, waiting for transfers between devices, from_plane(): lax.ppermute(part, 'dp', [(i, i ^ flip) for i in range(4)])  10.5 us
    pallas_call x1, Pallas kernels, attend(): pl.pallas_call(attend_kernel, grid_spec=pltpu.PrefetchScalarGridSpec(num_...  8.75 us
    pallas_call x1, Pallas kernels, expand_act(): pl.pallas_call(functools.partial(expand_kernel, weight=weight, tile=tile)...  8.54 us
  transfers between devices with their start and end apart: 54, of which 24 were waited for; matrix products, arithmetic and copies ran while one was open for 3% of the time, Pallas kernels for 33%

commit v1 on v0

--- a/solution.py
+++ b/solution.py
@@ -636,49 +636,56 @@
     )(left, right)
 
 
-def store_halves(out, core, grads, pos, along, extra):
-    rows, wide = out.shape[3], grads.shape[1]
-    for chip in range(4):
-        for up in range(2):
-            at = ((chip * 2 + core) * 2 + up) * rows
-            to = (chip ^ pos[0], up ^ pos[2], along ^ pos[3])
-            out[(*to, slice(None), slice(0, wide))] = grads[at : at + rows].astype(BF16)
-            if extra is not None:
-                out[(*to, slice(None), slice(wide, None))] = jnp.zeros((rows, 128), BF16)
-                out[(*to, slice(0, 16), slice(wide, None))] = extra[chip * 2 + core].astype(BF16)
-
-
-def store_stacked(out, core, grads, pos, chip):
-    rows, wide = out.shape[3], grads.shape[1]
-    for quarter in range(4):
-        for part in range(2):
-            at = ((core * 4 + quarter) * 2 + part) * rows
-            to = (chip ^ pos[0], (quarter // 2) ^ pos[2], (quarter % 2) ^ pos[3])
-            out[(*to, slice(None), slice(part * wide, (part + 1) * wide))] = grads[at : at + rows].astype(BF16)
+def regroup_kernel(values, out):
+    part = values.shape[1] // 8
+    blocks = [values[:, shard * part : (shard + 1) * part] for shard in (0, 2, 4, 6, 1, 3, 5, 7)]
+    out[...] = jnp.concatenate(blocks, axis=1)
+
+
+def regroup(values):
+    return held_call(regroup_kernel, "regroup", [values.shape], [values])[0]
 
 
 def by_core(pos, mine, theirs, store):
-    for core in range(2):
-
-        @pl.when(pos[1] == core)
-        def _(core=core):
-            store(mine, core)
-            store(theirs, 1 - core)
+    store(mine, pos[1])
+    store(theirs, 1 - pos[1])
 
 
 def halves_grad_kernel(pos, left, right, *rest):
     extra, (mine, theirs) = (rest[0] if len(rest) == 3 else None), rest[-2:]
     along, half = pl.program_id(0), right.shape[1] // 2
-    grads = dot(left[...], right[:, columns_of(half)], TN)
-    by_core(pos, mine, theirs, lambda out, core: store_halves(out, core, grads, pos, along, extra))
+    columns, high, rows = right[:, columns_of(half)], left.shape[1] // 2, mine.shape[3]
+
+    def store(out, core):
+        grads = dot(left[:, pl.ds(pl.multiple_of(core * high, 128), high)], columns, TN)
+        for chip in range(4):
+            for up in range(2):
+                at = (chip * 2 + up) * rows
+                to = (chip ^ pos[0], up ^ pos[2], along ^ pos[3])
+                out[(*to, slice(None), slice(0, half))] = grads[at : at + rows].astype(BF16)
+                if extra is not None:
+                    out[(*to, slice(None), slice(half, None))] = jnp.zeros((rows, 128), BF16)
+                    out[(*to, slice(0, 16), slice(half, None))] = extra[chip * 2 + core].astype(BF16)
+
+    by_core(pos, mine, theirs, store)
 
 
 def stacked_grad_kernel(pos, left, right, mine, theirs):
-    high = left.shape[1] // 4
-    grads = dot(left[:, columns_of(2 * high)], right[...], TN)
-    for part in range(2):
-        chip, block = pl.program_id(0) * 2 + part, grads[part * high : (part + 1) * high]
-        by_core(pos, mine, theirs, lambda out, core: store_stacked(out, core, block, pos, chip))
+    high, rows, wide = left.shape[1] // 8, mine.shape[3], right.shape[1]
+
+    def store(out, core):
+        for part in range(2):
+            chip = pl.program_id(0) * 2 + part
+            columns = pl.ds(pl.multiple_of((chip * 2 + core) * high, 128), high)
+            grads = dot(left[:, columns], right[...], TN)
+            for quarter in range(4):
+                for side in range(2):
+                    at = (quarter * 2 + side) * rows
+                    to = (chip ^ pos[0], (quarter // 2) ^ pos[2], (quarter % 2) ^ pos[3])
+                    block = grads[at : at + rows].astype(BF16)
+                    out[(*to, slice(None), slice(side * wide, (side + 1) * wide))] = block
+
+    by_core(pos, mine, theirs, store)
 
 
 def pieces_grad(kernel, name, pos, left, right, shape, extra=()):
@@ -1056,7 +1063,8 @@
         mine_e = below(*near_e, far_e, wide=wide_e)
         plane_e = from_plane(mine_e)
         held = jnp.concatenate([held, *(chip[:16, wide_e:] for chip in (*near_e, far_e))], axis=0)
-        held = after(held, mine_e)
+        token_group = regroup(after(token_rows, plane_p))
+        held = after(held, mine_e, token_group)
         bias_full, hidden_bias, rows6 = spread(pos, [held, from_core(held)], width, expand_weight.shape[1])
         out_bias, gain1, shift1, down_bias, gain2, shift2 = (rows6[at : at + 1] for at in range(6))
     else:
@@ -1081,7 +1089,8 @@
     if pieces:
         far_s = after(far_s, context)
         near_s = [near_s, from_chip(far_s, 1)]
-        plane_e = below(*after(plane_e, far_s))
+        context_group = regroup(context_rows)
+        plane_e = below(*after(plane_e, far_s, context_group))
         mine_s = below(*after(near_s, plane_e), far_s, flops=COVER)
         left_s, right_s = left_right(mine_s)
         plane_s = [from_x(left_s), from_y(right_s)]
@@ -1095,11 +1104,12 @@
     active, slope, expand = expand_act(pos, normed_low, expand, hidden_bias)
     if pieces:
         plane_s = beside(*after(plane_s, active))
+        normed_group = regroup(after(normed_low, plane_s))
         other_s = [from_core(mine_s), from_core(plane_s)]
         sibling_s = from_core(after(shrink_weight, active))
         shrink = Weight(
             shapes[3],
-            [shrink_weight, sibling_s, mine_s, plane_s, *other_s],
+            [shrink_weight, sibling_s, mine_s, plane_s, *after(other_s, normed_group)],
             functools.partial(stacked_copies, high=shrink_weight.shape[0], wide=shrink_weight.shape[1]),
         )
     out_rows, shrink_low, second_grad, sums2, shrink = second_norm(
@@ -1116,7 +1126,7 @@
         keep_s, near_s, kept_s, send_s = shrink_sum(mine_s, after(theirs_s, expand_low))
         expand_low = after(expand_low, kept_s)
         near_s, send_s = from_chip(near_s, 1), from_x(send_s)
-        mine_e, theirs_e = halves_grad(pos, normed_low, expand_low)
+        mine_e, theirs_e = halves_grad(pos, normed_group, expand_low)
         theirs_e = from_core(theirs_e)
         expand_low = after(expand_low, mine_e)
     first_grad, branch_low, context_grad, sums1 = first_back(
@@ -1124,7 +1134,7 @@
     )
     if pieces:
         own_s, later_s = pair_sum(kept_s, after(send_s, branch_low))
-        mine_o, theirs_o = halves_grad(pos, context_rows, after(branch_low, own_s))
+        mine_o, theirs_o = halves_grad(pos, context_group, after(branch_low, own_s))
         theirs_o = from_core(theirs_o)
         later_s = from_y(later_s)
         keep_s, far_s = pair_sum(keep_s, after(near_s, mine_o))
@@ -1141,7 +1151,7 @@
     joined_grad_rows = joined_grad.reshape(rows, 3 * width)
     if pieces:
         extra = bundle(sums_joined, sums1, sums2, sums_hidden)
-        mine_p, theirs_p = halves_grad(pos, token_rows, joined_grad_rows, extra)
+        mine_p, theirs_p = halves_grad(pos, token_group, joined_grad_rows, extra)
         theirs_p = from_core(theirs_p)
         out_x, out_y = after((out_x, out_y), mine_p)
         own_x, later_x, own_y, later_y = middle_sum([own_x, later_x, out_x, own_y, later_y, out_y])

time: 212 us -> 210 us (level)
  waiting for transfers between devices: 67.8 us -> 61.2 us
  starting transfers between devices: 47.9 us -> 51.9 us
    ppermute x15, starting transfers between devices: 16.3 us -> 21.3 us  [from_chip(): return lax.ppermute(values, 'fsdp', [(i, i ^ 2 * flip) for i in range(8)])]
    pallas_call x16 -> x19, Pallas kernels: 3.49 us -> 5.38 us  [held_call(): pl.pallas_call(kernel, in_specs=[HELD] * len(values), out_specs=[HELD] *...]
  transfers between devices with their start and end apart: 54 -> 54, of which waited for: 24 -> 26; matrix products, arithmetic and copies ran while one was open for 3% -> 3% of each run, Pallas kernels for 33% -> 33%
where the time goes in v1:
time: 210 us
  Pallas kernels  88.1 us (42%)
  waiting for transfers between devices  61.2 us (29%)
  starting transfers between devices  51.9 us (25%)
  local copies, waits for them, and re-layouts  6.45 us (3%)
    ppermute x15, waiting for transfers between devices, from_chip(): return lax.ppermute(values, 'fsdp', [(i, i ^ 2 * flip) for i in range(8)])  28.4 us
    ppermute x15, starting transfers between devices, from_chip(): return lax.ppermute(values, 'fsdp', [(i, i ^ 2 * flip) for i in range(8)])  21.3 us
    pallas_call x4, Pallas kernels, pieces_grad(): pl.pallas_call(kernel, grid_spec=pltpu.PrefetchScalarGridSpec(num_scalar_...  19.7 us
    ppermute x6, waiting for transfers between devices, from_y(): return lax.ppermute(values, 'dp', [(i, i ^ 2) for i in range(4)])  15.2 us
    ppermute x12, starting transfers between devices, from_plane(): lax.ppermute(part, 'dp', [(i, i ^ flip) for i in range(4)])  14.2 us
    pallas_call x1, Pallas kernels, attend(): pl.pallas_call(attend_kernel, grid_spec=pltpu.PrefetchScalarGridSpec(num_...  8.75 us
    pallas_call x1, Pallas kernels, second_norm(): pl.pallas_call(functools.partial(second_kernel, weight=weight, seq=seq),...  8.63 us
    pallas_call x1, Pallas kernels, expand_act(): pl.pallas_call(functools.partial(expand_kernel, weight=weight, tile=tile)...  8.5 us
  transfers between devices with their start and end apart: 54, of which 26 were waited for; matrix products, arithmetic and copies ran while one was open for 3% of the time, Pallas kernels for 33%

profile of v1, /device:TPU:0, one launch (start us, length us, event | category | flops | bytes accessed | tf_op | source)
XLA Modules:
  0.0 209.6 jit_solution(16399825382385369281)
XLA Ops:
  2.1 3.7 %collective-permute-start.2 = (bf16[48,1152]{1,0:T(8,128)(2,1)S(1)}, bf16[48,1152]{1,0:T(8,128)(2,1)S(1)}, u32[]{:S(2)}, u32[]{:S(2)}) collective-permute-start(bf16[48,1152]{1,0:T(8,128)(2,1)S(1)} %dynamic_slice.11), channel_id=1, source_target_pairs={{0,4},{1,5},{2,6},{3,7},{4,0},{5,1},{6,2},{7,3},{8,12},{9,13},{10,... | collective-permute-start | bytes 331784 | tf_op jit(solution)/shard_map/ppermute | solution.py:924
  12.1 2.4 %collective-permute-done.2.refs_2_ = bf16[48,1152]{1,0:T(8,128)(2,1)S(1)} collective-permute-done((bf16[48,1152]{1,0:T(8,128)(2,1)S(1)}, bf16[48,1152]{1,0:T(8,128)(2,1)S(1)}, u32[]{:S(2)}, u32[]{:S(2)}) %collective-permute-start.2) | collective-permute-done | bytes 110624 | tf_op jit(solution)/shard_map/ppermute | solution.py:924
  16.4 2.6 %collective-permute-start.9 = (bf16[144,1152]{1,0:T(8,128)(2,1)S(1)}, bf16[144,1152]{1,0:T(8,128)(2,1)S(1)}, u32[]{:S(2)}, u32[]{:S(2)}) collective-permute-start(bf16[144,1152]{1,0:T(8,128)(2,1)S(1)} %below.5.rest_2_), channel_id=1, source_target_pairs={{0,24},{8,16},{16,8},{24,0},{1,25},{9,17},{17,9},{25,1},{2,26},{10... | collective-permute-start | bytes 995336 | tf_op jit(solution)/shard_map/ppermute | solution.py:907
  19.9 3.7 %collective-permute-start.5 = (bf16[48,2048]{1,0:T(8,128)(2,1)S(1)}, bf16[48,2048]{1,0:T(8,128)(2,1)S(1)}, u32[]{:S(2)}, u32[]{:S(2)}) collective-permute-start(bf16[48,2048]{1,0:T(8,128)(2,1)S(1)} %fusion.1), channel_id=1, source_target_pairs={{0,4},{1,5},{2,6},{3,7},{4,0},{5,1},{6,2},{7,3},{8,12},{9,13},{10,... | collective-permute-start | bytes 589832 | tf_op jit(solution)/shard_map/ppermute | solution.py:924
  24.0 8.2 %collective-permute-done.5.refs_2_ = bf16[48,2048]{1,0:T(8,128)(2,1)S(1)} collective-permute-done((bf16[48,2048]{1,0:T(8,128)(2,1)S(1)}, bf16[48,2048]{1,0:T(8,128)(2,1)S(1)}, u32[]{:S(2)}, u32[]{:S(2)}) %collective-permute-start.5) | collective-permute-done | bytes 196640 | tf_op jit(solution)/shard_map/ppermute | solution.py:924
  34.2 5.4 %collective-permute-done.6.refs_1_ = bf16[48,2048]{1,0:T(8,128)(2,1)S(1)} collective-permute-done((bf16[48,2048]{1,0:T(8,128)(2,1)S(1)}, bf16[48,2048]{1,0:T(8,128)(2,1)S(1)}, u32[]{:S(2)}, u32[]{:S(2)}) %collective-permute-start.6) | collective-permute-done | bytes 196640 | tf_op jit(solution)/shard_map/ppermute | solution.py:924
  41.4 2.4 %collective-permute-start.18 = (bf16[144,1920]{1,0:T(8,128)(2,1)S(1)}, bf16[144,1920]{1,0:T(8,128)(2,1)S(1)}, u32[]{:S(2)}, u32[]{:S(2)}) collective-permute-start(bf16[144,1920]{1,0:T(8,128)(2,1)S(1)} %below.7.rest_2_), channel_id=1, source_target_pairs={{0,24},{8,16},{16,8},{24,0},{1,25},{9,17},{17,9},{25,1},{2,26},{10... | collective-permute-start | bytes 1658888 | tf_op jit(solution)/shard_map/ppermute | solution.py:907
  45.6 5.5 %join.1 = (bf16[832,2304]{1,0:T(8,128)(2,1)}, bf16[768,2304]{1,0:T(8,128)(2,1)}) custom-call(s32[4]{0:T(128)S(1)} %pad_add_fusion.pos, bf16[832,768]{1,0:T(8,128)(2,1)S(1)} %bitcast.28, f32[1,2304]{1,0:T(1,128)S(1)} %get-tuple-element.168.bias, bf16[96,2304]{1,0:T(8,128)(2,1)S(1)} %copy-done.5, bf16[96,2304]{1,0:T(8,128)(2,1)S(1)} %copy-done.7, ...), custom_call_target="tpu_custom_call" | custom-call | tf_op jit(solution)/shard_map/join/pallas_call | solution.py:232
  51.1 1.8 collective-permute-start.13
  53.0 8.7 %attend.1 = (bf16[8,104,768]{2,1,0:T(8,128)(2,1)S(1)}, bf16[8,6,104,256]{3,2,1,0:T(8,128)(2,1)}) custom-call(s32[8]{0:T(128)S(1)} %copy-done.9, bf16[8,104,2304]{2,1,0:T(8,128)(2,1)} %bitcast.34), custom_call_target="tpu_custom_call" | custom-call | tf_op jit(solution)/shard_map/attend/pallas_call | solution.py:288
  62.7 5.7 %collective-permute-done.17.refs_1_ = bf16[144,1920]{1,0:T(8,128)(2,1)S(1)} collective-permute-done((bf16[144,1920]{1,0:T(8,128)(2,1)S(1)}, bf16[144,1920]{1,0:T(8,128)(2,1)S(1)}, u32[]{:S(2)}, u32[]{:S(2)}) %collective-permute-start.17) | collective-permute-done | bytes 552992 | tf_op jit(solution)/shard_map/ppermute | solution.py:907
  74.1 2.4 %first_norm.1 = (f32[832,768]{1,0:T(8,128)S(1)}, f32[832,1]{1,0:T(8,128)S(1)}, bf16[832,768]{1,0:T(8,128)(2,1)S(1)}, bf16[768,768]{1,0:T(8,128)(2,1)S(1)}) custom-call(s32[4]{0:T(128)S(1)} %pad_add_fusion.pos, bf16[832,768]{1,0:T(8,128)(2,1)S(1)} %bitcast.31, f32[1,768]{1,0:T(1,128)S(1)} %get-tuple-element.311.bias, bf16[832,768]{1,0:T(8,128)(2,1)S(1)} %bitcast.29, ...), custom_call_target="tpu_custom_call" | custom-call | tf_op jit(solution)/shard_map/first_norm/pallas_call | solution.py:424
  76.5 8.5 %expand_act.1 = (bf16[832,3072]{1,0:T(8,128)(2,1)S(1)}, bf16[832,3072]{1,0:T(8,128)(2,1)S(1)}, bf16[768,3072]{1,0:T(8,128)(2,1)S(1)}) custom-call(s32[4]{0:T(128)S(1)} %pad_add_fusion.pos, bf16[832,768]{1,0:T(8,128)(2,1)S(1)} %get-tuple-element.195.normed_low.values, f32[1,3072]{1,0:T(1,128)S(1)} %get-tuple-element.186.bias, bf16[96,3072]{1,0:T(8,128)(2,1)S(1)} %copy-done.4, ...), custom_call_target="tpu_custom_call" | custom-call | tf_op jit(solution)/shard_map/expand_act/pallas_call | solution.py:453
  88.5 8.6 %second_norm.1 = (bf16[832,768]{1,0:T(8,128)(2,1)}, bf16[832,768]{1,0:T(8,128)(2,1)S(1)}, f32[832,768]{1,0:T(8,128)S(1)}, f32[8,768]{1,0:T(8,128)S(1)}, bf16[3072,768]{1,0:T(8,128)(2,1)S(1)}) custom-call(s32[4]{0:T(128)S(1)} %pad_add_fusion.pos, s32[8]{0:T(128)S(1)} %copy-done.9, bf16[832,3072]{1,0:T(8,128)(2,1)S(1)} %get-tuple-element.188.active.left, ...), custom_call_target="tpu_custom_call" | custom-call | tf_op jit(solution)/shard_map/second_norm/pallas_call | solution.py:505
  97.1 5.9 %stacked_grad.1 = (bf16[4,2,2,48,1536]{4,3,2,1,0:T(8,128)(2,1)S(1)}, bf16[4,2,2,48,1536]{4,3,2,1,0:T(8,128)(2,1)S(1)}) custom-call(s32[4]{0:T(128)S(1)} %pad_add_fusion.pos, bf16[832,3072]{1,0:T(8,128)(2,1)S(1)} %get-tuple-element.188.active.left, bf16[832,768]{1,0:T(8,128)(2,1)S(1)} %get-tuple-element.202.right.low), custom_call_target="tpu_custom_call" | custom-call | tf_op jit(solution)/shard_map/stacked_grad/pallas_call | solution.py:693
  103.3 4.9 %hidden_back.1 = (bf16[832,3072]{1,0:T(8,128)(2,1)S(1)}, f32[1,3072]{1,0:T(1,128)S(1)}) custom-call(bf16[832,768]{1,0:T(8,128)(2,1)S(1)} %get-tuple-element.202.right.low, bf16[3072,768]{1,0:T(8,128)(2,1)S(1)} %get-tuple-element.203.weight, bf16[832,3072]{1,0:T(8,128)(2,1)S(1)} %get-tuple-element.204.slope), custom_call_target="tpu_custom_call" | custom-call | tf_op jit(solution)/shard_map/hidden_back/pallas_call | solution.py:538
  111.2 6.1 %halves_grad.3 = (bf16[4,2,2,48,1536]{4,3,2,1,0:T(8,128)(2,1)S(1)}, bf16[4,2,2,48,1536]{4,3,2,1,0:T(8,128)(2,1)S(1)}) custom-call(s32[4]{0:T(128)S(1)} %pad_add_fusion.pos, bf16[832,768]{1,0:T(8,128)(2,1)S(1)} %regroup.5.left, bf16[832,3072]{1,0:T(8,128)(2,1)S(1)} %get-tuple-element.211.right.hidden), custom_call_target="tpu_custom_call" | custom-call | tf_op jit(solution)/shard_map/halves_grad/pallas_call | solution.py:693
  117.4 6.0 %first_back.1 = (f32[832,768]{1,0:T(8,128)S(1)}, bf16[832,768]{1,0:T(8,128)(2,1)S(1)}, bf16[832,768]{1,0:T(8,128)(2,1)S(1)}, f32[8,768]{1,0:T(8,128)S(1)}) custom-call(bf16[832,3072]{1,0:T(8,128)(2,1)S(1)} %get-tuple-element.211.right.hidden, bf16[768,3072]{1,0:T(8,128)(2,1)S(1)} %get-tuple-element.212.weight, f32[832,768]{1,0:T(8,128)S(1)} %get-tuple-element.213.second, ...), custom_call_target="tpu_custom_call" | custom-call | flops 99999997952 | tf_op jit(solution)/shard_map/first_back/pallas_call | solution.py:578
  123.5 2.5 %halves_grad.4 = (bf16[4,2,2,48,384]{4,3,2,1,0:T(8,128)(2,1)S(1)}, bf16[4,2,2,48,384]{4,3,2,1,0:T(8,128)(2,1)S(1)}) custom-call(s32[4]{0:T(128)S(1)} %pad_add_fusion.pos, bf16[832,768]{1,0:T(8,128)(2,1)S(1)} %regroup.4.left, bf16[832,768]{1,0:T(8,128)(2,1)S(1)} %get-tuple-element.221.right), custom_call_target="tpu_custom_call" | custom-call | tf_op jit(solution)/shard_map/halves_grad/pallas_call | solution.py:693
  126.6 2.4 %collective-permute-done.32.received = bf16[2,4,48,1024]{3,2,1,0:T(8,128)(2,1)S(1)} collective-permute-done((bf16[2,4,48,1024]{3,2,1,0:T(8,128)(2,1)S(1)}, bf16[2,4,48,1024]{3,2,1,0:T(8,128)(2,1)S(1)}, u32[]{:S(2)}, u32[]{:S(2)}) %collective-permute-start.32) | collective-permute-done | bytes 786464 | tf_op jit(solution)/shard_map/ppermute | solution.py:924
  131.9 2.4 %collective-permute-start.39 = (bf16[4,48,1024]{2,1,0:T(8,128)(2,1)S(1)}, bf16[4,48,1024]{2,1,0:T(8,128)(2,1)S(1)}, u32[]{:S(2)}, u32[]{:S(2)}) collective-permute-start(bf16[4,48,1024]{2,1,0:T(8,128)(2,1)S(1)} %get-tuple-element.251), channel_id=1, source_target_pairs={{0,4},{1,5},{2,6},{3,7},{4,0},{5,1},{6,2},{7,3},{8,12},{9,13},{10,... | collective-permute-start | bytes 1179656 | tf_op jit(solution)/shard_map/ppermute | solution.py:924
  134.3 8.4 %attend_back.1 = (bf16[8,104,2304]{2,1,0:T(8,128)(2,1)S(1)}, f32[1,1536]{1,0:T(1,128)S(1)}) custom-call(bf16[8,104,2304]{2,1,0:T(8,128)(2,1)} %bitcast.35, bf16[8,6,104,256]{3,2,1,0:T(8,128)(2,1)} %get-tuple-element.199.probs, bf16[8,104,768]{2,1,0:T(8,128)(2,1)S(1)} %bitcast.33), custom_call_target="tpu_custom_call" | custom-call | tf_op jit(solution)/shard_map/attend_back/pallas_call | solution.py:350
  142.8 5.1 %halves_grad.5 = (bf16[4,2,2,48,1280]{4,3,2,1,0:T(8,128)(2,1)S(1)}, bf16[4,2,2,48,1280]{4,3,2,1,0:T(8,128)(2,1)S(1)}) custom-call(s32[4]{0:T(128)S(1)} %pad_add_fusion.pos, bf16[832,768]{1,0:T(8,128)(2,1)S(1)} %regroup.3.left, bf16[832,2304]{1,0:T(8,128)(2,1)S(1)} %bitcast.25, f32[8,16,128]{2,1,0:T(8,128)S(1)} %bundle.1.rest_0_), custom_call_target="tpu_custom_call" | custom-call | tf_op jit(solution)/shard_map/halves_grad/pallas_call | solution.py:693
  152.0 7.9 %collective-permute-done.37.received = bf16[2,48,1920]{2,1,0:T(8,128)(2,1)S(1)} collective-permute-done((bf16[2,48,1920]{2,1,0:T(8,128)(2,1)S(1)}, bf16[2,48,1920]{2,1,0:T(8,128)(2,1)S(1)}, u32[]{:S(2)}, u32[]{:S(2)}) %collective-permute-start.37) | collective-permute-done | bytes 368672 | tf_op jit(solution)/shard_map/ppermute | solution.py:916
  160.0 1.9 collective-permute-done.34.two
  165.3 4.5 %token_back.1 = f32[832,768]{1,0:T(8,128)} custom-call(bf16[832,2304]{1,0:T(8,128)(2,1)S(1)} %bitcast.26, bf16[768,2304]{1,0:T(8,128)(2,1)S(1)} %copy-done.1, f32[832,768]{1,0:T(8,128)S(1)} %get-tuple-element.263.first), custom_call_target="tpu_custom_call" | custom-call | tf_op jit(solution)/shard_map/token_back/pallas_call | solution.py:603
  169.8 5.2 %collective-permute-done.40.refs_2_ = bf16[2,2,48,1536]{3,2,1,0:T(8,128)(2,1)S(1)} collective-permute-done((bf16[2,2,48,1536]{3,2,1,0:T(8,128)(2,1)S(1)}, bf16[2,2,48,1536]{3,2,1,0:T(8,128)(2,1)S(1)}, u32[]{:S(2)}, u32[]{:S(2)}) %collective-permute-start.40) | collective-permute-done | bytes 589856 | tf_op jit(solution)/shard_map/ppermute | solution.py:912
  180.9 2.9 %collective-permute-done.42.received = bf16[2,48,1536]{2,1,0:T(8,128)(2,1)S(1)} collective-permute-done((bf16[2,48,1536]{2,1,0:T(8,128)(2,1)S(1)}, bf16[2,48,1536]{2,1,0:T(8,128)(2,1)S(1)}, u32[]{:S(2)}, u32[]{:S(2)}) %collective-permute-start.42) | collective-permute-done | bytes 294944 | tf_op jit(solution)/shard_map/ppermute | solution.py:916
  184.9 1.9 collective-permute-start.45
  186.8 2.0 collective-permute-done.46.refs_2_
  193.9 6.1 %collective-permute-done.47.refs_1_ = bf16[48,1280]{1,0:T(8,128)(2,1)S(1)} collective-permute-done((bf16[48,1280]{1,0:T(8,128)(2,1)S(1)}, bf16[48,1280]{1,0:T(8,128)(2,1)S(1)}, u32[]{:S(2)}, u32[]{:S(2)}) %collective-permute-start.47) | collective-permute-done | bytes 122912 | tf_op jit(solution)/shard_map/ppermute | solution.py:924
  203.6 2.2 %place.2 = (f32[384,768]{1,0:T(8,128)}, f32[96,3072]{1,0:T(8,128)}, f32[96,768]{1,0:T(8,128)}) custom-call(s32[4]{0:T(128)S(1)} %pad_add_fusion.pos, bf16[48,3456]{1,0:T(8,128)(2,1)S(1)} %last_sum.2.refs_0_, bf16[48,3456]{1,0:T(8,128)(2,1)S(1)} %collective-permute-done.51.refs_1_, bf16[48,3456]{1,0:T(8,128)(2,1)S(1)} %collective-permute-done.52.refs_2_, ...), custom_call_target="tpu_custom_call" | custom-call | tf_op jit(solution)/shard_map/place/pallas_call | solution.py:885
  (153 shorter events, 60.4 us)
Async XLA Ops:
  0.6 14.9 %collective-permute-start.3 = (bf16[96,2304]{1,0:T(8,128)(2,1)}, bf16[96,2304]{1,0:T(8,128)(2,1)S(1)}, u32[]{:S(2)}, u32[]{:S(2)}) collective-permute-start(bf16[96,2304]{1,0:T(8,128)(2,1)} %rest_0_.4), channel_id=1, source_target_pairs={{0,1},{1,0},{2,3},{3,2},{4,5},{5,4},{6,7},{7,6},{8,9},{9,8},{10,11... | collective-permute-start | bytes 1327112 | tf_op jit(solution)/shard_map/ppermute | solution.py:901
  2.1 12.4 %collective-permute-start.2 = (bf16[48,1152]{1,0:T(8,128)(2,1)S(1)}, bf16[48,1152]{1,0:T(8,128)(2,1)S(1)}, u32[]{:S(2)}, u32[]{:S(2)}) collective-permute-start(bf16[48,1152]{1,0:T(8,128)(2,1)S(1)} %dynamic_slice.11), channel_id=1, source_target_pairs={{0,4},{1,5},{2,6},{3,7},{4,0},{5,1},{6,2},{7,3},{8,12},{9,13},{10,... | collective-permute-start | bytes 331784 | tf_op jit(solution)/shard_map/ppermute | solution.py:924
  16.4 15.8 %collective-permute-start.9 = (bf16[144,1152]{1,0:T(8,128)(2,1)S(1)}, bf16[144,1152]{1,0:T(8,128)(2,1)S(1)}, u32[]{:S(2)}, u32[]{:S(2)}) collective-permute-start(bf16[144,1152]{1,0:T(8,128)(2,1)S(1)} %below.5.rest_2_), channel_id=1, source_target_pairs={{0,24},{8,16},{16,8},{24,0},{1,25},{9,17},{17,9},{25,1},{2,26},{10... | collective-permute-start | bytes 995336 | tf_op jit(solution)/shard_map/ppermute | solution.py:907
  18.9 14.4 %collective-permute-start.8 = (bf16[144,1152]{1,0:T(8,128)(2,1)S(1)}, bf16[144,1152]{1,0:T(8,128)(2,1)S(1)}, u32[]{:S(2)}, u32[]{:S(2)}) collective-permute-start(bf16[144,1152]{1,0:T(8,128)(2,1)S(1)} %below.5.rest_2_), channel_id=1, source_target_pairs={{0,16},{8,24},{16,0},{24,8},{1,17},{9,25},{17,1},{25,9},{2,18},{10... | collective-permute-start | bytes 995336 | tf_op jit(solution)/shard_map/ppermute | solution.py:907
  19.4 14.0 %collective-permute-start.7 = (bf16[144,1152]{1,0:T(8,128)(2,1)S(1)}, bf16[144,1152]{1,0:T(8,128)(2,1)S(1)}, u32[]{:S(2)}, u32[]{:S(2)}) collective-permute-start(bf16[144,1152]{1,0:T(8,128)(2,1)S(1)} %below.5.rest_2_), channel_id=1, source_target_pairs={{0,8},{8,0},{16,24},{24,16},{1,9},{9,1},{17,25},{25,17},{2,10},{10... | collective-permute-start | bytes 995336 | tf_op jit(solution)/shard_map/ppermute | solution.py:907
  19.9 12.3 %collective-permute-start.5 = (bf16[48,2048]{1,0:T(8,128)(2,1)S(1)}, bf16[48,2048]{1,0:T(8,128)(2,1)S(1)}, u32[]{:S(2)}, u32[]{:S(2)}) collective-permute-start(bf16[48,2048]{1,0:T(8,128)(2,1)S(1)} %fusion.1), channel_id=1, source_target_pairs={{0,4},{1,5},{2,6},{3,7},{4,0},{5,1},{6,2},{7,3},{8,12},{9,13},{10,... | collective-permute-start | bytes 589832 | tf_op jit(solution)/shard_map/ppermute | solution.py:924
  23.6 10.6 %collective-permute-start.4 = (bf16[48,2048]{1,0:T(8,128)(2,1)S(1)}, bf16[48,2048]{1,0:T(8,128)(2,1)S(1)}, u32[]{:S(2)}, u32[]{:S(2)}) collective-permute-start(bf16[48,2048]{1,0:T(8,128)(2,1)S(1)} %fusion.1), channel_id=1, source_target_pairs={{0,2},{1,3},{2,0},{3,1},{4,6},{5,7},{6,4},{7,5},{8,10},{9,11},{10,... | collective-permute-start | bytes 589832 | tf_op jit(solution)/shard_map/ppermute | solution.py:924
  32.2 11.7 %collective-permute-start.11 = (bf16[144,1152]{1,0:T(8,128)(2,1)S(1)}, bf16[144,1152]{1,0:T(8,128)(2,1)S(1)}, u32[]{:S(2)}, u32[]{:S(2)}) collective-permute-start(bf16[144,1152]{1,0:T(8,128)(2,1)S(1)} %below.5.rest_2_), channel_id=1, source_target_pairs={{0,1},{1,0},{2,3},{3,2},{4,5},{5,4},{6,7},{7,6},{8,9},{9,8},{10,11... | collective-permute-start | bytes 995336 | tf_op jit(solution)/shard_map/ppermute | solution.py:901
  41.0 20.7 %collective-permute-start.14 = (bf16[96,1536]{1,0:T(8,128)(2,1)S(1)}, bf16[96,1536]{1,0:T(8,128)(2,1)S(1)}, u32[]{:S(2)}, u32[]{:S(2)}) collective-permute-start(bf16[96,1536]{1,0:T(8,128)(2,1)S(1)} %pick.1), channel_id=1, source_target_pairs={{0,4},{1,5},{2,6},{3,7},{4,0},{5,1},{6,2},{7,3},{8,12},{9,13},{10,... | collective-permute-start | bytes 884744 | tf_op jit(solution)/shard_map/ppermute | solution.py:924
  41.4 21.2 %collective-permute-start.18 = (bf16[144,1920]{1,0:T(8,128)(2,1)S(1)}, bf16[144,1920]{1,0:T(8,128)(2,1)S(1)}, u32[]{:S(2)}, u32[]{:S(2)}) collective-permute-start(bf16[144,1920]{1,0:T(8,128)(2,1)S(1)} %below.7.rest_2_), channel_id=1, source_target_pairs={{0,24},{8,16},{16,8},{24,0},{1,25},{9,17},{17,9},{25,1},{2,26},{10... | collective-permute-start | bytes 1658888 | tf_op jit(solution)/shard_map/ppermute | solution.py:907
  43.9 24.5 %collective-permute-start.17 = (bf16[144,1920]{1,0:T(8,128)(2,1)S(1)}, bf16[144,1920]{1,0:T(8,128)(2,1)S(1)}, u32[]{:S(2)}, u32[]{:S(2)}) collective-permute-start(bf16[144,1920]{1,0:T(8,128)(2,1)S(1)} %below.7.rest_2_), channel_id=1, source_target_pairs={{0,16},{8,24},{16,0},{24,8},{1,17},{9,25},{17,1},{25,9},{2,18},{10... | collective-permute-start | bytes 1658888 | tf_op jit(solution)/shard_map/ppermute | solution.py:907
  44.4 24.1 %collective-permute-start.16 = (bf16[144,1920]{1,0:T(8,128)(2,1)S(1)}, bf16[144,1920]{1,0:T(8,128)(2,1)S(1)}, u32[]{:S(2)}, u32[]{:S(2)}) collective-permute-start(bf16[144,1920]{1,0:T(8,128)(2,1)S(1)} %below.7.rest_2_), channel_id=1, source_target_pairs={{0,8},{8,0},{16,24},{24,16},{1,9},{9,1},{17,25},{25,17},{2,10},{10... | collective-permute-start | bytes 1658888 | tf_op jit(solution)/shard_map/ppermute | solution.py:907
  51.1 18.0 %collective-permute-start.13 = (bf16[96,1536]{1,0:T(8,128)(2,1)S(1)}, bf16[96,1536]{1,0:T(8,128)(2,1)S(1)}, u32[]{:S(2)}, u32[]{:S(2)}) collective-permute-start(bf16[96,1536]{1,0:T(8,128)(2,1)S(1)} %pick.1), channel_id=1, source_target_pairs={{0,2},{1,3},{2,0},{3,1},{4,6},{5,7},{6,4},{7,5},{8,10},{9,11},{10,... | collective-permute-start | bytes 884744 | tf_op jit(solution)/shard_map/ppermute | solution.py:924
  62.6 10.1 %collective-permute-start.20 = (bf16[144,1920]{1,0:T(8,128)(2,1)S(1)}, bf16[144,1920]{1,0:T(8,128)(2,1)S(1)}, u32[]{:S(2)}, u32[]{:S(2)}) collective-permute-start(bf16[144,1920]{1,0:T(8,128)(2,1)S(1)} %below.7.rest_2_), channel_id=1, source_target_pairs={{0,1},{1,0},{2,3},{3,2},{4,5},{5,4},{6,7},{7,6},{8,9},{9,8},{10,11... | collective-permute-start | bytes 1658888 | tf_op jit(solution)/shard_map/ppermute | solution.py:901
  69.7 15.4 %collective-permute-start.24 = (bf16[288,768]{1,0:T(8,128)(2,1)S(1)}, bf16[288,768]{1,0:T(8,128)(2,1)S(1)}, u32[]{:S(2)}, u32[]{:S(2)}) collective-permute-start(bf16[288,768]{1,0:T(8,128)(2,1)S(1)} %get-tuple-element.191), channel_id=1, source_target_pairs={{0,8},{8,0},{16,24},{24,16},{1,9},{9,1},{17,25},{25,17},{2,10},{10... | collective-permute-start | bytes 1327112 | tf_op jit(solution)/shard_map/ppermute | solution.py:912
  71.2 13.8 %collective-permute-start.25 = (bf16[288,768]{1,0:T(8,128)(2,1)S(1)}, bf16[288,768]{1,0:T(8,128)(2,1)S(1)}, u32[]{:S(2)}, u32[]{:S(2)}) collective-permute-start(bf16[288,768]{1,0:T(8,128)(2,1)S(1)} %get-tuple-element.192), channel_id=1, source_target_pairs={{0,16},{8,24},{16,0},{24,8},{1,17},{9,25},{17,1},{25,9},{2,18},{10... | collective-permute-start | bytes 1327112 | tf_op jit(solution)/shard_map/ppermute | solution.py:916
  72.8 13.5 %collective-permute-start.26 = (bf16[288,1536]{1,0:T(8,128)(2,1)S(1)}, bf16[288,1536]{1,0:T(8,128)(2,1)S(1)}, u32[]{:S(2)}, u32[]{:S(2)}) collective-permute-start(bf16[288,1536]{1,0:T(8,128)(2,1)S(1)} %below.9.whole_ref.rest_2_), channel_id=1, source_target_pairs={{0,1},{1,0},{2,3},{3,2},{4,5},{5,4},{6,7},{7,6},{8,9},{9,8},{10,11... | collective-permute-start | bytes 2654216 | tf_op jit(solution)/shard_map/ppermute | solution.py:901
  108.8 14.5 %collective-permute-start.29 = (bf16[2,4,48,512]{3,2,1,0:T(8,128)(2,1)S(1)}, bf16[2,4,48,512]{3,2,1,0:T(8,128)(2,1)S(1)}, u32[]{:S(2)}, u32[]{:S(2)}) collective-permute-start(bf16[2,4,48,512]{3,2,1,0:T(8,128)(2,1)S(1)} %get-tuple-element.218), channel_id=1, source_target_pairs={{0,8},{8,0},{16,24},{24,16},{1,9},{9,1},{17,25},{25,17},{2,10},{10... | collective-permute-start | bytes 1179656 | tf_op jit(solution)/shard_map/ppermute | solution.py:912
  109.5 19.5 %collective-permute-start.32 = (bf16[2,4,48,1024]{3,2,1,0:T(8,128)(2,1)S(1)}, bf16[2,4,48,1024]{3,2,1,0:T(8,128)(2,1)S(1)}, u32[]{:S(2)}, u32[]{:S(2)}) collective-permute-start(bf16[2,4,48,1024]{3,2,1,0:T(8,128)(2,1)S(1)} %get-tuple-element.226), channel_id=1, source_target_pairs={{0,2},{1,3},{2,0},{3,1},{4,6},{5,7},{6,4},{7,5},{8,10},{9,11},{10,... | collective-permute-start | bytes 2359304 | tf_op jit(solution)/shard_map/ppermute | solution.py:924
  117.3 11.9 %collective-permute-start.30 = (bf16[4,2,2,48,1536]{4,3,2,1,0:T(8,128)(2,1)S(1)}, bf16[4,2,2,48,1536]{4,3,2,1,0:T(8,128)(2,1)S(1)}, u32[]{:S(2)}, u32[]{:S(2)}) collective-permute-start(bf16[4,2,2,48,1536]{4,3,2,1,0:T(8,128)(2,1)S(1)} %get-tuple-element.223), channel_id=1, source_target_pairs={{0,1},{1,0},{2,3},{3,2},{4,5},{5,4},{6,7},{7,6},{8,9},{9,8},{10,11... | collective-permute-start | bytes 7077896 | tf_op jit(solution)/shard_map/ppermute | solution.py:901
  129.9 18.1 %collective-permute-start.35 = (bf16[2,2,48,1920]{3,2,1,0:T(8,128)(2,1)S(1)}, bf16[2,2,48,1920]{3,2,1,0:T(8,128)(2,1)S(1)}, u32[]{:S(2)}, u32[]{:S(2)}) collective-permute-start(bf16[2,2,48,1920]{3,2,1,0:T(8,128)(2,1)S(1)} %get-tuple-element.242), channel_id=1, source_target_pairs={{0,8},{8,0},{16,24},{24,16},{1,9},{9,1},{17,25},{25,17},{2,10},{10... | collective-permute-start | bytes 2211848 | tf_op jit(solution)/shard_map/ppermute | solution.py:912
  131.4 17.3 %collective-permute-start.36 = (bf16[2,2,48,1920]{3,2,1,0:T(8,128)(2,1)S(1)}, bf16[2,2,48,1920]{3,2,1,0:T(8,128)(2,1)S(1)}, u32[]{:S(2)}, u32[]{:S(2)}) collective-permute-start(bf16[2,2,48,1920]{3,2,1,0:T(8,128)(2,1)S(1)} %get-tuple-element.243), channel_id=1, source_target_pairs={{0,16},{8,24},{16,0},{24,8},{1,17},{9,25},{17,1},{25,9},{2,18},{10... | collective-permute-start | bytes 2211848 | tf_op jit(solution)/shard_map/ppermute | solution.py:916
  131.9 20.0 %collective-permute-start.39 = (bf16[4,48,1024]{2,1,0:T(8,128)(2,1)S(1)}, bf16[4,48,1024]{2,1,0:T(8,128)(2,1)S(1)}, u32[]{:S(2)}, u32[]{:S(2)}) collective-permute-start(bf16[4,48,1024]{2,1,0:T(8,128)(2,1)S(1)} %get-tuple-element.251), channel_id=1, source_target_pairs={{0,4},{1,5},{2,6},{3,7},{4,0},{5,1},{6,2},{7,3},{8,12},{9,13},{10,... | collective-permute-start | bytes 1179656 | tf_op jit(solution)/shard_map/ppermute | solution.py:924
  149.1 10.7 %collective-permute-start.37 = (bf16[2,48,1920]{2,1,0:T(8,128)(2,1)S(1)}, bf16[2,48,1920]{2,1,0:T(8,128)(2,1)S(1)}, u32[]{:S(2)}, u32[]{:S(2)}) collective-permute-start(bf16[2,48,1920]{2,1,0:T(8,128)(2,1)S(1)} %get-tuple-element.249), channel_id=1, source_target_pairs={{0,16},{8,24},{16,0},{24,8},{1,17},{9,25},{17,1},{25,9},{2,18},{10... | collective-permute-start | bytes 1105928 | tf_op jit(solution)/shard_map/ppermute | solution.py:916
  150.8 11.2 %collective-permute-start.34 = (bf16[4,48,512]{2,1,0:T(8,128)(2,1)S(1)}, bf16[4,48,512]{2,1,0:T(8,128)(2,1)S(1)}, u32[]{:S(2)}, u32[]{:S(2)}) collective-permute-start(bf16[4,48,512]{2,1,0:T(8,128)(2,1)S(1)} %get-tuple-element.240), channel_id=1, source_target_pairs={{0,16},{8,24},{16,0},{24,8},{1,17},{9,25},{17,1},{25,9},{2,18},{10... | collective-permute-start | bytes 589832 | tf_op jit(solution)/shard_map/ppermute | solution.py:916
  152.0 10.1 %collective-permute-start.33 = (bf16[4,2,2,48,1280]{4,3,2,1,0:T(8,128)(2,1)S(1)}, bf16[4,2,2,48,1280]{4,3,2,1,0:T(8,128)(2,1)S(1)}, u32[]{:S(2)}, u32[]{:S(2)}) collective-permute-start(bf16[4,2,2,48,1280]{4,3,2,1,0:T(8,128)(2,1)S(1)} %get-tuple-element.239), channel_id=1, source_target_pairs={{0,1},{1,0},{2,3},{3,2},{4,5},{5,4},{6,7},{7,6},{8,9},{9,8},{10,11... | collective-permute-start | bytes 5898248 | tf_op jit(solution)/shard_map/ppermute | solution.py:901
  162.6 12.4 %collective-permute-start.40 = (bf16[2,2,48,1536]{3,2,1,0:T(8,128)(2,1)S(1)}, bf16[2,2,48,1536]{3,2,1,0:T(8,128)(2,1)S(1)}, u32[]{:S(2)}, u32[]{:S(2)}) collective-permute-start(bf16[2,2,48,1536]{3,2,1,0:T(8,128)(2,1)S(1)} %get-tuple-element.265), channel_id=1, source_target_pairs={{0,8},{8,0},{16,24},{24,16},{1,9},{9,1},{17,25},{25,17},{2,10},{10... | collective-permute-start | bytes 1769480 | tf_op jit(solution)/shard_map/ppermute | solution.py:912
  163.6 13.2 %collective-permute-start.41 = (bf16[2,2,48,1536]{3,2,1,0:T(8,128)(2,1)S(1)}, bf16[2,2,48,1536]{3,2,1,0:T(8,128)(2,1)S(1)}, u32[]{:S(2)}, u32[]{:S(2)}) collective-permute-start(bf16[2,2,48,1536]{3,2,1,0:T(8,128)(2,1)S(1)} %get-tuple-element.266), channel_id=1, source_target_pairs={{0,16},{8,24},{16,0},{24,8},{1,17},{9,25},{17,1},{25,9},{2,18},{10... | collective-permute-start | bytes 1769480 | tf_op jit(solution)/shard_map/ppermute | solution.py:916
  164.6 14.6 %collective-permute-start.44 = (bf16[2,48,2432]{2,1,0:T(8,128)(2,1)S(1)}, bf16[2,48,2432]{2,1,0:T(8,128)(2,1)S(1)}, u32[]{:S(2)}, u32[]{:S(2)}) collective-permute-start(bf16[2,48,2432]{2,1,0:T(8,128)(2,1)S(1)} %get-tuple-element.258), channel_id=1, source_target_pairs={{0,2},{1,3},{2,0},{3,1},{4,6},{5,7},{6,4},{7,5},{8,10},{9,11},{10,... | collective-permute-start | bytes 1400840 | tf_op jit(solution)/shard_map/ppermute | solution.py:924
  188.9 13.5 %collective-permute-start.53 = (bf16[48,3456]{1,0:T(8,128)(2,1)S(1)}, bf16[48,3456]{1,0:T(8,128)(2,1)S(1)}, u32[]{:S(2)}, u32[]{:S(2)}) collective-permute-start(bf16[48,3456]{1,0:T(8,128)(2,1)S(1)} %last_sum.2.refs_0_), channel_id=1, source_target_pairs={{0,24},{8,16},{16,8},{24,0},{1,25},{9,17},{17,9},{25,1},{2,26},{10... | collective-permute-start | bytes 995336 | tf_op jit(solution)/shard_map/ppermute | solution.py:907
  190.3 13.3 %collective-permute-start.52 = (bf16[48,3456]{1,0:T(8,128)(2,1)S(1)}, bf16[48,3456]{1,0:T(8,128)(2,1)S(1)}, u32[]{:S(2)}, u32[]{:S(2)}) collective-permute-start(bf16[48,3456]{1,0:T(8,128)(2,1)S(1)} %last_sum.2.refs_0_), channel_id=1, source_target_pairs={{0,16},{8,24},{16,0},{24,8},{1,17},{9,25},{17,1},{25,9},{2,18},{10... | collective-permute-start | bytes 995336 | tf_op jit(solution)/shard_map/ppermute | solution.py:907
  191.3 12.3 %collective-permute-start.51 = (bf16[48,3456]{1,0:T(8,128)(2,1)S(1)}, bf16[48,3456]{1,0:T(8,128)(2,1)S(1)}, u32[]{:S(2)}, u32[]{:S(2)}) collective-permute-start(bf16[48,3456]{1,0:T(8,128)(2,1)S(1)} %last_sum.2.refs_0_), channel_id=1, source_target_pairs={{0,8},{8,0},{16,24},{24,16},{1,9},{9,1},{17,25},{25,17},{2,10},{10... | collective-permute-start | bytes 995336 | tf_op jit(solution)/shard_map/ppermute | solution.py:907
  (32 other events, 186.7 us)

commit v2 on v1

--- a/solution.py
+++ b/solution.py
@@ -1042,7 +1042,8 @@
         quarter_e = [half_of(pos, expand_weight), half_of(pos, output_weight), jnp.pad(held, ((0, 32), (0, 0)))]
         quarter_e = jnp.concatenate(quarter_e, axis=1)
         wide_e = quarter_e.shape[1] - 128
-        chips_p = after(chips_p, sibling_p, quarter_e)
+        quarter_s, token_group = pick(pos, shrink_weight), regroup(token_rows)
+        chips_p = after(chips_p, sibling_p, quarter_e, quarter_s, token_group)
         mine_p = below(*chips_p)
         quarter_e = after(quarter_e, *chips_p)
         far_e = from_chip(quarter_e, 2)
@@ -1057,14 +1058,12 @@
             return Weight(shape, [shard, sibling, *group], copies)
 
         project = halves(shapes[0], project_weight, sibling_p, (mine_p, plane_p, *other_p), 0)
-        quarter_s = pick(pos, after(shrink_weight, quarter_e))
         quarter_s = after(quarter_s, plane_p)
         far_s = from_chip(quarter_s, 2)
         mine_e = below(*near_e, far_e, wide=wide_e)
         plane_e = from_plane(mine_e)
         held = jnp.concatenate([held, *(chip[:16, wide_e:] for chip in (*near_e, far_e))], axis=0)
-        token_group = regroup(after(token_rows, plane_p))
-        held = after(held, mine_e, token_group)
+        held = after(held, mine_e)
         bias_full, hidden_bias, rows6 = spread(pos, [held, from_core(held)], width, expand_weight.shape[1])
         out_bias, gain1, shift1, down_bias, gain2, shift2 = (rows6[at : at + 1] for at in range(6))
     else:

time: 210 us -> 209 us (level)
  transfers between devices with their start and end apart: 54 -> 54, of which waited for: 26 -> 26; matrix products, arithmetic and copies ran while one was open for 3% -> 2% of each run, Pallas kernels for 33% -> 34%
where the time goes in v2:
time: 209 us; the launch traced here: 208 us
  Pallas kernels  88 us (42%)
  waiting for transfers between devices  60.7 us (29%)
  starting transfers between devices  51.6 us (25%)
  local copies, waits for them, and re-layouts  5.65 us (3%)
    ppermute x15, waiting for transfers between devices, from_chip(): return lax.ppermute(values, 'fsdp', [(i, i ^ 2 * flip) for i in range(8)])  27.8 us
    ppermute x15, starting transfers between devices, from_chip(): return lax.ppermute(values, 'fsdp', [(i, i ^ 2 * flip) for i in range(8)])  21.1 us
    pallas_call x4, Pallas kernels, pieces_grad(): pl.pallas_call(kernel, grid_spec=pltpu.PrefetchScalarGridSpec(num_scalar_...  19.7 us
    ppermute x6, waiting for transfers between devices, from_y(): return lax.ppermute(values, 'dp', [(i, i ^ 2) for i in range(4)])  15.2 us
    ppermute x12, starting transfers between devices, from_plane(): lax.ppermute(part, 'dp', [(i, i ^ flip) for i in range(4)])  14.2 us
    pallas_call x1, Pallas kernels, attend(): pl.pallas_call(attend_kernel, grid_spec=pltpu.PrefetchScalarGridSpec(num_...  8.74 us
    pallas_call x1, Pallas kernels, second_norm(): pl.pallas_call(functools.partial(second_kernel, weight=weight, seq=seq),...  8.63 us
    pallas_call x1, Pallas kernels, expand_act(): pl.pallas_call(functools.partial(expand_kernel, weight=weight, tile=tile)...  8.5 us
  transfers between devices with their start and end apart: 54, of which 26 were waited for; matrix products, arithmetic and copies ran while one was open for 2% of the time, Pallas kernels for 34%

profile of v2, /device:TPU:0, one launch (start us, length us, event | category | flops | bytes accessed | tf_op | source)
XLA Modules:
  0.0 208.0 jit_solution(14576987385428740727)
XLA Ops:
  2.1 3.7 %collective-permute-start.2 = (bf16[48,1152]{1,0:T(8,128)(2,1)S(1)}, bf16[48,1152]{1,0:T(8,128)(2,1)S(1)}, u32[]{:S(2)}, u32[]{:S(2)}) collective-permute-start(bf16[48,1152]{1,0:T(8,128)(2,1)S(1)} %dynamic_slice.11), channel_id=1, source_target_pairs={{0,4},{1,5},{2,6},{3,7},{4,0},{5,1},{6,2},{7,3},{8,12},{9,13},{10,... | collective-permute-start | bytes 331784 | tf_op jit(solution)/shard_map/ppermute | solution.py:924
  15.7 2.6 %collective-permute-start.9 = (bf16[144,1152]{1,0:T(8,128)(2,1)S(1)}, bf16[144,1152]{1,0:T(8,128)(2,1)S(1)}, u32[]{:S(2)}, u32[]{:S(2)}) collective-permute-start(bf16[144,1152]{1,0:T(8,128)(2,1)S(1)} %below.5.rest_2_), channel_id=1, source_target_pairs={{0,24},{8,16},{16,8},{24,0},{1,25},{9,17},{17,9},{25,1},{2,26},{10... | collective-permute-start | bytes 995336 | tf_op jit(solution)/shard_map/ppermute | solution.py:907
  19.2 3.7 %collective-permute-start.5 = (bf16[48,2048]{1,0:T(8,128)(2,1)S(1)}, bf16[48,2048]{1,0:T(8,128)(2,1)S(1)}, u32[]{:S(2)}, u32[]{:S(2)}) collective-permute-start(bf16[48,2048]{1,0:T(8,128)(2,1)S(1)} %fusion.1), channel_id=1, source_target_pairs={{0,4},{1,5},{2,6},{3,7},{4,0},{5,1},{6,2},{7,3},{8,12},{9,13},{10,... | collective-permute-start | bytes 589832 | tf_op jit(solution)/shard_map/ppermute | solution.py:924
  23.3 8.2 %collective-permute-done.5.refs_2_ = bf16[48,2048]{1,0:T(8,128)(2,1)S(1)} collective-permute-done((bf16[48,2048]{1,0:T(8,128)(2,1)S(1)}, bf16[48,2048]{1,0:T(8,128)(2,1)S(1)}, u32[]{:S(2)}, u32[]{:S(2)}) %collective-permute-start.5) | collective-permute-done | bytes 196640 | tf_op jit(solution)/shard_map/ppermute | solution.py:924
  32.8 6.0 %collective-permute-done.6.refs_1_ = bf16[48,2048]{1,0:T(8,128)(2,1)S(1)} collective-permute-done((bf16[48,2048]{1,0:T(8,128)(2,1)S(1)}, bf16[48,2048]{1,0:T(8,128)(2,1)S(1)}, u32[]{:S(2)}, u32[]{:S(2)}) %collective-permute-start.6) | collective-permute-done | bytes 196640 | tf_op jit(solution)/shard_map/ppermute | solution.py:924
  39.9 2.4 %collective-permute-start.18 = (bf16[144,1920]{1,0:T(8,128)(2,1)S(1)}, bf16[144,1920]{1,0:T(8,128)(2,1)S(1)}, u32[]{:S(2)}, u32[]{:S(2)}) collective-permute-start(bf16[144,1920]{1,0:T(8,128)(2,1)S(1)} %below.7.rest_2_), channel_id=1, source_target_pairs={{0,24},{8,16},{16,8},{24,0},{1,25},{9,17},{17,9},{25,1},{2,26},{10... | collective-permute-start | bytes 1658888 | tf_op jit(solution)/shard_map/ppermute | solution.py:907
  44.2 5.5 %join.1 = (bf16[832,2304]{1,0:T(8,128)(2,1)}, bf16[768,2304]{1,0:T(8,128)(2,1)}) custom-call(s32[4]{0:T(128)S(1)} %pad_add_fusion.pos, bf16[832,768]{1,0:T(8,128)(2,1)S(1)} %bitcast.28, f32[1,2304]{1,0:T(1,128)S(1)} %get-tuple-element.165.bias, bf16[96,2304]{1,0:T(8,128)(2,1)S(1)} %copy-done.6, bf16[96,2304]{1,0:T(8,128)(2,1)S(1)} %collective-permute-done.3.rest_1_, ...), custom_call_target="tpu_custom_call" | custom-call | tf_op jit(solution)/shard_map/join/pallas_call | solution.py:232
  49.7 1.8 collective-permute-start.13
  51.5 8.7 %attend.1 = (bf16[8,104,768]{2,1,0:T(8,128)(2,1)S(1)}, bf16[8,6,104,256]{3,2,1,0:T(8,128)(2,1)}) custom-call(s32[8]{0:T(128)S(1)} %copy-done.8, bf16[8,104,2304]{2,1,0:T(8,128)(2,1)} %bitcast.34), custom_call_target="tpu_custom_call" | custom-call | tf_op jit(solution)/shard_map/attend/pallas_call | solution.py:288
  61.2 5.7 %collective-permute-done.17.refs_1_ = bf16[144,1920]{1,0:T(8,128)(2,1)S(1)} collective-permute-done((bf16[144,1920]{1,0:T(8,128)(2,1)S(1)}, bf16[144,1920]{1,0:T(8,128)(2,1)S(1)}, u32[]{:S(2)}, u32[]{:S(2)}) %collective-permute-start.17) | collective-permute-done | bytes 552992 | tf_op jit(solution)/shard_map/ppermute | solution.py:907
  72.7 2.4 %first_norm.1 = (f32[832,768]{1,0:T(8,128)S(1)}, f32[832,1]{1,0:T(8,128)S(1)}, bf16[832,768]{1,0:T(8,128)(2,1)S(1)}, bf16[768,768]{1,0:T(8,128)(2,1)S(1)}) custom-call(s32[4]{0:T(128)S(1)} %pad_add_fusion.pos, bf16[832,768]{1,0:T(8,128)(2,1)S(1)} %bitcast.31, f32[1,768]{1,0:T(1,128)S(1)} %get-tuple-element.307.bias, bf16[832,768]{1,0:T(8,128)(2,1)S(1)} %bitcast.29, ...), custom_call_target="tpu_custom_call" | custom-call | tf_op jit(solution)/shard_map/first_norm/pallas_call | solution.py:424
  75.0 8.5 %expand_act.1 = (bf16[832,3072]{1,0:T(8,128)(2,1)S(1)}, bf16[832,3072]{1,0:T(8,128)(2,1)S(1)}, bf16[768,3072]{1,0:T(8,128)(2,1)S(1)}) custom-call(s32[4]{0:T(128)S(1)} %pad_add_fusion.pos, bf16[832,768]{1,0:T(8,128)(2,1)S(1)} %get-tuple-element.191.normed_low.values, f32[1,3072]{1,0:T(1,128)S(1)} %get-tuple-element.182.bias, bf16[96,3072]{1,0:T(8,128)(2,1)S(1)} %copy-done.5, ...), custom_call_target="tpu_custom_call" | custom-call | tf_op jit(solution)/shard_map/expand_act/pallas_call | solution.py:453
  87.0 8.6 %second_norm.1 = (bf16[832,768]{1,0:T(8,128)(2,1)}, bf16[832,768]{1,0:T(8,128)(2,1)S(1)}, f32[832,768]{1,0:T(8,128)S(1)}, f32[8,768]{1,0:T(8,128)S(1)}, bf16[3072,768]{1,0:T(8,128)(2,1)S(1)}) custom-call(s32[4]{0:T(128)S(1)} %pad_add_fusion.pos, s32[8]{0:T(128)S(1)} %copy-done.8, bf16[832,3072]{1,0:T(8,128)(2,1)S(1)} %get-tuple-element.184.active.left, ...), custom_call_target="tpu_custom_call" | custom-call | tf_op jit(solution)/shard_map/second_norm/pallas_call | solution.py:505
  95.6 5.9 %stacked_grad.1 = (bf16[4,2,2,48,1536]{4,3,2,1,0:T(8,128)(2,1)S(1)}, bf16[4,2,2,48,1536]{4,3,2,1,0:T(8,128)(2,1)S(1)}) custom-call(s32[4]{0:T(128)S(1)} %pad_add_fusion.pos, bf16[832,3072]{1,0:T(8,128)(2,1)S(1)} %get-tuple-element.184.active.left, bf16[832,768]{1,0:T(8,128)(2,1)S(1)} %get-tuple-element.198.right.low), custom_call_target="tpu_custom_call" | custom-call | tf_op jit(solution)/shard_map/stacked_grad/pallas_call | solution.py:693
  101.8 4.9 %hidden_back.1 = (bf16[832,3072]{1,0:T(8,128)(2,1)S(1)}, f32[1,3072]{1,0:T(1,128)S(1)}) custom-call(bf16[832,768]{1,0:T(8,128)(2,1)S(1)} %get-tuple-element.198.right.low, bf16[3072,768]{1,0:T(8,128)(2,1)S(1)} %get-tuple-element.199.weight, bf16[832,3072]{1,0:T(8,128)(2,1)S(1)} %get-tuple-element.200.slope), custom_call_target="tpu_custom_call" | custom-call | tf_op jit(solution)/shard_map/hidden_back/pallas_call | solution.py:538
  107.9 1.7 collective-permute-start.32
  109.6 6.1 %halves_grad.3 = (bf16[4,2,2,48,1536]{4,3,2,1,0:T(8,128)(2,1)S(1)}, bf16[4,2,2,48,1536]{4,3,2,1,0:T(8,128)(2,1)S(1)}) custom-call(s32[4]{0:T(128)S(1)} %pad_add_fusion.pos, bf16[832,768]{1,0:T(8,128)(2,1)S(1)} %regroup.5.left, bf16[832,3072]{1,0:T(8,128)(2,1)S(1)} %get-tuple-element.207.right.hidden), custom_call_target="tpu_custom_call" | custom-call | tf_op jit(solution)/shard_map/halves_grad/pallas_call | solution.py:693
  115.8 6.0 %first_back.1 = (f32[832,768]{1,0:T(8,128)S(1)}, bf16[832,768]{1,0:T(8,128)(2,1)S(1)}, bf16[832,768]{1,0:T(8,128)(2,1)S(1)}, f32[8,768]{1,0:T(8,128)S(1)}) custom-call(bf16[832,3072]{1,0:T(8,128)(2,1)S(1)} %get-tuple-element.207.right.hidden, bf16[768,3072]{1,0:T(8,128)(2,1)S(1)} %get-tuple-element.208.weight, f32[832,768]{1,0:T(8,128)S(1)} %get-tuple-element.209.second, ...), custom_call_target="tpu_custom_call" | custom-call | flops 99999997952 | tf_op jit(solution)/shard_map/first_back/pallas_call | solution.py:578
  121.9 2.5 %halves_grad.4 = (bf16[4,2,2,48,384]{4,3,2,1,0:T(8,128)(2,1)S(1)}, bf16[4,2,2,48,384]{4,3,2,1,0:T(8,128)(2,1)S(1)}) custom-call(s32[4]{0:T(128)S(1)} %pad_add_fusion.pos, bf16[832,768]{1,0:T(8,128)(2,1)S(1)} %regroup.4.left, bf16[832,768]{1,0:T(8,128)(2,1)S(1)} %get-tuple-element.217.right), custom_call_target="tpu_custom_call" | custom-call | tf_op jit(solution)/shard_map/halves_grad/pallas_call | solution.py:693
  125.0 2.4 %collective-permute-done.32.received = bf16[2,4,48,1024]{3,2,1,0:T(8,128)(2,1)S(1)} collective-permute-done((bf16[2,4,48,1024]{3,2,1,0:T(8,128)(2,1)S(1)}, bf16[2,4,48,1024]{3,2,1,0:T(8,128)(2,1)S(1)}, u32[]{:S(2)}, u32[]{:S(2)}) %collective-permute-start.32) | collective-permute-done | bytes 786464 | tf_op jit(solution)/shard_map/ppermute | solution.py:924
  130.4 2.4 %collective-permute-start.39 = (bf16[4,48,1024]{2,1,0:T(8,128)(2,1)S(1)}, bf16[4,48,1024]{2,1,0:T(8,128)(2,1)S(1)}, u32[]{:S(2)}, u32[]{:S(2)}) collective-permute-start(bf16[4,48,1024]{2,1,0:T(8,128)(2,1)S(1)} %get-tuple-element.247), channel_id=1, source_target_pairs={{0,4},{1,5},{2,6},{3,7},{4,0},{5,1},{6,2},{7,3},{8,12},{9,13},{10,... | collective-permute-start | bytes 1179656 | tf_op jit(solution)/shard_map/ppermute | solution.py:924
  132.7 8.4 %attend_back.1 = (bf16[8,104,2304]{2,1,0:T(8,128)(2,1)S(1)}, f32[1,1536]{1,0:T(1,128)S(1)}) custom-call(bf16[8,104,2304]{2,1,0:T(8,128)(2,1)} %bitcast.35, bf16[8,6,104,256]{3,2,1,0:T(8,128)(2,1)} %get-tuple-element.195.probs, bf16[8,104,768]{2,1,0:T(8,128)(2,1)S(1)} %bitcast.33), custom_call_target="tpu_custom_call" | custom-call | tf_op jit(solution)/shard_map/attend_back/pallas_call | solution.py:350
  141.3 5.1 %halves_grad.5 = (bf16[4,2,2,48,1280]{4,3,2,1,0:T(8,128)(2,1)S(1)}, bf16[4,2,2,48,1280]{4,3,2,1,0:T(8,128)(2,1)S(1)}) custom-call(s32[4]{0:T(128)S(1)} %pad_add_fusion.pos, bf16[832,768]{1,0:T(8,128)(2,1)S(1)} %regroup.3.left, bf16[832,2304]{1,0:T(8,128)(2,1)S(1)} %bitcast.25, f32[8,16,128]{2,1,0:T(8,128)S(1)} %bundle.1.rest_0_), custom_call_target="tpu_custom_call" | custom-call | tf_op jit(solution)/shard_map/halves_grad/pallas_call | solution.py:693
  150.4 7.9 %collective-permute-done.37.received = bf16[2,48,1920]{2,1,0:T(8,128)(2,1)S(1)} collective-permute-done((bf16[2,48,1920]{2,1,0:T(8,128)(2,1)S(1)}, bf16[2,48,1920]{2,1,0:T(8,128)(2,1)S(1)}, u32[]{:S(2)}, u32[]{:S(2)}) %collective-permute-start.37) | collective-permute-done | bytes 368672 | tf_op jit(solution)/shard_map/ppermute | solution.py:916
  158.4 1.9 collective-permute-done.34.two
  163.7 4.5 %token_back.1 = f32[832,768]{1,0:T(8,128)} custom-call(bf16[832,2304]{1,0:T(8,128)(2,1)S(1)} %bitcast.26, bf16[768,2304]{1,0:T(8,128)(2,1)S(1)} %copy-done.2, f32[832,768]{1,0:T(8,128)S(1)} %get-tuple-element.259.first), custom_call_target="tpu_custom_call" | custom-call | tf_op jit(solution)/shard_map/token_back/pallas_call | solution.py:603
  168.1 5.3 %collective-permute-done.40.refs_2_ = bf16[2,2,48,1536]{3,2,1,0:T(8,128)(2,1)S(1)} collective-permute-done((bf16[2,2,48,1536]{3,2,1,0:T(8,128)(2,1)S(1)}, bf16[2,2,48,1536]{3,2,1,0:T(8,128)(2,1)S(1)}, u32[]{:S(2)}, u32[]{:S(2)}) %collective-permute-start.40) | collective-permute-done | bytes 589856 | tf_op jit(solution)/shard_map/ppermute | solution.py:912
  179.3 2.9 %collective-permute-done.42.received = bf16[2,48,1536]{2,1,0:T(8,128)(2,1)S(1)} collective-permute-done((bf16[2,48,1536]{2,1,0:T(8,128)(2,1)S(1)}, bf16[2,48,1536]{2,1,0:T(8,128)(2,1)S(1)}, u32[]{:S(2)}, u32[]{:S(2)}) %collective-permute-start.42) | collective-permute-done | bytes 294944 | tf_op jit(solution)/shard_map/ppermute | solution.py:916
  183.3 1.8 collective-permute-start.45
  185.1 2.1 %collective-permute-done.46.refs_2_ = bf16[48,2432]{1,0:T(8,128)(2,1)S(1)} collective-permute-done((bf16[48,2432]{1,0:T(8,128)(2,1)S(1)}, bf16[48,2432]{1,0:T(8,128)(2,1)S(1)}, u32[]{:S(2)}, u32[]{:S(2)}) %collective-permute-start.46) | collective-permute-done | bytes 233504 | tf_op jit(solution)/shard_map/ppermute | solution.py:924
  192.3 6.1 %collective-permute-done.47.refs_1_ = bf16[48,1280]{1,0:T(8,128)(2,1)S(1)} collective-permute-done((bf16[48,1280]{1,0:T(8,128)(2,1)S(1)}, bf16[48,1280]{1,0:T(8,128)(2,1)S(1)}, u32[]{:S(2)}, u32[]{:S(2)}) %collective-permute-start.47) | collective-permute-done | bytes 122912 | tf_op jit(solution)/shard_map/ppermute | solution.py:924
  202.0 2.2 %place.2 = (f32[384,768]{1,0:T(8,128)}, f32[96,3072]{1,0:T(8,128)}, f32[96,768]{1,0:T(8,128)}) custom-call(s32[4]{0:T(128)S(1)} %pad_add_fusion.pos, bf16[48,3456]{1,0:T(8,128)(2,1)S(1)} %last_sum.2.refs_0_, bf16[48,3456]{1,0:T(8,128)(2,1)S(1)} %collective-permute-done.51.refs_1_, bf16[48,3456]{1,0:T(8,128)(2,1)S(1)} %collective-permute-done.52.refs_2_, ...), custom_call_target="tpu_custom_call" | custom-call | tf_op jit(solution)/shard_map/place/pallas_call | solution.py:885
  (163 shorter events, 58.7 us)
Async XLA Ops:
  0.7 14.9 %collective-permute-start.3 = (bf16[96,2304]{1,0:T(8,128)(2,1)}, bf16[96,2304]{1,0:T(8,128)(2,1)S(1)}, u32[]{:S(2)}, u32[]{:S(2)}) collective-permute-start(bf16[96,2304]{1,0:T(8,128)(2,1)} %rest_0_.4), channel_id=1, source_target_pairs={{0,1},{1,0},{2,3},{3,2},{4,5},{5,4},{6,7},{7,6},{8,9},{9,8},{10,11... | collective-permute-start | bytes 1327112 | tf_op jit(solution)/shard_map/ppermute | solution.py:901
  2.1 12.4 %collective-permute-start.2 = (bf16[48,1152]{1,0:T(8,128)(2,1)S(1)}, bf16[48,1152]{1,0:T(8,128)(2,1)S(1)}, u32[]{:S(2)}, u32[]{:S(2)}) collective-permute-start(bf16[48,1152]{1,0:T(8,128)(2,1)S(1)} %dynamic_slice.11), channel_id=1, source_target_pairs={{0,4},{1,5},{2,6},{3,7},{4,0},{5,1},{6,2},{7,3},{8,12},{9,13},{10,... | collective-permute-start | bytes 331784 | tf_op jit(solution)/shard_map/ppermute | solution.py:924
  15.7 15.8 %collective-permute-start.9 = (bf16[144,1152]{1,0:T(8,128)(2,1)S(1)}, bf16[144,1152]{1,0:T(8,128)(2,1)S(1)}, u32[]{:S(2)}, u32[]{:S(2)}) collective-permute-start(bf16[144,1152]{1,0:T(8,128)(2,1)S(1)} %below.5.rest_2_), channel_id=1, source_target_pairs={{0,24},{8,16},{16,8},{24,0},{1,25},{9,17},{17,9},{25,1},{2,26},{10... | collective-permute-start | bytes 995336 | tf_op jit(solution)/shard_map/ppermute | solution.py:907
  18.2 14.4 %collective-permute-start.8 = (bf16[144,1152]{1,0:T(8,128)(2,1)S(1)}, bf16[144,1152]{1,0:T(8,128)(2,1)S(1)}, u32[]{:S(2)}, u32[]{:S(2)}) collective-permute-start(bf16[144,1152]{1,0:T(8,128)(2,1)S(1)} %below.5.rest_2_), channel_id=1, source_target_pairs={{0,16},{8,24},{16,0},{24,8},{1,17},{9,25},{17,1},{25,9},{2,18},{10... | collective-permute-start | bytes 995336 | tf_op jit(solution)/shard_map/ppermute | solution.py:907
  18.7 14.0 %collective-permute-start.7 = (bf16[144,1152]{1,0:T(8,128)(2,1)S(1)}, bf16[144,1152]{1,0:T(8,128)(2,1)S(1)}, u32[]{:S(2)}, u32[]{:S(2)}) collective-permute-start(bf16[144,1152]{1,0:T(8,128)(2,1)S(1)} %below.5.rest_2_), channel_id=1, source_target_pairs={{0,8},{8,0},{16,24},{24,16},{1,9},{9,1},{17,25},{25,17},{2,10},{10... | collective-permute-start | bytes 995336 | tf_op jit(solution)/shard_map/ppermute | solution.py:907
  19.2 12.3 %collective-permute-start.5 = (bf16[48,2048]{1,0:T(8,128)(2,1)S(1)}, bf16[48,2048]{1,0:T(8,128)(2,1)S(1)}, u32[]{:S(2)}, u32[]{:S(2)}) collective-permute-start(bf16[48,2048]{1,0:T(8,128)(2,1)S(1)} %fusion.1), channel_id=1, source_target_pairs={{0,4},{1,5},{2,6},{3,7},{4,0},{5,1},{6,2},{7,3},{8,12},{9,13},{10,... | collective-permute-start | bytes 589832 | tf_op jit(solution)/shard_map/ppermute | solution.py:924
  22.9 9.9 %collective-permute-start.4 = (bf16[48,2048]{1,0:T(8,128)(2,1)S(1)}, bf16[48,2048]{1,0:T(8,128)(2,1)S(1)}, u32[]{:S(2)}, u32[]{:S(2)}) collective-permute-start(bf16[48,2048]{1,0:T(8,128)(2,1)S(1)} %fusion.1), channel_id=1, source_target_pairs={{0,2},{1,3},{2,0},{3,1},{4,6},{5,7},{6,4},{7,5},{8,10},{9,11},{10,... | collective-permute-start | bytes 589832 | tf_op jit(solution)/shard_map/ppermute | solution.py:924
  31.5 10.9 %collective-permute-start.11 = (bf16[144,1152]{1,0:T(8,128)(2,1)S(1)}, bf16[144,1152]{1,0:T(8,128)(2,1)S(1)}, u32[]{:S(2)}, u32[]{:S(2)}) collective-permute-start(bf16[144,1152]{1,0:T(8,128)(2,1)S(1)} %below.5.rest_2_), channel_id=1, source_target_pairs={{0,1},{1,0},{2,3},{3,2},{4,5},{5,4},{6,7},{7,6},{8,9},{9,8},{10,11... | collective-permute-start | bytes 995336 | tf_op jit(solution)/shard_map/ppermute | solution.py:901
  39.5 20.7 %collective-permute-start.14 = (bf16[96,1536]{1,0:T(8,128)(2,1)S(1)}, bf16[96,1536]{1,0:T(8,128)(2,1)S(1)}, u32[]{:S(2)}, u32[]{:S(2)}) collective-permute-start(bf16[96,1536]{1,0:T(8,128)(2,1)S(1)} %pick.1), channel_id=1, source_target_pairs={{0,4},{1,5},{2,6},{3,7},{4,0},{5,1},{6,2},{7,3},{8,12},{9,13},{10,... | collective-permute-start | bytes 884744 | tf_op jit(solution)/shard_map/ppermute | solution.py:924
  39.9 21.2 %collective-permute-start.18 = (bf16[144,1920]{1,0:T(8,128)(2,1)S(1)}, bf16[144,1920]{1,0:T(8,128)(2,1)S(1)}, u32[]{:S(2)}, u32[]{:S(2)}) collective-permute-start(bf16[144,1920]{1,0:T(8,128)(2,1)S(1)} %below.7.rest_2_), channel_id=1, source_target_pairs={{0,24},{8,16},{16,8},{24,0},{1,25},{9,17},{17,9},{25,1},{2,26},{10... | collective-permute-start | bytes 1658888 | tf_op jit(solution)/shard_map/ppermute | solution.py:907
  42.4 24.5 %collective-permute-start.17 = (bf16[144,1920]{1,0:T(8,128)(2,1)S(1)}, bf16[144,1920]{1,0:T(8,128)(2,1)S(1)}, u32[]{:S(2)}, u32[]{:S(2)}) collective-permute-start(bf16[144,1920]{1,0:T(8,128)(2,1)S(1)} %below.7.rest_2_), channel_id=1, source_target_pairs={{0,16},{8,24},{16,0},{24,8},{1,17},{9,25},{17,1},{25,9},{2,18},{10... | collective-permute-start | bytes 1658888 | tf_op jit(solution)/shard_map/ppermute | solution.py:907
  42.9 24.1 %collective-permute-start.16 = (bf16[144,1920]{1,0:T(8,128)(2,1)S(1)}, bf16[144,1920]{1,0:T(8,128)(2,1)S(1)}, u32[]{:S(2)}, u32[]{:S(2)}) collective-permute-start(bf16[144,1920]{1,0:T(8,128)(2,1)S(1)} %below.7.rest_2_), channel_id=1, source_target_pairs={{0,8},{8,0},{16,24},{24,16},{1,9},{9,1},{17,25},{25,17},{2,10},{10... | collective-permute-start | bytes 1658888 | tf_op jit(solution)/shard_map/ppermute | solution.py:907
  49.7 18.0 %collective-permute-start.13 = (bf16[96,1536]{1,0:T(8,128)(2,1)S(1)}, bf16[96,1536]{1,0:T(8,128)(2,1)S(1)}, u32[]{:S(2)}, u32[]{:S(2)}) collective-permute-start(bf16[96,1536]{1,0:T(8,128)(2,1)S(1)} %pick.1), channel_id=1, source_target_pairs={{0,2},{1,3},{2,0},{3,1},{4,6},{5,7},{6,4},{7,5},{8,10},{9,11},{10,... | collective-permute-start | bytes 884744 | tf_op jit(solution)/shard_map/ppermute | solution.py:924
  61.2 10.1 %collective-permute-start.20 = (bf16[144,1920]{1,0:T(8,128)(2,1)S(1)}, bf16[144,1920]{1,0:T(8,128)(2,1)S(1)}, u32[]{:S(2)}, u32[]{:S(2)}) collective-permute-start(bf16[144,1920]{1,0:T(8,128)(2,1)S(1)} %below.7.rest_2_), channel_id=1, source_target_pairs={{0,1},{1,0},{2,3},{3,2},{4,5},{5,4},{6,7},{7,6},{8,9},{9,8},{10,11... | collective-permute-start | bytes 1658888 | tf_op jit(solution)/shard_map/ppermute | solution.py:901
  68.2 15.4 %collective-permute-start.24 = (bf16[288,768]{1,0:T(8,128)(2,1)S(1)}, bf16[288,768]{1,0:T(8,128)(2,1)S(1)}, u32[]{:S(2)}, u32[]{:S(2)}) collective-permute-start(bf16[288,768]{1,0:T(8,128)(2,1)S(1)} %get-tuple-element.187), channel_id=1, source_target_pairs={{0,8},{8,0},{16,24},{24,16},{1,9},{9,1},{17,25},{25,17},{2,10},{10... | collective-permute-start | bytes 1327112 | tf_op jit(solution)/shard_map/ppermute | solution.py:912
  69.8 13.8 %collective-permute-start.25 = (bf16[288,768]{1,0:T(8,128)(2,1)S(1)}, bf16[288,768]{1,0:T(8,128)(2,1)S(1)}, u32[]{:S(2)}, u32[]{:S(2)}) collective-permute-start(bf16[288,768]{1,0:T(8,128)(2,1)S(1)} %get-tuple-element.188), channel_id=1, source_target_pairs={{0,16},{8,24},{16,0},{24,8},{1,17},{9,25},{17,1},{25,9},{2,18},{10... | collective-permute-start | bytes 1327112 | tf_op jit(solution)/shard_map/ppermute | solution.py:916
  71.3 13.5 %collective-permute-start.26 = (bf16[288,1536]{1,0:T(8,128)(2,1)S(1)}, bf16[288,1536]{1,0:T(8,128)(2,1)S(1)}, u32[]{:S(2)}, u32[]{:S(2)}) collective-permute-start(bf16[288,1536]{1,0:T(8,128)(2,1)S(1)} %below.9.whole_ref.rest_2_), channel_id=1, source_target_pairs={{0,1},{1,0},{2,3},{3,2},{4,5},{5,4},{6,7},{7,6},{8,9},{9,8},{10,11... | collective-permute-start | bytes 2654216 | tf_op jit(solution)/shard_map/ppermute | solution.py:901
  107.3 14.6 %collective-permute-start.29 = (bf16[2,4,48,512]{3,2,1,0:T(8,128)(2,1)S(1)}, bf16[2,4,48,512]{3,2,1,0:T(8,128)(2,1)S(1)}, u32[]{:S(2)}, u32[]{:S(2)}) collective-permute-start(bf16[2,4,48,512]{3,2,1,0:T(8,128)(2,1)S(1)} %get-tuple-element.214), channel_id=1, source_target_pairs={{0,8},{8,0},{16,24},{24,16},{1,9},{9,1},{17,25},{25,17},{2,10},{10... | collective-permute-start | bytes 1179656 | tf_op jit(solution)/shard_map/ppermute | solution.py:912
  107.9 19.5 %collective-permute-start.32 = (bf16[2,4,48,1024]{3,2,1,0:T(8,128)(2,1)S(1)}, bf16[2,4,48,1024]{3,2,1,0:T(8,128)(2,1)S(1)}, u32[]{:S(2)}, u32[]{:S(2)}) collective-permute-start(bf16[2,4,48,1024]{3,2,1,0:T(8,128)(2,1)S(1)} %get-tuple-element.222), channel_id=1, source_target_pairs={{0,2},{1,3},{2,0},{3,1},{4,6},{5,7},{6,4},{7,5},{8,10},{9,11},{10,... | collective-permute-start | bytes 2359304 | tf_op jit(solution)/shard_map/ppermute | solution.py:924
  115.7 11.9 %collective-permute-start.30 = (bf16[4,2,2,48,1536]{4,3,2,1,0:T(8,128)(2,1)S(1)}, bf16[4,2,2,48,1536]{4,3,2,1,0:T(8,128)(2,1)S(1)}, u32[]{:S(2)}, u32[]{:S(2)}) collective-permute-start(bf16[4,2,2,48,1536]{4,3,2,1,0:T(8,128)(2,1)S(1)} %get-tuple-element.219), channel_id=1, source_target_pairs={{0,1},{1,0},{2,3},{3,2},{4,5},{5,4},{6,7},{7,6},{8,9},{9,8},{10,11... | collective-permute-start | bytes 7077896 | tf_op jit(solution)/shard_map/ppermute | solution.py:901
  128.3 18.1 %collective-permute-start.35 = (bf16[2,2,48,1920]{3,2,1,0:T(8,128)(2,1)S(1)}, bf16[2,2,48,1920]{3,2,1,0:T(8,128)(2,1)S(1)}, u32[]{:S(2)}, u32[]{:S(2)}) collective-permute-start(bf16[2,2,48,1920]{3,2,1,0:T(8,128)(2,1)S(1)} %get-tuple-element.238), channel_id=1, source_target_pairs={{0,8},{8,0},{16,24},{24,16},{1,9},{9,1},{17,25},{25,17},{2,10},{10... | collective-permute-start | bytes 2211848 | tf_op jit(solution)/shard_map/ppermute | solution.py:912
  129.9 17.4 %collective-permute-start.36 = (bf16[2,2,48,1920]{3,2,1,0:T(8,128)(2,1)S(1)}, bf16[2,2,48,1920]{3,2,1,0:T(8,128)(2,1)S(1)}, u32[]{:S(2)}, u32[]{:S(2)}) collective-permute-start(bf16[2,2,48,1920]{3,2,1,0:T(8,128)(2,1)S(1)} %get-tuple-element.239), channel_id=1, source_target_pairs={{0,16},{8,24},{16,0},{24,8},{1,17},{9,25},{17,1},{25,9},{2,18},{10... | collective-permute-start | bytes 2211848 | tf_op jit(solution)/shard_map/ppermute | solution.py:916
  130.4 20.0 %collective-permute-start.39 = (bf16[4,48,1024]{2,1,0:T(8,128)(2,1)S(1)}, bf16[4,48,1024]{2,1,0:T(8,128)(2,1)S(1)}, u32[]{:S(2)}, u32[]{:S(2)}) collective-permute-start(bf16[4,48,1024]{2,1,0:T(8,128)(2,1)S(1)} %get-tuple-element.247), channel_id=1, source_target_pairs={{0,4},{1,5},{2,6},{3,7},{4,0},{5,1},{6,2},{7,3},{8,12},{9,13},{10,... | collective-permute-start | bytes 1179656 | tf_op jit(solution)/shard_map/ppermute | solution.py:924
  147.6 10.7 %collective-permute-start.37 = (bf16[2,48,1920]{2,1,0:T(8,128)(2,1)S(1)}, bf16[2,48,1920]{2,1,0:T(8,128)(2,1)S(1)}, u32[]{:S(2)}, u32[]{:S(2)}) collective-permute-start(bf16[2,48,1920]{2,1,0:T(8,128)(2,1)S(1)} %get-tuple-element.245), channel_id=1, source_target_pairs={{0,16},{8,24},{16,0},{24,8},{1,17},{9,25},{17,1},{25,9},{2,18},{10... | collective-permute-start | bytes 1105928 | tf_op jit(solution)/shard_map/ppermute | solution.py:916
  149.2 11.2 %collective-permute-start.34 = (bf16[4,48,512]{2,1,0:T(8,128)(2,1)S(1)}, bf16[4,48,512]{2,1,0:T(8,128)(2,1)S(1)}, u32[]{:S(2)}, u32[]{:S(2)}) collective-permute-start(bf16[4,48,512]{2,1,0:T(8,128)(2,1)S(1)} %get-tuple-element.236), channel_id=1, source_target_pairs={{0,16},{8,24},{16,0},{24,8},{1,17},{9,25},{17,1},{25,9},{2,18},{10... | collective-permute-start | bytes 589832 | tf_op jit(solution)/shard_map/ppermute | solution.py:916
  150.4 10.1 %collective-permute-start.33 = (bf16[4,2,2,48,1280]{4,3,2,1,0:T(8,128)(2,1)S(1)}, bf16[4,2,2,48,1280]{4,3,2,1,0:T(8,128)(2,1)S(1)}, u32[]{:S(2)}, u32[]{:S(2)}) collective-permute-start(bf16[4,2,2,48,1280]{4,3,2,1,0:T(8,128)(2,1)S(1)} %get-tuple-element.235), channel_id=1, source_target_pairs={{0,1},{1,0},{2,3},{3,2},{4,5},{5,4},{6,7},{7,6},{8,9},{9,8},{10,11... | collective-permute-start | bytes 5898248 | tf_op jit(solution)/shard_map/ppermute | solution.py:901
  161.0 12.4 %collective-permute-start.40 = (bf16[2,2,48,1536]{3,2,1,0:T(8,128)(2,1)S(1)}, bf16[2,2,48,1536]{3,2,1,0:T(8,128)(2,1)S(1)}, u32[]{:S(2)}, u32[]{:S(2)}) collective-permute-start(bf16[2,2,48,1536]{3,2,1,0:T(8,128)(2,1)S(1)} %get-tuple-element.261), channel_id=1, source_target_pairs={{0,8},{8,0},{16,24},{24,16},{1,9},{9,1},{17,25},{25,17},{2,10},{10... | collective-permute-start | bytes 1769480 | tf_op jit(solution)/shard_map/ppermute | solution.py:912
  162.0 13.2 %collective-permute-start.41 = (bf16[2,2,48,1536]{3,2,1,0:T(8,128)(2,1)S(1)}, bf16[2,2,48,1536]{3,2,1,0:T(8,128)(2,1)S(1)}, u32[]{:S(2)}, u32[]{:S(2)}) collective-permute-start(bf16[2,2,48,1536]{3,2,1,0:T(8,128)(2,1)S(1)} %get-tuple-element.262), channel_id=1, source_target_pairs={{0,16},{8,24},{16,0},{24,8},{1,17},{9,25},{17,1},{25,9},{2,18},{10... | collective-permute-start | bytes 1769480 | tf_op jit(solution)/shard_map/ppermute | solution.py:916
  163.0 14.6 %collective-permute-start.44 = (bf16[2,48,2432]{2,1,0:T(8,128)(2,1)S(1)}, bf16[2,48,2432]{2,1,0:T(8,128)(2,1)S(1)}, u32[]{:S(2)}, u32[]{:S(2)}) collective-permute-start(bf16[2,48,2432]{2,1,0:T(8,128)(2,1)S(1)} %get-tuple-element.254), channel_id=1, source_target_pairs={{0,2},{1,3},{2,0},{3,1},{4,6},{5,7},{6,4},{7,5},{8,10},{9,11},{10,... | collective-permute-start | bytes 1400840 | tf_op jit(solution)/shard_map/ppermute | solution.py:924
  187.3 13.6 %collective-permute-start.53 = (bf16[48,3456]{1,0:T(8,128)(2,1)S(1)}, bf16[48,3456]{1,0:T(8,128)(2,1)S(1)}, u32[]{:S(2)}, u32[]{:S(2)}) collective-permute-start(bf16[48,3456]{1,0:T(8,128)(2,1)S(1)} %last_sum.2.refs_0_), channel_id=1, source_target_pairs={{0,24},{8,16},{16,8},{24,0},{1,25},{9,17},{17,9},{25,1},{2,26},{10... | collective-permute-start | bytes 995336 | tf_op jit(solution)/shard_map/ppermute | solution.py:907
  188.7 13.3 %collective-permute-start.52 = (bf16[48,3456]{1,0:T(8,128)(2,1)S(1)}, bf16[48,3456]{1,0:T(8,128)(2,1)S(1)}, u32[]{:S(2)}, u32[]{:S(2)}) collective-permute-start(bf16[48,3456]{1,0:T(8,128)(2,1)S(1)} %last_sum.2.refs_0_), channel_id=1, source_target_pairs={{0,16},{8,24},{16,0},{24,8},{1,17},{9,25},{17,1},{25,9},{2,18},{10... | collective-permute-start | bytes 995336 | tf_op jit(solution)/shard_map/ppermute | solution.py:907
  189.8 12.3 %collective-permute-start.51 = (bf16[48,3456]{1,0:T(8,128)(2,1)S(1)}, bf16[48,3456]{1,0:T(8,128)(2,1)S(1)}, u32[]{:S(2)}, u32[]{:S(2)}) collective-permute-start(bf16[48,3456]{1,0:T(8,128)(2,1)S(1)} %last_sum.2.refs_0_), channel_id=1, source_target_pairs={{0,8},{8,0},{16,24},{24,16},{1,9},{9,1},{17,25},{25,17},{2,10},{10... | collective-permute-start | bytes 995336 | tf_op jit(solution)/shard_map/ppermute | solution.py:907
  (37 other events, 242.8 us)

commit v3 on v2

--- a/solution.py
+++ b/solution.py
@@ -469,34 +469,30 @@
     pieces, (out, low, grad, sums), full, (held, sems) = *weight.split(rest[:-2]), rest[-2:]
     weight.arrive(pieces, full, pos)
     sums[...] = jnp.zeros_like(sums)
-    tile = rows_of(held.shape[0], 4 * seq)
-    count = held.shape[0] // tile
-
-    def write(at):
-        rows = pl.ds(pl.multiple_of(at * tile, 16), tile)
-        return pltpu.make_async_copy(held.at[rows, :], out.at[rows, :], sems.at[at])
-
-    def chunk(at, carry):
-        rows = pl.ds(pl.multiple_of(at * tile, 16), tile)
+    chunks = chunk_slices(held.shape[0], 208)
+    writes = [
+        pltpu.make_async_copy(held.at[rows, :], out.at[rows, :], sems.at[at]) for at, rows in enumerate(chunks)
+    ]
+
+    def normalise(at, shrunk):
+        rows = chunks[at]
         normed = unit[rows, :] * gain[...] + shift[...]
-        unit2, scale2 = norm_parts(normed + (dot(active[rows, :], full[...]) + bias[...]))
+        unit2, scale2 = norm_parts(normed + (shrunk + bias[...]))
         held[rows, :] = (unit2 * gain2[...] + shift2[...]).astype(BF16)
-        write(at).start()
-        row = lax.broadcasted_iota(jnp.int32, (tile, 1), 0)
+        writes[at].start()
+        row = lax.broadcasted_iota(jnp.int32, (rows.stop - rows.start, 1), 0) + rows.start
         live = jnp.zeros(row.shape, jnp.bool_)
-        for pair in range(tile // seq):
-            valid = captions[at * (tile // seq) + pair] + 2 + REGIONS
-            live = live | ((row >= pair * seq) & (row < pair * seq + valid))
+        for pair in range(rows.start // seq, (rows.stop - 1) // seq + 1):
+            live = live | ((row >= pair * seq) & (row < pair * seq + captions[pair] + 2 + REGIONS))
         upstream = jnp.where(live, cotangent[rows, :].astype(F32), 0.0)
         second = norm_back(upstream, unit2, scale2, gain2[...])
         grad[rows, :] = second
         low[rows, :] = second.astype(BF16)
         add_sums(sums, (second, upstream * unit2, upstream))
-        return carry
-
-    lax.fori_loop(0, count, chunk, 0)
-    for at in range(count):
-        write(at).wait()
+
+    chunked(len(chunks), lambda at: dot(active[chunks[at], :], full[...]), normalise)
+    for write in writes:
+        write.wait()
 
 
 def second_norm(pos, captions, active, weight, bias, unit, gain, shift, gain2, shift2, cotangent, seq):

time: 209 us -> 208 us (level)
  no operation moved by 1% of the time
where the time goes in v3:
time: 208 us; the launch traced here: 207 us
  Pallas kernels  87.2 us (42%)
  waiting for transfers between devices  60.7 us (29%)
  starting transfers between devices  51.6 us (25%)
  local copies, waits for them, and re-layouts  5.65 us (3%)
    ppermute x15, waiting for transfers between devices, from_chip(): return lax.ppermute(values, 'fsdp', [(i, i ^ 2 * flip) for i in range(8)])  27.8 us
    ppermute x15, starting transfers between devices, from_chip(): return lax.ppermute(values, 'fsdp', [(i, i ^ 2 * flip) for i in range(8)])  21.1 us
    pallas_call x4, Pallas kernels, pieces_grad(): pl.pallas_call(kernel, grid_spec=pltpu.PrefetchScalarGridSpec(num_scalar_...  19.7 us
    ppermute x6, waiting for transfers between devices, from_y(): return lax.ppermute(values, 'dp', [(i, i ^ 2) for i in range(4)])  15.2 us
    ppermute x12, starting transfers between devices, from_plane(): lax.ppermute(part, 'dp', [(i, i ^ flip) for i in range(4)])  14.2 us
    pallas_call x1, Pallas kernels, attend(): pl.pallas_call(attend_kernel, grid_spec=pltpu.PrefetchScalarGridSpec(num_...  8.74 us
    pallas_call x1, Pallas kernels, expand_act(): pl.pallas_call(functools.partial(expand_kernel, weight=weight, tile=tile)...  8.69 us
    ppermute x12, waiting for transfers between devices, from_plane(): lax.ppermute(part, 'dp', [(i, i ^ flip) for i in range(4)])  8.47 us
  transfers between devices with their start and end apart: 54, of which 26 were waited for; matrix products, arithmetic and copies ran while one was open for 2% of the time, Pallas kernels for 34%

profile of v3, /device:TPU:0, one launch (start us, length us, event | category | flops | bytes accessed | tf_op | source)
XLA Modules:
  0.0 207.1 jit_solution(16192840499873623663)
XLA Ops:
  2.1 3.7 %collective-permute-start.2 = (bf16[48,1152]{1,0:T(8,128)(2,1)S(1)}, bf16[48,1152]{1,0:T(8,128)(2,1)S(1)}, u32[]{:S(2)}, u32[]{:S(2)}) collective-permute-start(bf16[48,1152]{1,0:T(8,128)(2,1)S(1)} %dynamic_slice.11), channel_id=1, source_target_pairs={{0,4},{1,5},{2,6},{3,7},{4,0},{5,1},{6,2},{7,3},{8,12},{9,13},{10,... | collective-permute-start | bytes 331784 | tf_op jit(solution)/shard_map/ppermute | solution.py:920
  15.7 2.6 %collective-permute-start.9 = (bf16[144,1152]{1,0:T(8,128)(2,1)S(1)}, bf16[144,1152]{1,0:T(8,128)(2,1)S(1)}, u32[]{:S(2)}, u32[]{:S(2)}) collective-permute-start(bf16[144,1152]{1,0:T(8,128)(2,1)S(1)} %below.5.rest_2_), channel_id=1, source_target_pairs={{0,24},{8,16},{16,8},{24,0},{1,25},{9,17},{17,9},{25,1},{2,26},{10... | collective-permute-start | bytes 995336 | tf_op jit(solution)/shard_map/ppermute | solution.py:903
  19.2 3.7 %collective-permute-start.5 = (bf16[48,2048]{1,0:T(8,128)(2,1)S(1)}, bf16[48,2048]{1,0:T(8,128)(2,1)S(1)}, u32[]{:S(2)}, u32[]{:S(2)}) collective-permute-start(bf16[48,2048]{1,0:T(8,128)(2,1)S(1)} %fusion.1), channel_id=1, source_target_pairs={{0,4},{1,5},{2,6},{3,7},{4,0},{5,1},{6,2},{7,3},{8,12},{9,13},{10,... | collective-permute-start | bytes 589832 | tf_op jit(solution)/shard_map/ppermute | solution.py:920
  23.3 8.2 %collective-permute-done.5.refs_2_ = bf16[48,2048]{1,0:T(8,128)(2,1)S(1)} collective-permute-done((bf16[48,2048]{1,0:T(8,128)(2,1)S(1)}, bf16[48,2048]{1,0:T(8,128)(2,1)S(1)}, u32[]{:S(2)}, u32[]{:S(2)}) %collective-permute-start.5) | collective-permute-done | bytes 196640 | tf_op jit(solution)/shard_map/ppermute | solution.py:920
  32.8 6.0 %collective-permute-done.6.refs_1_ = bf16[48,2048]{1,0:T(8,128)(2,1)S(1)} collective-permute-done((bf16[48,2048]{1,0:T(8,128)(2,1)S(1)}, bf16[48,2048]{1,0:T(8,128)(2,1)S(1)}, u32[]{:S(2)}, u32[]{:S(2)}) %collective-permute-start.6) | collective-permute-done | bytes 196640 | tf_op jit(solution)/shard_map/ppermute | solution.py:920
  39.9 2.4 %collective-permute-start.18 = (bf16[144,1920]{1,0:T(8,128)(2,1)S(1)}, bf16[144,1920]{1,0:T(8,128)(2,1)S(1)}, u32[]{:S(2)}, u32[]{:S(2)}) collective-permute-start(bf16[144,1920]{1,0:T(8,128)(2,1)S(1)} %below.7.rest_2_), channel_id=1, source_target_pairs={{0,24},{8,16},{16,8},{24,0},{1,25},{9,17},{17,9},{25,1},{2,26},{10... | collective-permute-start | bytes 1658888 | tf_op jit(solution)/shard_map/ppermute | solution.py:903
  44.2 5.5 %join.1 = (bf16[832,2304]{1,0:T(8,128)(2,1)}, bf16[768,2304]{1,0:T(8,128)(2,1)}) custom-call(s32[4]{0:T(128)S(1)} %pad_add_fusion.pos, bf16[832,768]{1,0:T(8,128)(2,1)S(1)} %bitcast.28, f32[1,2304]{1,0:T(1,128)S(1)} %get-tuple-element.165.bias, bf16[96,2304]{1,0:T(8,128)(2,1)S(1)} %copy-done.6, bf16[96,2304]{1,0:T(8,128)(2,1)S(1)} %collective-permute-done.3.rest_1_, ...), custom_call_target="tpu_custom_call" | custom-call | tf_op jit(solution)/shard_map/join/pallas_call | solution.py:232
  49.7 1.8 collective-permute-start.13
  51.5 8.7 %attend.1 = (bf16[8,104,768]{2,1,0:T(8,128)(2,1)S(1)}, bf16[8,6,104,256]{3,2,1,0:T(8,128)(2,1)}) custom-call(s32[8]{0:T(128)S(1)} %copy-done.8, bf16[8,104,2304]{2,1,0:T(8,128)(2,1)} %bitcast.34), custom_call_target="tpu_custom_call" | custom-call | tf_op jit(solution)/shard_map/attend/pallas_call | solution.py:288
  61.2 5.7 %collective-permute-done.17.refs_1_ = bf16[144,1920]{1,0:T(8,128)(2,1)S(1)} collective-permute-done((bf16[144,1920]{1,0:T(8,128)(2,1)S(1)}, bf16[144,1920]{1,0:T(8,128)(2,1)S(1)}, u32[]{:S(2)}, u32[]{:S(2)}) %collective-permute-start.17) | collective-permute-done | bytes 552992 | tf_op jit(solution)/shard_map/ppermute | solution.py:903
  72.7 2.4 %first_norm.1 = (f32[832,768]{1,0:T(8,128)S(1)}, f32[832,1]{1,0:T(8,128)S(1)}, bf16[832,768]{1,0:T(8,128)(2,1)S(1)}, bf16[768,768]{1,0:T(8,128)(2,1)S(1)}) custom-call(s32[4]{0:T(128)S(1)} %pad_add_fusion.pos, bf16[832,768]{1,0:T(8,128)(2,1)S(1)} %bitcast.31, f32[1,768]{1,0:T(1,128)S(1)} %get-tuple-element.307.bias, bf16[832,768]{1,0:T(8,128)(2,1)S(1)} %bitcast.29, ...), custom_call_target="tpu_custom_call" | custom-call | tf_op jit(solution)/shard_map/first_norm/pallas_call | solution.py:424
  75.0 8.7 %expand_act.1 = (bf16[832,3072]{1,0:T(8,128)(2,1)S(1)}, bf16[832,3072]{1,0:T(8,128)(2,1)S(1)}, bf16[768,3072]{1,0:T(8,128)(2,1)S(1)}) custom-call(s32[4]{0:T(128)S(1)} %pad_add_fusion.pos, bf16[832,768]{1,0:T(8,128)(2,1)S(1)} %get-tuple-element.191.normed_low.values, f32[1,3072]{1,0:T(1,128)S(1)} %get-tuple-element.182.bias, bf16[96,3072]{1,0:T(8,128)(2,1)S(1)} %copy-done.5, ...), custom_call_target="tpu_custom_call" | custom-call | tf_op jit(solution)/shard_map/expand_act/pallas_call | solution.py:453
  87.2 7.6 %second_norm.1 = (bf16[832,768]{1,0:T(8,128)(2,1)}, bf16[832,768]{1,0:T(8,128)(2,1)S(1)}, f32[832,768]{1,0:T(8,128)S(1)}, f32[8,768]{1,0:T(8,128)S(1)}, bf16[3072,768]{1,0:T(8,128)(2,1)S(1)}) custom-call(s32[4]{0:T(128)S(1)} %pad_add_fusion.pos, s32[8]{0:T(128)S(1)} %copy-done.8, bf16[832,3072]{1,0:T(8,128)(2,1)S(1)} %get-tuple-element.184.active.left, ...), custom_call_target="tpu_custom_call" | custom-call | tf_op jit(solution)/shard_map/second_norm/pallas_call | solution.py:501
  94.8 5.9 %stacked_grad.1 = (bf16[4,2,2,48,1536]{4,3,2,1,0:T(8,128)(2,1)S(1)}, bf16[4,2,2,48,1536]{4,3,2,1,0:T(8,128)(2,1)S(1)}) custom-call(s32[4]{0:T(128)S(1)} %pad_add_fusion.pos, bf16[832,3072]{1,0:T(8,128)(2,1)S(1)} %get-tuple-element.184.active.left, bf16[832,768]{1,0:T(8,128)(2,1)S(1)} %get-tuple-element.198.right.low), custom_call_target="tpu_custom_call" | custom-call | tf_op jit(solution)/shard_map/stacked_grad/pallas_call | solution.py:689
  100.9 4.9 %hidden_back.1 = (bf16[832,3072]{1,0:T(8,128)(2,1)S(1)}, f32[1,3072]{1,0:T(1,128)S(1)}) custom-call(bf16[832,768]{1,0:T(8,128)(2,1)S(1)} %get-tuple-element.198.right.low, bf16[3072,768]{1,0:T(8,128)(2,1)S(1)} %get-tuple-element.199.weight, bf16[832,3072]{1,0:T(8,128)(2,1)S(1)} %get-tuple-element.200.slope), custom_call_target="tpu_custom_call" | custom-call | tf_op jit(solution)/shard_map/hidden_back/pallas_call | solution.py:534
  107.0 1.7 collective-permute-start.32
  108.7 6.1 %halves_grad.3 = (bf16[4,2,2,48,1536]{4,3,2,1,0:T(8,128)(2,1)S(1)}, bf16[4,2,2,48,1536]{4,3,2,1,0:T(8,128)(2,1)S(1)}) custom-call(s32[4]{0:T(128)S(1)} %pad_add_fusion.pos, bf16[832,768]{1,0:T(8,128)(2,1)S(1)} %regroup.5.left, bf16[832,3072]{1,0:T(8,128)(2,1)S(1)} %get-tuple-element.207.right.hidden), custom_call_target="tpu_custom_call" | custom-call | tf_op jit(solution)/shard_map/halves_grad/pallas_call | solution.py:689
  114.9 6.0 %first_back.1 = (f32[832,768]{1,0:T(8,128)S(1)}, bf16[832,768]{1,0:T(8,128)(2,1)S(1)}, bf16[832,768]{1,0:T(8,128)(2,1)S(1)}, f32[8,768]{1,0:T(8,128)S(1)}) custom-call(bf16[832,3072]{1,0:T(8,128)(2,1)S(1)} %get-tuple-element.207.right.hidden, bf16[768,3072]{1,0:T(8,128)(2,1)S(1)} %get-tuple-element.208.weight, f32[832,768]{1,0:T(8,128)S(1)} %get-tuple-element.209.second, ...), custom_call_target="tpu_custom_call" | custom-call | flops 99999997952 | tf_op jit(solution)/shard_map/first_back/pallas_call | solution.py:574
  121.1 2.5 %halves_grad.4 = (bf16[4,2,2,48,384]{4,3,2,1,0:T(8,128)(2,1)S(1)}, bf16[4,2,2,48,384]{4,3,2,1,0:T(8,128)(2,1)S(1)}) custom-call(s32[4]{0:T(128)S(1)} %pad_add_fusion.pos, bf16[832,768]{1,0:T(8,128)(2,1)S(1)} %regroup.4.left, bf16[832,768]{1,0:T(8,128)(2,1)S(1)} %get-tuple-element.217.right), custom_call_target="tpu_custom_call" | custom-call | tf_op jit(solution)/shard_map/halves_grad/pallas_call | solution.py:689
  124.2 2.4 %collective-permute-done.32.received = bf16[2,4,48,1024]{3,2,1,0:T(8,128)(2,1)S(1)} collective-permute-done((bf16[2,4,48,1024]{3,2,1,0:T(8,128)(2,1)S(1)}, bf16[2,4,48,1024]{3,2,1,0:T(8,128)(2,1)S(1)}, u32[]{:S(2)}, u32[]{:S(2)}) %collective-permute-start.32) | collective-permute-done | bytes 786464 | tf_op jit(solution)/shard_map/ppermute | solution.py:920
  129.5 2.4 %collective-permute-start.39 = (bf16[4,48,1024]{2,1,0:T(8,128)(2,1)S(1)}, bf16[4,48,1024]{2,1,0:T(8,128)(2,1)S(1)}, u32[]{:S(2)}, u32[]{:S(2)}) collective-permute-start(bf16[4,48,1024]{2,1,0:T(8,128)(2,1)S(1)} %get-tuple-element.247), channel_id=1, source_target_pairs={{0,4},{1,5},{2,6},{3,7},{4,0},{5,1},{6,2},{7,3},{8,12},{9,13},{10,... | collective-permute-start | bytes 1179656 | tf_op jit(solution)/shard_map/ppermute | solution.py:920
  131.9 8.4 %attend_back.1 = (bf16[8,104,2304]{2,1,0:T(8,128)(2,1)S(1)}, f32[1,1536]{1,0:T(1,128)S(1)}) custom-call(bf16[8,104,2304]{2,1,0:T(8,128)(2,1)} %bitcast.35, bf16[8,6,104,256]{3,2,1,0:T(8,128)(2,1)} %get-tuple-element.195.probs, bf16[8,104,768]{2,1,0:T(8,128)(2,1)S(1)} %bitcast.33), custom_call_target="tpu_custom_call" | custom-call | tf_op jit(solution)/shard_map/attend_back/pallas_call | solution.py:350
  140.4 5.1 %halves_grad.5 = (bf16[4,2,2,48,1280]{4,3,2,1,0:T(8,128)(2,1)S(1)}, bf16[4,2,2,48,1280]{4,3,2,1,0:T(8,128)(2,1)S(1)}) custom-call(s32[4]{0:T(128)S(1)} %pad_add_fusion.pos, bf16[832,768]{1,0:T(8,128)(2,1)S(1)} %regroup.3.left, bf16[832,2304]{1,0:T(8,128)(2,1)S(1)} %bitcast.25, f32[8,16,128]{2,1,0:T(8,128)S(1)} %bundle.1.rest_0_), custom_call_target="tpu_custom_call" | custom-call | tf_op jit(solution)/shard_map/halves_grad/pallas_call | solution.py:689
  149.5 7.9 %collective-permute-done.37.received = bf16[2,48,1920]{2,1,0:T(8,128)(2,1)S(1)} collective-permute-done((bf16[2,48,1920]{2,1,0:T(8,128)(2,1)S(1)}, bf16[2,48,1920]{2,1,0:T(8,128)(2,1)S(1)}, u32[]{:S(2)}, u32[]{:S(2)}) %collective-permute-start.37) | collective-permute-done | bytes 368672 | tf_op jit(solution)/shard_map/ppermute | solution.py:912
  157.6 1.9 collective-permute-done.34.two
  162.8 4.5 %token_back.1 = f32[832,768]{1,0:T(8,128)} custom-call(bf16[832,2304]{1,0:T(8,128)(2,1)S(1)} %bitcast.26, bf16[768,2304]{1,0:T(8,128)(2,1)S(1)} %copy-done.2, f32[832,768]{1,0:T(8,128)S(1)} %get-tuple-element.259.first), custom_call_target="tpu_custom_call" | custom-call | tf_op jit(solution)/shard_map/token_back/pallas_call | solution.py:599
  167.3 5.3 %collective-permute-done.40.refs_2_ = bf16[2,2,48,1536]{3,2,1,0:T(8,128)(2,1)S(1)} collective-permute-done((bf16[2,2,48,1536]{3,2,1,0:T(8,128)(2,1)S(1)}, bf16[2,2,48,1536]{3,2,1,0:T(8,128)(2,1)S(1)}, u32[]{:S(2)}, u32[]{:S(2)}) %collective-permute-start.40) | collective-permute-done | bytes 589856 | tf_op jit(solution)/shard_map/ppermute | solution.py:908
  178.5 2.9 %collective-permute-done.42.received = bf16[2,48,1536]{2,1,0:T(8,128)(2,1)S(1)} collective-permute-done((bf16[2,48,1536]{2,1,0:T(8,128)(2,1)S(1)}, bf16[2,48,1536]{2,1,0:T(8,128)(2,1)S(1)}, u32[]{:S(2)}, u32[]{:S(2)}) %collective-permute-start.42) | collective-permute-done | bytes 294944 | tf_op jit(solution)/shard_map/ppermute | solution.py:912
  182.5 1.8 collective-permute-start.45
  184.3 2.1 %collective-permute-done.46.refs_2_ = bf16[48,2432]{1,0:T(8,128)(2,1)S(1)} collective-permute-done((bf16[48,2432]{1,0:T(8,128)(2,1)S(1)}, bf16[48,2432]{1,0:T(8,128)(2,1)S(1)}, u32[]{:S(2)}, u32[]{:S(2)}) %collective-permute-start.46) | collective-permute-done | bytes 233504 | tf_op jit(solution)/shard_map/ppermute | solution.py:920
  191.4 6.1 %collective-permute-done.47.refs_1_ = bf16[48,1280]{1,0:T(8,128)(2,1)S(1)} collective-permute-done((bf16[48,1280]{1,0:T(8,128)(2,1)S(1)}, bf16[48,1280]{1,0:T(8,128)(2,1)S(1)}, u32[]{:S(2)}, u32[]{:S(2)}) %collective-permute-start.47) | collective-permute-done | bytes 122912 | tf_op jit(solution)/shard_map/ppermute | solution.py:920
  201.2 2.2 %place.2 = (f32[384,768]{1,0:T(8,128)}, f32[96,3072]{1,0:T(8,128)}, f32[96,768]{1,0:T(8,128)}) custom-call(s32[4]{0:T(128)S(1)} %pad_add_fusion.pos, bf16[48,3456]{1,0:T(8,128)(2,1)S(1)} %last_sum.2.refs_0_, bf16[48,3456]{1,0:T(8,128)(2,1)S(1)} %collective-permute-done.51.refs_1_, bf16[48,3456]{1,0:T(8,128)(2,1)S(1)} %collective-permute-done.52.refs_2_, ...), custom_call_target="tpu_custom_call" | custom-call | tf_op jit(solution)/shard_map/place/pallas_call | solution.py:881
  (163 shorter events, 58.6 us)
Async XLA Ops:
  0.7 14.9 %collective-permute-start.3 = (bf16[96,2304]{1,0:T(8,128)(2,1)}, bf16[96,2304]{1,0:T(8,128)(2,1)S(1)}, u32[]{:S(2)}, u32[]{:S(2)}) collective-permute-start(bf16[96,2304]{1,0:T(8,128)(2,1)} %rest_0_.4), channel_id=1, source_target_pairs={{0,1},{1,0},{2,3},{3,2},{4,5},{5,4},{6,7},{7,6},{8,9},{9,8},{10,11... | collective-permute-start | bytes 1327112 | tf_op jit(solution)/shard_map/ppermute | solution.py:897
  2.1 12.4 %collective-permute-start.2 = (bf16[48,1152]{1,0:T(8,128)(2,1)S(1)}, bf16[48,1152]{1,0:T(8,128)(2,1)S(1)}, u32[]{:S(2)}, u32[]{:S(2)}) collective-permute-start(bf16[48,1152]{1,0:T(8,128)(2,1)S(1)} %dynamic_slice.11), channel_id=1, source_target_pairs={{0,4},{1,5},{2,6},{3,7},{4,0},{5,1},{6,2},{7,3},{8,12},{9,13},{10,... | collective-permute-start | bytes 331784 | tf_op jit(solution)/shard_map/ppermute | solution.py:920
  15.7 15.8 %collective-permute-start.9 = (bf16[144,1152]{1,0:T(8,128)(2,1)S(1)}, bf16[144,1152]{1,0:T(8,128)(2,1)S(1)}, u32[]{:S(2)}, u32[]{:S(2)}) collective-permute-start(bf16[144,1152]{1,0:T(8,128)(2,1)S(1)} %below.5.rest_2_), channel_id=1, source_target_pairs={{0,24},{8,16},{16,8},{24,0},{1,25},{9,17},{17,9},{25,1},{2,26},{10... | collective-permute-start | bytes 995336 | tf_op jit(solution)/shard_map/ppermute | solution.py:903
  18.2 14.4 %collective-permute-start.8 = (bf16[144,1152]{1,0:T(8,128)(2,1)S(1)}, bf16[144,1152]{1,0:T(8,128)(2,1)S(1)}, u32[]{:S(2)}, u32[]{:S(2)}) collective-permute-start(bf16[144,1152]{1,0:T(8,128)(2,1)S(1)} %below.5.rest_2_), channel_id=1, source_target_pairs={{0,16},{8,24},{16,0},{24,8},{1,17},{9,25},{17,1},{25,9},{2,18},{10... | collective-permute-start | bytes 995336 | tf_op jit(solution)/shard_map/ppermute | solution.py:903
  18.7 14.0 %collective-permute-start.7 = (bf16[144,1152]{1,0:T(8,128)(2,1)S(1)}, bf16[144,1152]{1,0:T(8,128)(2,1)S(1)}, u32[]{:S(2)}, u32[]{:S(2)}) collective-permute-start(bf16[144,1152]{1,0:T(8,128)(2,1)S(1)} %below.5.rest_2_), channel_id=1, source_target_pairs={{0,8},{8,0},{16,24},{24,16},{1,9},{9,1},{17,25},{25,17},{2,10},{10... | collective-permute-start | bytes 995336 | tf_op jit(solution)/shard_map/ppermute | solution.py:903
  19.2 12.3 %collective-permute-start.5 = (bf16[48,2048]{1,0:T(8,128)(2,1)S(1)}, bf16[48,2048]{1,0:T(8,128)(2,1)S(1)}, u32[]{:S(2)}, u32[]{:S(2)}) collective-permute-start(bf16[48,2048]{1,0:T(8,128)(2,1)S(1)} %fusion.1), channel_id=1, source_target_pairs={{0,4},{1,5},{2,6},{3,7},{4,0},{5,1},{6,2},{7,3},{8,12},{9,13},{10,... | collective-permute-start | bytes 589832 | tf_op jit(solution)/shard_map/ppermute | solution.py:920
  31.5 10.9 %collective-permute-start.11 = (bf16[144,1152]{1,0:T(8,128)(2,1)S(1)}, bf16[144,1152]{1,0:T(8,128)(2,1)S(1)}, u32[]{:S(2)}, u32[]{:S(2)}) collective-permute-start(bf16[144,1152]{1,0:T(8,128)(2,1)S(1)} %below.5.rest_2_), channel_id=1, source_target_pairs={{0,1},{1,0},{2,3},{3,2},{4,5},{5,4},{6,7},{7,6},{8,9},{9,8},{10,11... | collective-permute-start | bytes 995336 | tf_op jit(solution)/shard_map/ppermute | solution.py:897
  39.5 20.7 %collective-permute-start.14 = (bf16[96,1536]{1,0:T(8,128)(2,1)S(1)}, bf16[96,1536]{1,0:T(8,128)(2,1)S(1)}, u32[]{:S(2)}, u32[]{:S(2)}) collective-permute-start(bf16[96,1536]{1,0:T(8,128)(2,1)S(1)} %pick.1), channel_id=1, source_target_pairs={{0,4},{1,5},{2,6},{3,7},{4,0},{5,1},{6,2},{7,3},{8,12},{9,13},{10,... | collective-permute-start | bytes 884744 | tf_op jit(solution)/shard_map/ppermute | solution.py:920
  39.9 21.2 %collective-permute-start.18 = (bf16[144,1920]{1,0:T(8,128)(2,1)S(1)}, bf16[144,1920]{1,0:T(8,128)(2,1)S(1)}, u32[]{:S(2)}, u32[]{:S(2)}) collective-permute-start(bf16[144,1920]{1,0:T(8,128)(2,1)S(1)} %below.7.rest_2_), channel_id=1, source_target_pairs={{0,24},{8,16},{16,8},{24,0},{1,25},{9,17},{17,9},{25,1},{2,26},{10... | collective-permute-start | bytes 1658888 | tf_op jit(solution)/shard_map/ppermute | solution.py:903
  42.4 24.5 %collective-permute-start.17 = (bf16[144,1920]{1,0:T(8,128)(2,1)S(1)}, bf16[144,1920]{1,0:T(8,128)(2,1)S(1)}, u32[]{:S(2)}, u32[]{:S(2)}) collective-permute-start(bf16[144,1920]{1,0:T(8,128)(2,1)S(1)} %below.7.rest_2_), channel_id=1, source_target_pairs={{0,16},{8,24},{16,0},{24,8},{1,17},{9,25},{17,1},{25,9},{2,18},{10... | collective-permute-start | bytes 1658888 | tf_op jit(solution)/shard_map/ppermute | solution.py:903
  42.9 24.1 %collective-permute-start.16 = (bf16[144,1920]{1,0:T(8,128)(2,1)S(1)}, bf16[144,1920]{1,0:T(8,128)(2,1)S(1)}, u32[]{:S(2)}, u32[]{:S(2)}) collective-permute-start(bf16[144,1920]{1,0:T(8,128)(2,1)S(1)} %below.7.rest_2_), channel_id=1, source_target_pairs={{0,8},{8,0},{16,24},{24,16},{1,9},{9,1},{17,25},{25,17},{2,10},{10... | collective-permute-start | bytes 1658888 | tf_op jit(solution)/shard_map/ppermute | solution.py:903
  49.7 18.0 %collective-permute-start.13 = (bf16[96,1536]{1,0:T(8,128)(2,1)S(1)}, bf16[96,1536]{1,0:T(8,128)(2,1)S(1)}, u32[]{:S(2)}, u32[]{:S(2)}) collective-permute-start(bf16[96,1536]{1,0:T(8,128)(2,1)S(1)} %pick.1), channel_id=1, source_target_pairs={{0,2},{1,3},{2,0},{3,1},{4,6},{5,7},{6,4},{7,5},{8,10},{9,11},{10,... | collective-permute-start | bytes 884744 | tf_op jit(solution)/shard_map/ppermute | solution.py:920
  61.2 10.1 %collective-permute-start.20 = (bf16[144,1920]{1,0:T(8,128)(2,1)S(1)}, bf16[144,1920]{1,0:T(8,128)(2,1)S(1)}, u32[]{:S(2)}, u32[]{:S(2)}) collective-permute-start(bf16[144,1920]{1,0:T(8,128)(2,1)S(1)} %below.7.rest_2_), channel_id=1, source_target_pairs={{0,1},{1,0},{2,3},{3,2},{4,5},{5,4},{6,7},{7,6},{8,9},{9,8},{10,11... | collective-permute-start | bytes 1658888 | tf_op jit(solution)/shard_map/ppermute | solution.py:897
  68.2 15.6 %collective-permute-start.24 = (bf16[288,768]{1,0:T(8,128)(2,1)S(1)}, bf16[288,768]{1,0:T(8,128)(2,1)S(1)}, u32[]{:S(2)}, u32[]{:S(2)}) collective-permute-start(bf16[288,768]{1,0:T(8,128)(2,1)S(1)} %get-tuple-element.187), channel_id=1, source_target_pairs={{0,8},{8,0},{16,24},{24,16},{1,9},{9,1},{17,25},{25,17},{2,10},{10... | collective-permute-start | bytes 1327112 | tf_op jit(solution)/shard_map/ppermute | solution.py:908
  69.8 14.0 %collective-permute-start.25 = (bf16[288,768]{1,0:T(8,128)(2,1)S(1)}, bf16[288,768]{1,0:T(8,128)(2,1)S(1)}, u32[]{:S(2)}, u32[]{:S(2)}) collective-permute-start(bf16[288,768]{1,0:T(8,128)(2,1)S(1)} %get-tuple-element.188), channel_id=1, source_target_pairs={{0,16},{8,24},{16,0},{24,8},{1,17},{9,25},{17,1},{25,9},{2,18},{10... | collective-permute-start | bytes 1327112 | tf_op jit(solution)/shard_map/ppermute | solution.py:912
  71.3 13.7 %collective-permute-start.26 = (bf16[288,1536]{1,0:T(8,128)(2,1)S(1)}, bf16[288,1536]{1,0:T(8,128)(2,1)S(1)}, u32[]{:S(2)}, u32[]{:S(2)}) collective-permute-start(bf16[288,1536]{1,0:T(8,128)(2,1)S(1)} %below.9.whole_ref.rest_2_), channel_id=1, source_target_pairs={{0,1},{1,0},{2,3},{3,2},{4,5},{5,4},{6,7},{7,6},{8,9},{9,8},{10,11... | collective-permute-start | bytes 2654216 | tf_op jit(solution)/shard_map/ppermute | solution.py:897
  106.4 14.6 %collective-permute-start.29 = (bf16[2,4,48,512]{3,2,1,0:T(8,128)(2,1)S(1)}, bf16[2,4,48,512]{3,2,1,0:T(8,128)(2,1)S(1)}, u32[]{:S(2)}, u32[]{:S(2)}) collective-permute-start(bf16[2,4,48,512]{3,2,1,0:T(8,128)(2,1)S(1)} %get-tuple-element.214), channel_id=1, source_target_pairs={{0,8},{8,0},{16,24},{24,16},{1,9},{9,1},{17,25},{25,17},{2,10},{10... | collective-permute-start | bytes 1179656 | tf_op jit(solution)/shard_map/ppermute | solution.py:908
  107.0 19.5 %collective-permute-start.32 = (bf16[2,4,48,1024]{3,2,1,0:T(8,128)(2,1)S(1)}, bf16[2,4,48,1024]{3,2,1,0:T(8,128)(2,1)S(1)}, u32[]{:S(2)}, u32[]{:S(2)}) collective-permute-start(bf16[2,4,48,1024]{3,2,1,0:T(8,128)(2,1)S(1)} %get-tuple-element.222), channel_id=1, source_target_pairs={{0,2},{1,3},{2,0},{3,1},{4,6},{5,7},{6,4},{7,5},{8,10},{9,11},{10,... | collective-permute-start | bytes 2359304 | tf_op jit(solution)/shard_map/ppermute | solution.py:920
  114.9 11.9 %collective-permute-start.30 = (bf16[4,2,2,48,1536]{4,3,2,1,0:T(8,128)(2,1)S(1)}, bf16[4,2,2,48,1536]{4,3,2,1,0:T(8,128)(2,1)S(1)}, u32[]{:S(2)}, u32[]{:S(2)}) collective-permute-start(bf16[4,2,2,48,1536]{4,3,2,1,0:T(8,128)(2,1)S(1)} %get-tuple-element.219), channel_id=1, source_target_pairs={{0,1},{1,0},{2,3},{3,2},{4,5},{5,4},{6,7},{7,6},{8,9},{9,8},{10,11... | collective-permute-start | bytes 7077896 | tf_op jit(solution)/shard_map/ppermute | solution.py:897
  127.4 18.1 %collective-permute-start.35 = (bf16[2,2,48,1920]{3,2,1,0:T(8,128)(2,1)S(1)}, bf16[2,2,48,1920]{3,2,1,0:T(8,128)(2,1)S(1)}, u32[]{:S(2)}, u32[]{:S(2)}) collective-permute-start(bf16[2,2,48,1920]{3,2,1,0:T(8,128)(2,1)S(1)} %get-tuple-element.238), channel_id=1, source_target_pairs={{0,8},{8,0},{16,24},{24,16},{1,9},{9,1},{17,25},{25,17},{2,10},{10... | collective-permute-start | bytes 2211848 | tf_op jit(solution)/shard_map/ppermute | solution.py:908
  129.0 17.4 %collective-permute-start.36 = (bf16[2,2,48,1920]{3,2,1,0:T(8,128)(2,1)S(1)}, bf16[2,2,48,1920]{3,2,1,0:T(8,128)(2,1)S(1)}, u32[]{:S(2)}, u32[]{:S(2)}) collective-permute-start(bf16[2,2,48,1920]{3,2,1,0:T(8,128)(2,1)S(1)} %get-tuple-element.239), channel_id=1, source_target_pairs={{0,16},{8,24},{16,0},{24,8},{1,17},{9,25},{17,1},{25,9},{2,18},{10... | collective-permute-start | bytes 2211848 | tf_op jit(solution)/shard_map/ppermute | solution.py:912
  129.5 20.0 %collective-permute-start.39 = (bf16[4,48,1024]{2,1,0:T(8,128)(2,1)S(1)}, bf16[4,48,1024]{2,1,0:T(8,128)(2,1)S(1)}, u32[]{:S(2)}, u32[]{:S(2)}) collective-permute-start(bf16[4,48,1024]{2,1,0:T(8,128)(2,1)S(1)} %get-tuple-element.247), channel_id=1, source_target_pairs={{0,4},{1,5},{2,6},{3,7},{4,0},{5,1},{6,2},{7,3},{8,12},{9,13},{10,... | collective-permute-start | bytes 1179656 | tf_op jit(solution)/shard_map/ppermute | solution.py:920
  146.7 10.7 %collective-permute-start.37 = (bf16[2,48,1920]{2,1,0:T(8,128)(2,1)S(1)}, bf16[2,48,1920]{2,1,0:T(8,128)(2,1)S(1)}, u32[]{:S(2)}, u32[]{:S(2)}) collective-permute-start(bf16[2,48,1920]{2,1,0:T(8,128)(2,1)S(1)} %get-tuple-element.245), channel_id=1, source_target_pairs={{0,16},{8,24},{16,0},{24,8},{1,17},{9,25},{17,1},{25,9},{2,18},{10... | collective-permute-start | bytes 1105928 | tf_op jit(solution)/shard_map/ppermute | solution.py:912
  147.5 9.9 %collective-permute-start.38 = (bf16[2,48,1920]{2,1,0:T(8,128)(2,1)S(1)}, bf16[2,48,1920]{2,1,0:T(8,128)(2,1)S(1)}, u32[]{:S(2)}, u32[]{:S(2)}) collective-permute-start(bf16[2,48,1920]{2,1,0:T(8,128)(2,1)S(1)} %get-tuple-element.246), channel_id=1, source_target_pairs={{0,8},{8,0},{16,24},{24,16},{1,9},{9,1},{17,25},{25,17},{2,10},{10... | collective-permute-start | bytes 1105928 | tf_op jit(solution)/shard_map/ppermute | solution.py:908
  148.3 11.2 %collective-permute-start.34 = (bf16[4,48,512]{2,1,0:T(8,128)(2,1)S(1)}, bf16[4,48,512]{2,1,0:T(8,128)(2,1)S(1)}, u32[]{:S(2)}, u32[]{:S(2)}) collective-permute-start(bf16[4,48,512]{2,1,0:T(8,128)(2,1)S(1)} %get-tuple-element.236), channel_id=1, source_target_pairs={{0,16},{8,24},{16,0},{24,8},{1,17},{9,25},{17,1},{25,9},{2,18},{10... | collective-permute-start | bytes 589832 | tf_op jit(solution)/shard_map/ppermute | solution.py:912
  149.5 10.1 %collective-permute-start.33 = (bf16[4,2,2,48,1280]{4,3,2,1,0:T(8,128)(2,1)S(1)}, bf16[4,2,2,48,1280]{4,3,2,1,0:T(8,128)(2,1)S(1)}, u32[]{:S(2)}, u32[]{:S(2)}) collective-permute-start(bf16[4,2,2,48,1280]{4,3,2,1,0:T(8,128)(2,1)S(1)} %get-tuple-element.235), channel_id=1, source_target_pairs={{0,1},{1,0},{2,3},{3,2},{4,5},{5,4},{6,7},{7,6},{8,9},{9,8},{10,11... | collective-permute-start | bytes 5898248 | tf_op jit(solution)/shard_map/ppermute | solution.py:897
  160.2 12.4 %collective-permute-start.40 = (bf16[2,2,48,1536]{3,2,1,0:T(8,128)(2,1)S(1)}, bf16[2,2,48,1536]{3,2,1,0:T(8,128)(2,1)S(1)}, u32[]{:S(2)}, u32[]{:S(2)}) collective-permute-start(bf16[2,2,48,1536]{3,2,1,0:T(8,128)(2,1)S(1)} %get-tuple-element.261), channel_id=1, source_target_pairs={{0,8},{8,0},{16,24},{24,16},{1,9},{9,1},{17,25},{25,17},{2,10},{10... | collective-permute-start | bytes 1769480 | tf_op jit(solution)/shard_map/ppermute | solution.py:908
  161.1 13.2 %collective-permute-start.41 = (bf16[2,2,48,1536]{3,2,1,0:T(8,128)(2,1)S(1)}, bf16[2,2,48,1536]{3,2,1,0:T(8,128)(2,1)S(1)}, u32[]{:S(2)}, u32[]{:S(2)}) collective-permute-start(bf16[2,2,48,1536]{3,2,1,0:T(8,128)(2,1)S(1)} %get-tuple-element.262), channel_id=1, source_target_pairs={{0,16},{8,24},{16,0},{24,8},{1,17},{9,25},{17,1},{25,9},{2,18},{10... | collective-permute-start | bytes 1769480 | tf_op jit(solution)/shard_map/ppermute | solution.py:912
  162.1 14.6 %collective-permute-start.44 = (bf16[2,48,2432]{2,1,0:T(8,128)(2,1)S(1)}, bf16[2,48,2432]{2,1,0:T(8,128)(2,1)S(1)}, u32[]{:S(2)}, u32[]{:S(2)}) collective-permute-start(bf16[2,48,2432]{2,1,0:T(8,128)(2,1)S(1)} %get-tuple-element.254), channel_id=1, source_target_pairs={{0,2},{1,3},{2,0},{3,1},{4,6},{5,7},{6,4},{7,5},{8,10},{9,11},{10,... | collective-permute-start | bytes 1400840 | tf_op jit(solution)/shard_map/ppermute | solution.py:920
  186.5 13.6 %collective-permute-start.53 = (bf16[48,3456]{1,0:T(8,128)(2,1)S(1)}, bf16[48,3456]{1,0:T(8,128)(2,1)S(1)}, u32[]{:S(2)}, u32[]{:S(2)}) collective-permute-start(bf16[48,3456]{1,0:T(8,128)(2,1)S(1)} %last_sum.2.refs_0_), channel_id=1, source_target_pairs={{0,24},{8,16},{16,8},{24,0},{1,25},{9,17},{17,9},{25,1},{2,26},{10... | collective-permute-start | bytes 995336 | tf_op jit(solution)/shard_map/ppermute | solution.py:903
  187.9 13.3 %collective-permute-start.52 = (bf16[48,3456]{1,0:T(8,128)(2,1)S(1)}, bf16[48,3456]{1,0:T(8,128)(2,1)S(1)}, u32[]{:S(2)}, u32[]{:S(2)}) collective-permute-start(bf16[48,3456]{1,0:T(8,128)(2,1)S(1)} %last_sum.2.refs_0_), channel_id=1, source_target_pairs={{0,16},{8,24},{16,0},{24,8},{1,17},{9,25},{17,1},{25,9},{2,18},{10... | collective-permute-start | bytes 995336 | tf_op jit(solution)/shard_map/ppermute | solution.py:903
  188.9 12.3 %collective-permute-start.51 = (bf16[48,3456]{1,0:T(8,128)(2,1)S(1)}, bf16[48,3456]{1,0:T(8,128)(2,1)S(1)}, u32[]{:S(2)}, u32[]{:S(2)}) collective-permute-start(bf16[48,3456]{1,0:T(8,128)(2,1)S(1)} %last_sum.2.refs_0_), channel_id=1, source_target_pairs={{0,8},{8,0},{16,24},{24,16},{1,9},{9,1},{17,25},{25,17},{2,10},{10... | collective-permute-start | bytes 995336 | tf_op jit(solution)/shard_map/ppermute | solution.py:903
  (37 other events, 242.7 us)
